TPU v7x, 32 devices: a whole 2x2x4 slice. The times are simulated.
32 devices in a mesh: section: 4 (over z), batch: 4 (over y, x), mp: 2 (over core).
Axes of the slice: x: 2, y: 2, z: 4, core: 2. Of those that a mesh axis runs over, the one named last changes fastest.
Arguments:
- tokens: bfloat16 [4, 2, 1024, 1024], P('batch', None, 'mp'), may hold values from -6 to 6
- cotangent: bfloat16 [4, 2, 1024, 1024], P('batch', None, 'mp'), may hold values from -6 to 6
- document_starts: int32 [4, 2, 1, 4], P('batch'), may hold values from 0 to 1023, as said below
- pre_gain: bfloat16 [4, 2, 1024], P('section'), may hold values from 0.099609375 to 1.8984375
- pre_bias: bfloat16 [4, 2, 1024], P('section'), may hold values from -1.75 to 1.75
- project_weight: bfloat16 [4, 3, 1024, 1024], P('section', None, None, 'mp'), may hold values from -0.1875 to 0.1875
- project_bias: bfloat16 [4, 2, 1024], P('section', None, 'mp'), may hold values from -3 to 3
- head_scale: bfloat16 [4, 16], P('section', 'mp'), may hold values from 0.5 to 2
- post_gain: bfloat16 [4, 1024], P('section', 'mp'), may hold values from 0.099609375 to 1.8984375
- post_bias: bfloat16 [4, 1024], P('section', 'mp'), may hold values from -1.75 to 1.75
- output_weight: bfloat16 [4, 1024, 1024], P('section', 'mp'), may hold values from -0.1875 to 0.1875
- expand_weight: bfloat16 [4, 1024, 4096], P('section', None, 'mp'), may hold values from -0.1875 to 0.1875
- expand_bias: bfloat16 [4, 4096], P('section', 'mp'), may hold values from -3 to 3
- middle_gain: bfloat16 [4, 4096], P('section', 'mp'), may hold values from 0.099609375 to 1.8984375
- middle_bias: bfloat16 [4, 4096], P('section', 'mp'), may hold values from -1.75 to 1.75
- reduce_weight: bfloat16 [4, 4096, 1024], P('section', 'mp'), may hold values from -0.09375 to 0.09375
- branch_bias: bfloat16 [4, 2, 1024], P('section'), may hold values from -1.75 to 1.75
Outputs:
- hidden_states: bfloat16 [4, 4, 2, 1024, 1024], P('section', 'batch', None, 'mp')
- input_gradient: bfloat16 [4, 4, 2, 1024, 1024], P('section', 'batch', None, 'mp')
- pre_gain_gradient: float32 [4, 2, 1024], P('section')
- pre_bias_gradient: float32 [4, 2, 1024], P('section')
- project_weight_gradient: float32 [4, 3, 1024, 1024], P('section', None, None, 'mp')
- project_bias_gradient: float32 [4, 2, 1024], P('section', None, 'mp')
- head_scale_gradient: float32 [4, 16], P('section', 'mp')
- post_gain_gradient: float32 [4, 1024], P('section', 'mp')
- post_bias_gradient: float32 [4, 1024], P('section', 'mp')
- output_weight_gradient: float32 [4, 1024, 1024], P('section', 'mp')
- expand_weight_gradient: float32 [4, 1024, 4096], P('section', None, 'mp')
- expand_bias_gradient: float32 [4, 4096], P('section', 'mp')
- middle_gain_gradient: float32 [4, 4096], P('section', 'mp')
- middle_bias_gradient: float32 [4, 4096], P('section', 'mp')
- reduce_weight_gradient: float32 [4, 4096, 1024], P('section', 'mp')
- branch_bias_gradient: float32 [4, 2, 1024], P('section')
Inputs may be any that keep to these rules, and one draw needn't show every extreme that they name: `document_starts`: each row's offsets are non-decreasing and begin with 0; in every batch shard one of its 2 x 1 row is a single document (all offsets 0).
All inputs are finite; a program needn't handle non-finite values.
Results may differ from a plain program's by a relative error of at most 0.025.
Values may be sent and summed in bfloat16 or wider, within the bound.
No kernel may reach another device: no remote copies, remote signals or barrier semaphores. Data moves between devices by JAX's collectives and lax.ppermute only.
A program may use at most 512 MiB of HBM per device.

v0:
```python
from functools import partial

import jax
import jax.numpy as jnp
from jax import lax
from jax.experimental import pallas as pl
from jax.experimental.pallas import tpu as pltpu
from jax.sharding import PartitionSpec as P

EPSILON = 1e-05
CHUNK = 128
KEYS = 256
TILE = 512
HIDE = -1e30
F32 = jnp.float32
BF16 = jnp.bfloat16
VMEM = pl.BlockSpec(memory_space=pltpu.VMEM)
SMEM = pl.BlockSpec(memory_space=pltpu.SMEM)
HBM = pl.BlockSpec(memory_space=pltpu.HBM)


def dot_nn(left, right):
    return jnp.dot(left, right, preferred_element_type=F32)


def dot_nt(left, right):
    return lax.dot_general(left, right, (((1,), (1,)), ((), ())), preferred_element_type=F32)


def dot_tn(left, right):
    return lax.dot_general(left, right, (((0,), (0,)), ((), ())), preferred_element_type=F32)


def norm_parts(values):
    centre = values - jnp.mean(values, axis=-1, keepdims=True)
    inv_std = lax.rsqrt(jnp.mean(centre * centre, axis=-1, keepdims=True) + EPSILON)
    return centre * inv_std, inv_std


def norm_back(scaled, normed, inv_std):
    mean_one = jnp.mean(scaled, axis=-1, keepdims=True)
    mean_two = jnp.mean(scaled * normed, axis=-1, keepdims=True)
    return inv_std * (scaled - mean_one - normed * mean_two)


def column_sum(values):
    return jnp.sum(values, axis=0, keepdims=True)


def document_start(starts_ref, place):
    first = jnp.zeros_like(place)
    for k in range(starts_ref.shape[0]):
        start = starts_ref[k]
        first = jnp.maximum(first, jnp.where(place >= start, start, 0))
    return first


def half_masks():
    lane = lax.broadcasted_iota(jnp.int32, (1, 128), 1)
    return (lane < 64).astype(BF16), (lane >= 64).astype(BF16)


def stack_heads(pair):
    even, odd = half_masks()
    return jnp.concatenate([pair * even, pair * odd], axis=0)


def pick_heads(stacked):
    rows = stacked.shape[0] // 2
    lane = lax.broadcasted_iota(jnp.int32, (1, 128), 1)
    return jnp.where(lane < 64, stacked[:rows], stacked[rows:])


def copies_of(pairs, sems):
    return [pltpu.make_async_copy(a, b, sems.at[i]) for i, (a, b) in enumerate(pairs)]


def attend_kernel(
    tick_ref, section_ref, starts_ref, tok_ref, inc_ref, wp_a, wp_b, wo_a, wo_b, vec_ref,
    k_in, v_in, x_in, h1_in, q_in, o_in, lse_in, post_in, mid_in,
    k_ref, v_ref, x_buf, h1_buf, q_buf, o_buf, lse_buf, post_buf, mid_buf, mid_ref,
    x_s, h1_s, q_s, o_s, lse_s, post_s, hide_s, sems,
):
    del k_in, v_in, x_in, h1_in, q_in, o_in, lse_in, post_in, mid_in
    rows = mid_ref.shape[0]
    length, width = k_ref.shape
    half = width // 2
    section = section_ref[0]
    chunk = tick_ref[0] - 2 * section
    live = (chunk >= 0) & (chunk < length // rows)

    @pl.when(live)
    def _():
        first = pl.multiple_of(chunk * rows, rows)
        here = pl.ds(first, rows)

        @pl.when(section == 0)
        def _():
            x_s[...] = tok_ref[here, :]

        @pl.when(section != 0)
        def _():
            x_s[...] = inc_ref[...]

        layer_in = x_s[...].astype(F32)
        normed, _ = norm_parts(layer_in)
        h1 = (normed * vec_ref[0:1] + vec_ref[1:2]).astype(BF16)
        h1_s[...] = h1
        for side, weight in ((0, wp_a), (1, wp_b)):
            at = slice(side * half, (side + 1) * half)
            q = (dot_nn(h1, weight[0]) + vec_ref[2:3, at]).astype(BF16)
            q_s[:, at] = q * jnp.asarray(0.125, BF16)
            k_ref[here, at] = dot_nn(h1, weight[1]).astype(BF16)
            v_ref[here, at] = (dot_nn(h1, weight[2]) + vec_ref[3:4, at]).astype(BF16)

        def attend(keys):
            place = first + lax.broadcasted_iota(jnp.int32, (rows, 1), 0)
            start = document_start(starts_ref, place)
            key_at = lax.broadcasted_iota(jnp.int32, (rows, keys), 1)
            hide_s[:, :keys] = jnp.where((key_at <= place) & (key_at >= start), 0.0, HIDE)
            lane = lax.broadcasted_iota(jnp.int32, (rows, 128), 1)

            def one_pair(pair, lse):
                at = pl.ds(pl.multiple_of(pair * 128, 128), 128)
                queries = stack_heads(q_s[:, at])
                hide = hide_s[:, :keys]
                scores = dot_nt(queries, k_ref[0:keys, at]) + jnp.concatenate([hide, hide], axis=0)
                top = jnp.max(scores, axis=-1, keepdims=True)
                raised = jnp.exp(scores - top)
                total = jnp.sum(raised, axis=-1, keepdims=True)
                out = dot_nn(raised.astype(BF16), v_ref[0:keys, at]) / total
                o_s[:, at] = pick_heads(out)
                now = top + jnp.log(total)
                lse = jnp.where(lane == 2 * pair, now[:rows], lse)
                return jnp.where(lane == 2 * pair + 1, now[rows:], lse)

            lse = lax.fori_loop(0, width // 128, one_pair, jnp.zeros((rows, 128), F32))
            lse_s[...] = lse.T

        for count in range(length // KEYS):

            @pl.when(first // KEYS == count)
            def _():
                attend((count + 1) * KEYS)

        post_normed, _ = norm_parts(o_s[...] * vec_ref[4:5])
        post = (post_normed * vec_ref[5:6] + vec_ref[6:7]).astype(BF16)
        post_s[...] = post
        mid_ref[...] = (
            layer_in + dot_nn(post[:, :half], wo_a[...]) + dot_nn(post[:, half:], wo_b[...])
            + vec_ref[7:8]
        )
        copies = copies_of(
            (
                (x_s, x_buf.at[here]), (h1_s, h1_buf.at[here]), (q_s, q_buf.at[here]),
                (o_s, o_buf.at[here]), (lse_s, lse_buf.at[chunk]), (post_s, post_buf.at[here]),
                (mid_ref, mid_buf.at[here]),
            ),
            sems,
        )
        for copy in copies:
            copy.start()
        for copy in copies:
            copy.wait()


def gelu_parts(pre):
    phi = 0.5 + 0.5 * lax.erf(pre * 0.7071067811865476)
    density = jnp.exp(pre * pre * -0.5) * 0.3989422804014327
    return pre * phi, phi + pre * density


def expand_kernel(
    tick_ref, section_ref, mid_ref, we_a, we_b, wr_a, wr_b, vec_ref, wide_ref,
    h2_in, g_in, gp_in, m_in, st_in, hid_in,
    h2_buf, g_buf, gp_buf, m_buf, st_buf, hid_buf, out_ref,
    h2_s, gf_s, g_s, gp_s, m_s, st_s, sems,
):
    del h2_in, g_in, gp_in, m_in, st_in, hid_in
    rows = mid_ref.shape[0]
    half = we_a.shape[1]
    units = 2 * half
    length = h2_buf.shape[0]
    chunk = tick_ref[0] - 2 * section_ref[0]

    @pl.when((chunk >= 0) & (chunk < length // rows))
    def _():
        here = pl.ds(pl.multiple_of(chunk * rows, rows), rows)
        normed, _ = norm_parts(mid_ref[...])
        h2 = (normed * vec_ref[0:1] + vec_ref[1:2]).astype(BF16)
        h2_s[...] = h2
        total = jnp.zeros((rows, 1), F32)
        for tile in range(units // TILE):
            weight = we_a if tile * TILE < half else we_b
            inner = tile * TILE % half
            at = slice(tile * TILE, (tile + 1) * TILE)
            pre = dot_nn(h2, weight[:, inner:inner + TILE]) + wide_ref[0:1, at]
            active, slope = gelu_parts(pre)
            gf_s[:, at] = active
            g_s[:, at] = active.astype(BF16)
            gp_s[:, at] = slope.astype(BF16)
            total += jnp.sum(active, axis=-1, keepdims=True)
        mean = total / units
        square = jnp.zeros((rows, 1), F32)
        for tile in range(units // TILE):
            centre = gf_s[:, tile * TILE:(tile + 1) * TILE] - mean
            square += jnp.sum(centre * centre, axis=-1, keepdims=True)
        inv_std = lax.rsqrt(square / units + EPSILON)
        lane = lax.broadcasted_iota(jnp.int32, (rows, 128), 1)
        st_s[...] = jnp.where(lane == 0, mean, inv_std)
        out = mid_ref[...] + vec_ref[2:3]
        for tile in range(units // TILE):
            weight = wr_a if tile * TILE < half else wr_b
            inner = tile * TILE % half
            at = slice(tile * TILE, (tile + 1) * TILE)
            active = (gf_s[:, at] - mean) * inv_std * wide_ref[1:2, at] + wide_ref[2:3, at]
            active = active.astype(BF16)
            m_s[:, at] = active
            out += dot_nn(active, weight[inner:inner + TILE, :])
        out_ref[...] = out.astype(BF16)
        copies = copies_of(
            (
                (h2_s, h2_buf.at[here]), (g_s, g_buf.at[here]), (gp_s, gp_buf.at[here]),
                (m_s, m_buf.at[here]), (st_s, st_buf.at[here]), (out_ref, hid_buf.at[here]),
            ),
            sems,
        )
        for copy in copies:
            copy.start()
        for copy in copies:
            copy.wait()


def expand_back_kernel(
    tick_ref, section_ref, cot_ref, inc_ref, wr_a, wr_b, we_a, we_b, vec_ref, wide_ref,
    g_buf, gp_buf, st_buf, mid_buf,
    sum_in, wsum_in, df_in, dur_in, dmr_in,
    sum_ref, wsum_ref, df_buf, dur_buf, dmr_buf, dmid_ref,
    g_s, gp_s, st_s, mid_s, df_s, z_s, dur_s, dmr_s, in_sems, out_sems,
):
    del sum_in, wsum_in, df_in, dur_in, dmr_in
    rows = dmid_ref.shape[0]
    half = wr_a.shape[1]
    units = 2 * half
    length = g_buf.shape[0]
    count = length // rows
    section = section_ref[0]
    last = section_ref[1] - 1
    chunk = count - 1 - (tick_ref[0] - 2 * (last - section))

    @pl.when((chunk >= 0) & (chunk < count))
    def _():
        here = pl.ds(pl.multiple_of(chunk * rows, rows), rows)
        loads = copies_of(
            (
                (g_buf.at[here], g_s), (gp_buf.at[here], gp_s), (st_buf.at[here], st_s),
                (mid_buf.at[here], mid_s),
            ),
            in_sems,
        )
        for copy in loads:
            copy.start()

        @pl.when(section == last)
        def _():
            df_s[...] = cot_ref[here, :]

        @pl.when(section != last)
        def _():
            df_s[...] = inc_ref[...]

        grad_low = df_s[...]
        sum_ref[0:1] += column_sum(grad_low.astype(F32))
        for copy in loads:
            copy.wait()
        mean = st_s[:, 0:1]
        inv_std = st_s[:, 1:2]
        one = jnp.zeros((rows, 1), F32)
        two = jnp.zeros((rows, 1), F32)
        for tile in range(units // TILE):
            weight = wr_a if tile * TILE < half else wr_b
            inner = tile * TILE % half
            at = slice(tile * TILE, (tile + 1) * TILE)
            grad = dot_nn(grad_low, weight[:, inner:inner + TILE])
            normed = (g_s[:, at].astype(F32) - mean) * inv_std
            wsum_ref[0:1, at] += column_sum(grad * normed)
            wsum_ref[1:2, at] += column_sum(grad)
            scaled = grad * wide_ref[1:2, at]
            z_s[:, at] = scaled
            one += jnp.sum(scaled, axis=-1, keepdims=True)
            two += jnp.sum(scaled * normed, axis=-1, keepdims=True)
        one = one / units
        two = two / units
        grad_second = jnp.zeros((rows, dmid_ref.shape[1]), F32)
        for tile in range(units // TILE):
            weight = we_a if tile * TILE < half else we_b
            inner = tile * TILE % half
            at = slice(tile * TILE, (tile + 1) * TILE)
            normed = (g_s[:, at].astype(F32) - mean) * inv_std
            grad = inv_std * (z_s[:, at] - one - normed * two) * gp_s[:, at].astype(F32)
            wsum_ref[2:3, at] += column_sum(grad)
            low = grad.astype(BF16)
            dur_s[:, at] = low
            grad_second += dot_nn(low, weight[inner:inner + TILE, :])
        normed, inv_std = norm_parts(mid_s[...])
        sum_ref[1:2] += column_sum(grad_second * normed)
        sum_ref[2:3] += column_sum(grad_second)
        grad_mid = grad_low.astype(F32) + norm_back(grad_second * vec_ref[0:1], normed, inv_std)
        sum_ref[3:4] += column_sum(grad_mid)
        dmid_ref[...] = grad_mid
        dmr_s[...] = grad_mid.astype(BF16)
        stores = copies_of(
            ((df_s, df_buf.at[here]), (dur_s, dur_buf.at[here]), (dmr_s, dmr_buf.at[here])),
            out_sems,
        )
        for copy in stores:
            copy.start()
        for copy in stores:
            copy.wait()


def attend_back_kernel(
    tick_ref, section_ref, starts_ref, dmid_ref, wo_a, wo_b, wp_a, wp_b, vec_ref, k_ref, v_ref,
    x_buf, q_buf, o_buf, lse_buf,
    sum_in, dk_in, dv_in, dq_in, dkr_in, dvr_in, ig_in,
    sum_ref, dk_ref, dv_ref, dq_buf, dkr_buf, dvr_buf, ig_buf, out_ref,
    x_s, q_s, o_s, lse_s, do_s, dqf_s, hide_s, dq_s, dkr_s, dvr_s, in_sems, out_sems,
):
    del sum_in, dk_in, dv_in, dq_in, dkr_in, dvr_in, ig_in
    rows = dmid_ref.shape[0]
    length, width = k_ref.shape
    half = width // 2
    count = length // rows
    section = section_ref[0]
    last = section_ref[1] - 1
    chunk = count - 1 - (tick_ref[0] - 2 * (last - section))

    @pl.when((chunk >= 0) & (chunk < count))
    def _():
        first = pl.multiple_of(chunk * rows, rows)
        here = pl.ds(first, rows)
        loads = copies_of(
            (
                (x_buf.at[here], x_s), (q_buf.at[here], q_s), (o_buf.at[here], o_s),
                (lse_buf.at[chunk], lse_s),
            ),
            in_sems,
        )
        for copy in loads:
            copy.start()

        @pl.when(chunk == count - 1)
        def _():
            dk_ref[...] = jnp.zeros_like(dk_ref)
            dv_ref[...] = jnp.zeros_like(dv_ref)

        low = dmid_ref[...].astype(BF16)
        grad_post = jnp.concatenate([dot_nn(low, wo_a[...]), dot_nn(low, wo_b[...])], axis=1)
        for copy in loads:
            copy.wait()
        attended = o_s[...]
        normed, inv_std = norm_parts(attended * vec_ref[4:5])
        sum_ref[0:1] += column_sum(grad_post * normed)
        sum_ref[1:2] += column_sum(grad_post)
        grad_mixed = norm_back(grad_post * vec_ref[5:6], normed, inv_std)
        sum_ref[2:3] += column_sum(grad_mixed * attended)
        do_s[...] = (grad_mixed * vec_ref[4:5]).astype(BF16)

        def attend(keys):
            place = first + lax.broadcasted_iota(jnp.int32, (1, rows), 1)
            start = document_start(starts_ref, place)
            key_at = lax.broadcasted_iota(jnp.int32, (keys, rows), 0)
            hide_s[:keys, :] = jnp.where((key_at <= place) & (key_at >= start), 0.0, HIDE)

            def one_pair(pair, carry):
                at = pl.ds(pl.multiple_of(pair * 128, 128), 128)
                queries = stack_heads(q_s[:, at])
                grad_pair = do_s[:, at]
                grads = stack_heads(grad_pair)
                product = (grad_pair.astype(F32) * o_s[:, at]).T
                delta = jnp.concatenate(
                    [column_sum(product[:64]), column_sum(product[64:])], axis=1
                )
                lse = jnp.concatenate(
                    [lse_s[pl.ds(2 * pair, 1), :], lse_s[pl.ds(2 * pair + 1, 1), :]], axis=1
                )
                hide = hide_s[:keys, :]
                key_pair = k_ref[0:keys, at]
                scores = dot_nt(key_pair, queries) + jnp.concatenate([hide, hide], axis=1)
                probs = jnp.exp(scores - lse)
                grad_probs = dot_nt(v_ref[0:keys, at], grads)
                grad_scores = (probs * (grad_probs - delta)).astype(BF16)
                dk_ref[0:keys, at] += dot_nn(grad_scores, queries)
                dv_ref[0:keys, at] += dot_nn(probs.astype(BF16), grads)
                dqf_s[:, at] = pick_heads(dot_tn(grad_scores, key_pair)) * 0.125
                return carry

            lax.fori_loop(0, width // 128, one_pair, 0)

        for number in range(length // KEYS):

            @pl.when(first // KEYS == number)
            def _():
                attend((number + 1) * KEYS)

        grad_query = dqf_s[...]
        grad_value = dv_ref[here, :]
        sum_ref[3:4] += column_sum(grad_query)
        sum_ref[4:5] += column_sum(grad_value)
        dq_s[...] = grad_query.astype(BF16)
        dkr_s[...] = dk_ref[here, :].astype(BF16)
        dvr_s[...] = grad_value.astype(BF16)
        grad_first = jnp.zeros((rows, width), F32)
        for number, part in enumerate((dq_s, dkr_s, dvr_s)):
            grad_first += dot_nn(part[:, :half], wp_a[number])
            grad_first += dot_nn(part[:, half:], wp_b[number])
        normed, inv_std = norm_parts(x_s[...].astype(F32))
        sum_ref[5:6] += column_sum(grad_first * normed)
        sum_ref[6:7] += column_sum(grad_first)
        out = dmid_ref[...] + norm_back(grad_first * vec_ref[0:1], normed, inv_std)
        out_ref[...] = out.astype(BF16)
        stores = copies_of(
            (
                (dq_s, dq_buf.at[here]), (dkr_s, dkr_buf.at[here]), (dvr_s, dvr_buf.at[here]),
                (out_ref, ig_buf.at[here]),
            ),
            out_sems,
        )
        for copy in stores:
            copy.start()
        for copy in stores:
            copy.wait()


def flip_kernel(in_ref, out_ref):
    size = in_ref.shape[0]
    across = lax.broadcasted_iota(jnp.int32, (size, size), 1)
    down = lax.broadcasted_iota(jnp.int32, (size, size), 0)
    same = (across == down).astype(BF16)
    width = in_ref.shape[1]
    for part in range(width // size):
        at = slice(part * size, (part + 1) * size)
        out_ref[at, :] = dot_nt(same, in_ref[:, at]).astype(BF16)


def flipped(weight):
    rows, columns = weight.shape
    size = 256
    return pl.pallas_call(
        flip_kernel,
        grid=(rows // size,),
        in_specs=[pl.BlockSpec((size, columns), lambda i: (i, 0))],
        out_specs=pl.BlockSpec((columns, size), lambda i: (0, i)),
        out_shape=jax.ShapeDtypeStruct((columns, rows), weight.dtype),
        compiler_params=pltpu.CompilerParams(vmem_limit_bytes=16 * 2**20),
    )(weight)


def empty_kernel(*refs):
    del refs


def empty(shapes):
    return pl.pallas_call(
        empty_kernel,
        out_specs=[HBM] * len(shapes),
        out_shape=[pltpu.HBM(shape, dtype) for shape, dtype in shapes],
    )()


def call(kernel, inputs, specs, carried, carried_specs, fresh, fresh_specs, scratch, limit, flops):
    first = len(inputs)
    shapes = [
        pltpu.HBM(a.shape, a.dtype) if spec is HBM else jax.ShapeDtypeStruct(a.shape, a.dtype)
        for a, spec in zip(carried, carried_specs)
    ] + fresh
    return pl.pallas_call(
        kernel,
        in_specs=specs + carried_specs,
        out_specs=carried_specs + fresh_specs,
        out_shape=shapes,
        scratch_shapes=scratch,
        input_output_aliases={first + i: i for i in range(len(carried))},
        compiler_params=pltpu.CompilerParams(vmem_limit_bytes=limit),
        cost_estimate=pl.CostEstimate(flops=flops, bytes_accessed=2**22, transcendentals=0),
    )(*inputs, *carried)


def local(
    tokens, cotangent, document_starts, pre_gain, pre_bias, project_weight, project_bias,
    head_scale, post_gain, post_bias, output_weight, expand_weight, expand_bias, middle_gain,
    middle_bias, reduce_weight, branch_bias,
):
    sections = lax.axis_size("section")
    section = lax.axis_index("section")
    parts = lax.axis_size("mp")
    part = lax.axis_index("mp")
    micro, rows_here, width = tokens.shape[1:]
    length = rows_here * parts
    chunk = CHUNK
    count = length // chunk
    heads = head_scale.shape[1] * parts
    head = width // heads
    units = expand_bias.shape[1] * parts
    paired = parts == 2 and micro == 2

    if paired:

        def swapped(value):
            return lax.ppermute(value, "mp", [(0, 1), (1, 0)])

        def both(value, axis):
            del axis
            return value, swapped(value)

        def whole_rows(value):
            mine = lax.dynamic_index_in_dim(value, part, 0, keepdims=False)
            theirs = swapped(lax.dynamic_index_in_dim(value, 1 - part, 0, keepdims=False))
            return jnp.where(
                part == 0, jnp.concatenate([mine, theirs]), jnp.concatenate([theirs, mine])
            )

        def spread_rows(value):
            mine = lax.dynamic_slice_in_dim(value, part * rows_here, rows_here, 0)
            theirs = swapped(
                lax.dynamic_slice_in_dim(value, (1 - part) * rows_here, rows_here, 0)
            )
            return jnp.where(part == 0, jnp.stack([mine, theirs]), jnp.stack([theirs, mine]))

        def owned_sum(own, other):
            return own + swapped(other).astype(F32)

        block = part
        copies = 1.0
    else:

        def both(value, axis):
            whole = lax.all_gather(value, "mp", axis=axis, tiled=True)
            return tuple(jnp.split(whole, 2, axis=axis))

        def whole_rows(value):
            whole = lax.all_gather(value, "mp", axis=1, tiled=True)
            return lax.dynamic_index_in_dim(whole, part * micro // parts, 0, keepdims=False)

        def spread_rows(value):
            whole = lax.all_gather(value, "mp", axis=0)
            whole = whole[:: parts // micro]
            return lax.dynamic_slice_in_dim(whole, part * rows_here, rows_here, 1)

        block = part * micro // parts
        copies = micro / parts

    def wide(value, axis=0):
        return jnp.concatenate(both(value, axis), axis=axis)

    split = jnp.concatenate(
        [
            project_bias[0], jnp.repeat(head_scale[0], head)[None], post_gain, post_bias,
            expand_bias.reshape(-1, width // parts), middle_gain.reshape(-1, width // parts),
            middle_bias.reshape(-1, width // parts),
        ]
    )
    split_own, split_other = both(split, 1) if paired else (None, None)
    ratio = units // width

    def feature(first):
        if paired:
            return jnp.concatenate([split_own[first], split_other[first]]).astype(F32)
        return wide(split[first]).astype(F32)

    def unit(first):
        if paired:
            return jnp.concatenate(
                [split_own[first:first + ratio], split_other[first:first + ratio]]
            ).reshape(-1).astype(F32)
        return wide(split[first:first + ratio].reshape(-1)).astype(F32)

    gains = pre_gain[0].astype(F32)
    shifts = pre_bias[0].astype(F32)
    branch = branch_bias[0].astype(F32)
    vec_a = jnp.stack(
        [gains[0], shifts[0], feature(0), feature(1), feature(2), feature(3), feature(4), branch[0]]
    )
    vec_f = jnp.stack([gains[1], shifts[1], branch[1]])
    wide_f = jnp.stack([unit(5), unit(5 + ratio), unit(5 + 2 * ratio)])

    wp_a, wp_b = both(project_weight[0], 2)
    wo_a, wo_b = both(output_weight[0], 0)
    we_a, we_b = both(expand_weight[0], 1)
    wr_a, wr_b = both(reduce_weight[0], 0)
    token_rows = whole_rows(tokens[0])
    cotangent_rows = whole_rows(cotangent[0])
    starts = lax.dynamic_index_in_dim(document_starts[0], block, 0, keepdims=False)[0]
    place = jnp.stack([section, jnp.int32(sections)]).astype(jnp.int32)

    def sized(columns, dtype):
        return ((length, columns), dtype)

    (
        x_buf, h1_buf, q_buf, o_buf, lse_buf, post_buf, mid_buf,
        h2_buf, g_buf, gp_buf, m_buf, st_buf, hid_buf,
        df_buf, dur_buf, dmr_buf, dq_buf, dkr_buf, dvr_buf, ig_buf, dk_acc, dv_acc,
    ) = empty(
        [
            sized(width, BF16), sized(width, BF16), sized(width, BF16), sized(width, F32),
            ((count, 128, chunk), F32), sized(width, BF16), sized(width, F32),
            sized(width, BF16), sized(units, BF16), sized(units, BF16), sized(units, BF16),
            sized(128, F32), sized(width, BF16),
            sized(width, BF16), sized(units, BF16), sized(width, BF16), sized(width, BF16),
            sized(width, BF16), sized(width, BF16), sized(width, BF16), sized(width, F32),
            sized(width, F32),
        ]
    )
    k_all = jnp.zeros((length, width), BF16)
    v_all = jnp.zeros((length, width), BF16)
    dma = pltpu.SemaphoreType.DMA
    dense = 2 * chunk * width

    def shifted(value, distance):
        route = [(i, i + distance) for i in range(sections) if 0 <= i + distance < sections]
        return lax.ppermute(value, "section", route)

    ticks = count + 2 * (sections - 1)
    blank = jnp.zeros((chunk, width), BF16)
    incoming = blank
    sent = None
    for tick in range(ticks):
        now = jnp.full((1,), tick, jnp.int32)
        arriving = shifted(sent, 1) if sent is not None and tick + 1 < ticks else blank
        (
            k_all, v_all, x_buf, h1_buf, q_buf, o_buf, lse_buf, post_buf, mid_buf, middle,
        ) = call(
            attend_kernel,
            (now, place, starts, token_rows, incoming, wp_a, wp_b, wo_a, wo_b, vec_a),
            [SMEM, SMEM, SMEM] + [VMEM] * 7,
            (k_all, v_all, x_buf, h1_buf, q_buf, o_buf, lse_buf, post_buf, mid_buf),
            [VMEM, VMEM] + [HBM] * 7,
            [jax.ShapeDtypeStruct((chunk, width), F32)],
            [VMEM],
            [
                pltpu.VMEM((chunk, width), BF16), pltpu.VMEM((chunk, width), BF16),
                pltpu.VMEM((chunk, width), BF16), pltpu.VMEM((chunk, width), F32),
                pltpu.VMEM((128, chunk), F32), pltpu.VMEM((chunk, width), BF16),
                pltpu.VMEM((chunk, length), F32), dma((7,)),
            ],
            24 * 2**20,
            8 * dense * width,
        )
        h2_buf, g_buf, gp_buf, m_buf, st_buf, hid_buf, sent = call(
            expand_kernel,
            (now, place, middle, we_a, we_b, wr_a, wr_b, vec_f, wide_f),
            [SMEM, SMEM] + [VMEM] * 7,
            (h2_buf, g_buf, gp_buf, m_buf, st_buf, hid_buf),
            [HBM] * 6,
            [jax.ShapeDtypeStruct((chunk, width), BF16)],
            [VMEM],
            [
                pltpu.VMEM((chunk, width), BF16), pltpu.VMEM((chunk, units), F32),
                pltpu.VMEM((chunk, units), BF16), pltpu.VMEM((chunk, units), BF16),
                pltpu.VMEM((chunk, units), BF16), pltpu.VMEM((chunk, 128), F32), dma((6,)),
            ],
            24 * 2**20,
            2 * dense * units,
        )
        incoming = arriving

    wrt_a, wrt_b = flipped(wr_a), flipped(wr_b)
    wet_a, wet_b = flipped(we_a), flipped(we_b)
    wot_a, wot_b = flipped(wo_a), flipped(wo_b)
    wpt_a = jnp.stack([flipped(wp_a[i]) for i in range(3)])
    wpt_b = jnp.stack([flipped(wp_b[i]) for i in range(3)])
    sum_f = jnp.zeros((4, width), F32)
    sum_w = jnp.zeros((3, units), F32)
    sum_a = jnp.zeros((7, width), F32)
    incoming = blank
    sent = None
    for tick in range(ticks):
        now = jnp.full((1,), tick, jnp.int32)
        arriving = shifted(sent, -1) if sent is not None and tick + 1 < ticks else blank
        sum_f, sum_w, df_buf, dur_buf, dmr_buf, grad_mid = call(
            expand_back_kernel,
            (
                now, place, cotangent_rows, incoming, wrt_a, wrt_b, wet_a, wet_b, vec_f, wide_f,
                g_buf, gp_buf, st_buf, mid_buf,
            ),
            [SMEM, SMEM] + [VMEM] * 8 + [HBM] * 4,
            (sum_f, sum_w, df_buf, dur_buf, dmr_buf),
            [VMEM, VMEM] + [HBM] * 3,
            [jax.ShapeDtypeStruct((chunk, width), F32)],
            [VMEM],
            [
                pltpu.VMEM((chunk, units), BF16), pltpu.VMEM((chunk, units), BF16),
                pltpu.VMEM((chunk, 128), F32), pltpu.VMEM((chunk, width), F32),
                pltpu.VMEM((chunk, width), BF16), pltpu.VMEM((chunk, units), F32),
                pltpu.VMEM((chunk, units), BF16), pltpu.VMEM((chunk, width), BF16),
                dma((4,)), dma((3,)),
            ],
            24 * 2**20,
            2 * dense * units,
        )
        sum_a, dk_acc, dv_acc, dq_buf, dkr_buf, dvr_buf, ig_buf, sent = call(
            attend_back_kernel,
            (
                now, place, starts, grad_mid, wot_a, wot_b, wpt_a, wpt_b, vec_a, k_all, v_all,
                x_buf, q_buf, o_buf, lse_buf,
            ),
            [SMEM, SMEM, SMEM] + [VMEM] * 8 + [HBM] * 4,
            (sum_a, dk_acc, dv_acc, dq_buf, dkr_buf, dvr_buf, ig_buf),
            [VMEM, VMEM, VMEM] + [HBM] * 4,
            [jax.ShapeDtypeStruct((chunk, width), BF16)],
            [VMEM],
            [
                pltpu.VMEM((chunk, width), BF16), pltpu.VMEM((chunk, width), BF16),
                pltpu.VMEM((chunk, width), F32), pltpu.VMEM((128, chunk), F32),
                pltpu.VMEM((chunk, width), BF16), pltpu.VMEM((chunk, width), F32),
                pltpu.VMEM((length, chunk), F32), pltpu.VMEM((chunk, width), BF16),
                pltpu.VMEM((chunk, width), BF16), pltpu.VMEM((chunk, width), BF16),
                dma((4,)), dma((4,)),
            ],
            24 * 2**20,
            12 * dense * width,
        )
        incoming = arriving

    def weight_gradient(left, right, axis):
        whole = left.shape[1], right.shape[1]
        if paired:
            cut = whole[axis] // 2
            pieces = []
            for side in (1, 0):
                a, b = left, right
                if axis == 0:
                    a = left[:, side * cut:(side + 1) * cut]
                else:
                    b = right[:, side * cut:(side + 1) * cut]
                pieces.append(dot_tn(a, b))
            return (pieces[1] + swapped(pieces[0].astype(BF16)).astype(F32)).astype(BF16)
        full = dot_tn(left, right).astype(BF16)
        summed = lax.psum_scatter(full, "mp", scatter_dimension=axis, tiled=True)
        return (summed.astype(F32) * copies).astype(BF16)

    def over_batch(value):
        return lax.psum(value, "batch").astype(F32)

    reduce_grad = over_batch(weight_gradient(m_buf, df_buf, 0))
    expand_grad = over_batch(weight_gradient(h2_buf, dur_buf, 1))
    output_grad = weight_gradient(post_buf, dmr_buf, 0)
    project_grad = jnp.stack(
        [weight_gradient(h1_buf, right, 1) for right in (dq_buf, dkr_buf, dvr_buf)]
    )
    output_grad, project_grad = lax.psum((output_grad, project_grad), "batch")
    output_grad, project_grad = output_grad.astype(F32), project_grad.astype(F32)

    shared = jnp.stack([sum_a[5], sum_f[1], sum_a[6], sum_f[2], sum_f[3], sum_f[0]])
    narrow = jnp.stack([sum_a[3], sum_a[4], sum_a[2], sum_a[0], sum_a[1]])
    broad = jnp.stack([sum_w[2], sum_w[0], sum_w[1]])

    def packed(side):
        cut, wide_cut = width // 2, units // 2
        return jnp.concatenate(
            [
                shared.reshape(-1),
                narrow[:, side * cut:(side + 1) * cut].reshape(-1),
                broad[:, side * wide_cut:(side + 1) * wide_cut].reshape(-1),
            ]
        )

    if paired:
        small = lax.psum(owned_sum(packed(0), packed(1)), "batch")
        here, there = width // 2, units // 2
        shared = small[:6 * width].reshape(6, width)
        narrow = small[6 * width:6 * width + 5 * here].reshape(5, here)
        broad = small[6 * width + 5 * here:].reshape(3, there)
    else:
        small = lax.psum(
            jnp.concatenate([shared.reshape(-1), narrow.reshape(-1), broad.reshape(-1)]),
            ("batch", "mp"),
        ) * copies
        shared = small[:6 * width].reshape(6, width)
        narrow = small[6 * width:11 * width].reshape(5, width)
        broad = small[11 * width:].reshape(3, units)
        narrow = lax.dynamic_slice_in_dim(narrow, part * (width // parts), width // parts, 1)
        broad = lax.dynamic_slice_in_dim(broad, part * (units // parts), units // parts, 1)

    return (
        spread_rows(hid_buf)[None, None],
        spread_rows(ig_buf)[None, None],
        shared[0:2][None],
        shared[2:4][None],
        project_grad[None],
        narrow[0:2][None],
        jnp.sum(narrow[2].reshape(-1, head), axis=1)[None],
        narrow[3][None],
        narrow[4][None],
        output_grad[None],
        expand_grad[None],
        broad[0][None],
        broad[1][None],
        broad[2][None],
        reduce_grad[None],
        shared[4:6][None],
    )


def solution(mesh):
    layered = P("section", None, None)
    split = P("section", "mp")
    rows = P("section", "mp", None)
    columns = P("section", None, "mp")
    projected = P("section", None, None, "mp")
    tokens = P("batch", None, "mp", None)
    states = P("section", "batch", None, "mp", None)
    return jax.shard_map(
        local,
        mesh=mesh,
        in_specs=(
            tokens, tokens, P("batch", None, None, None), layered, layered, projected, columns,
            split, split, split, rows, columns, split, split, split, rows, layered,
        ),
        out_specs=(
            states, states, layered, layered, projected, columns, split, split, split, rows,
            columns, split, split, split, rows, layered,
        ),
        check_vma=False,
    )
```

profile of v0, /device:TPU:0, one launch (start us, length us, event | category | flops | bytes accessed | tf_op | source)
XLA Modules:
  0.0 1147.7 jit_solution(1922448619802151342)
XLA Ops:
  61.0 8.6 shard_map.289
  72.9 8.6 shard_map.291
  82.8 8.4 shard_map.290
  91.3 8.4 shard_map.292
  115.9 8.8 shard_map.293
  134.4 9.2 shard_map.294
  143.6 8.4 shard_map.296
  153.4 10.1 shard_map.297
  173.3 10.5 shard_map.298
  193.5 10.6 shard_map.301
  213.8 11.1 shard_map.302
  245.3 10.6 shard_map.306
  274.4 10.3 shard_map.310
  296.8 11.5 shard_map.314
  378.3 9.7 shard_map.333
  425.3 8.5 shard_map.336
  472.9 9.7 shard_map.338
  525.9 12.6 %shard_map.343 = (f32[7,1024]{1,0:T(8,128)S(1)}, f32[1024,1024]{1,0:T(8,128)S(1)}, f32[1024,1024]{1,0:T(8,128)S(1)}, bf16[1024,1024]{1,0:T(8,128)(2,1)}, bf16[10...) custom-call(s32[1]{0:T(128)} %constant.68.clone.1.tick_ref, ...), custom_call_target="tpu_custom_call", output_to_operand_aliasing={{0}: (15, {}), {1}: (16, {}), {2}: (17, {}), {3}: (18, {}),... | custom-call | flops 3221225472 | bytes 4194304 | tf_op jit(solution)/shard_map/pallas_call | solution.py:477
  569.4 11.6 %shard_map.344 = (f32[7,1024]{1,0:T(8,128)S(1)}, f32[1024,1024]{1,0:T(8,128)S(1)}, f32[1024,1024]{1,0:T(8,128)S(1)}, bf16[1024,1024]{1,0:T(8,128)(2,1)}, bf16[10...) custom-call(s32[1]{0:T(128)} %constant.21.clone.1.tick_ref, ...), custom_call_target="tpu_custom_call", output_to_operand_aliasing={{0}: (15, {}), {1}: (16, {}), {2}: (17, {}), {3}: (18, {}),... | custom-call | flops 3221225472 | bytes 4194304 | tf_op jit(solution)/shard_map/pallas_call | solution.py:477
  594.0 10.0 shard_map.345
  615.0 10.2 shard_map.347
  656.1 10.6 shard_map.348
  697.7 9.1 shard_map.351
  723.9 8.5 shard_map.350
  772.1 23.4 %collective-permute-done.30.inc_ref = bf16[128,1024]{1,0:T(8,128)(2,1)S(1)} collective-permute-done((bf16[128,1024]{1,0:T(8,128)(2,1)S(1)}, bf16[128,1024]{1,0:T(8,128)(2,1)S(1)}, u32[]{:S(2)}, u32[]{:S(2)}) %collective-permute-start.30) | collective-permute-done | bytes 262176 | tf_op jit(solution)/shard_map/ppermute | solution.py:621
  795.5 9.2 shard_map.354
  804.7 9.6 fusion.13
  814.5 9.7 fusion.10
  825.6 11.5 %shard_map.355 = (f32[7,1024]{1,0:T(8,128)S(1)}, f32[1024,1024]{1,0:T(8,128)S(1)}, f32[1024,1024]{1,0:T(8,128)S(1)}, bf16[1024,1024]{1,0:T(8,128)(2,1)}, bf16[10...) custom-call(s32[1]{0:T(128)} %constant.71.clone.1.tick_ref, ...), custom_call_target="tpu_custom_call", output_to_operand_aliasing={{0}: (15, {}), {1}: (16, {}), {2}: (17, {}), {3}: (18, {}),... | custom-call | flops 3221225472 | bytes 4194304 | tf_op jit(solution)/shard_map/pallas_call | solution.py:477
  837.1 9.0 shard_map.356
  889.2 20.3 %psum.35 = f32[14848]{0:T(1024)S(1)} all-reduce(f32[14848]{0:T(1024)S(1)} %fusion.33), channel_id=1, replica_groups=mesh['section'=4,'batch'=4,'mp'=2] {'batch'}, use_global_device_ids=true, to_apply=%region_0.1 | all-reduce | flops 14848 | bytes 118784 | tf_op jit(solution)/shard_map/psum | solution.py:769
  915.5 208.7 %all-reduce.3.cloned.1.call-done = (bf16[1,3,1024,512]{3,2,1,0:T(8,128)(2,1)}, bf16[1,512,1024]{2,1,0:T(8,128)(2,1)}, bf16[1,1024,2048]{2,1,0:T(8,128)(2,1)}, bf16[1,2048,1024]{2,1,0:T(8,128)(2,1)}) async-done(((bf16[1,3,1024,512]{3,2,1,0:T(8,128)(2,1)}, bf16[1,512,1024]{2,1,0:T(8,128)(2,1)}, bf16[1,1024,2048]{2,1,0:T(8,128)(2,1)}, bf16[1,2048,1024]{2,1,0:T(8,128)(2,1)}), ...) | async-done | bytes 12582928 | tf_op jit(solution)/shard_map/psum | solution.py:751
  (684 shorter events, 594.0 us)
Async XLA Ops:
  7.2 1116.9 %all-reduce.3.cloned.1.call-start = ((), (), s32[]{:S(2)}) async-start(), calls=%async_computation | async-start | bytes 25165824 | tf_op jit(solution)/shard_map/psum | solution.py:751
  11.2 32.8 %collective-permute-start.3 = (bf16[17,512]{1,0:T(8,128)(2,1)S(1)}, bf16[17,512]{1,0:T(8,128)(2,1)S(1)}, u32[]{:S(2)}, u32[]{:S(2)}) collective-permute-start(bf16[17,512]{1,0:T(8,128)(2,1)S(1)} %concatenate.115), channel_id=1, source_target_pairs={{0,1},{1,0},{2,3},{3,2},{4,5},{5,4},{6,7},{7,6},{8,9},{9,8},{10,11... | collective-permute-start | bytes 52232 | tf_op jit(solution)/shard_map/ppermute | solution.py:510
  11.8 32.4 %collective-permute-start.2 = (bf16[512,1024]{1,0:T(8,128)(2,1)}, bf16[512,1024]{1,0:T(8,128)(2,1)S(1)}, u32[]{:S(2)}, u32[]{:S(2)}) collective-permute-start(bf16[512,1024]{1,0:T(8,128)(2,1)} %bitcast.148), channel_id=1, source_target_pairs={{0,1},{1,0},{2,3},{3,2},{4,5},{5,4},{6,7},{7,6},{8,9},{9,8},{10,11... | collective-permute-start | bytes 3145736 | tf_op jit(solution)/shard_map/ppermute | solution.py:510
  11.8 41.3 %collective-permute-start.1 = (bf16[3,1024,512]{2,1,0:T(8,128)(2,1)}, bf16[3,1024,512]{2,1,0:T(8,128)(2,1)}, u32[]{:S(2)}, u32[]{:S(2)}) collective-permute-start(bf16[3,1024,512]{2,1,0:T(8,128)(2,1)} %bitcast.133), channel_id=1, source_target_pairs={{0,1},{1,0},{2,3},{3,2},{4,5},{5,4},{6,7},{7,6},{8,9},{9,8},{10,11... | collective-permute-start | bytes 9437192 | tf_op jit(solution)/shard_map/ppermute | solution.py:510
  12.3 59.3 %collective-permute-start.4 = (bf16[1024,2048]{1,0:T(8,128)(2,1)}, bf16[1024,2048]{1,0:T(8,128)(2,1)}, u32[]{:S(2)}, u32[]{:S(2)}) collective-permute-start(bf16[1024,2048]{1,0:T(8,128)(2,1)} %bitcast.101), channel_id=1, source_target_pairs={{0,1},{1,0},{2,3},{3,2},{4,5},{5,4},{6,7},{7,6},{8,9},{9,8},{10,11... | collective-permute-start | bytes 12582920 | tf_op jit(solution)/shard_map/ppermute | solution.py:510
  12.4 59.2 %collective-permute-start.5 = (bf16[2048,1024]{1,0:T(8,128)(2,1)}, bf16[2048,1024]{1,0:T(8,128)(2,1)}, u32[]{:S(2)}, u32[]{:S(2)}) collective-permute-start(bf16[2048,1024]{1,0:T(8,128)(2,1)} %bitcast.117), channel_id=1, source_target_pairs={{0,1},{1,0},{2,3},{3,2},{4,5},{5,4},{6,7},{7,6},{8,9},{9,8},{10,11... | collective-permute-start | bytes 12582920 | tf_op jit(solution)/shard_map/ppermute | solution.py:510
  81.5 34.4 %collective-permute-start.7 = (bf16[128,1024]{1,0:T(8,128)(2,1)S(1)}, bf16[128,1024]{1,0:T(8,128)(2,1)S(1)}, u32[]{:S(2)}, u32[]{:S(2)}) collective-permute-start(bf16[128,1024]{1,0:T(8,128)(2,1)S(1)} %get-tuple-element.497), channel_id=1, source_target_pairs={{0,8},{8,16},{16,24},{1,9},{9,17},{17,25},{2,10},{10,18},{18,26},{... | collective-permute-start | bytes 786440 | tf_op jit(solution)/shard_map/ppermute | solution.py:621
  99.7 34.7 %collective-permute-start.6 = (bf16[128,1024]{1,0:T(8,128)(2,1)S(1)}, bf16[128,1024]{1,0:T(8,128)(2,1)S(1)}, u32[]{:S(2)}, u32[]{:S(2)}) collective-permute-start(bf16[128,1024]{1,0:T(8,128)(2,1)S(1)} %get-tuple-element.496), channel_id=1, source_target_pairs={{0,8},{8,16},{16,24},{1,9},{9,17},{17,25},{2,10},{10,18},{18,26},{... | collective-permute-start | bytes 786440 | tf_op jit(solution)/shard_map/ppermute | solution.py:621
  133.1 20.3 %collective-permute-start.9 = (bf16[128,1024]{1,0:T(8,128)(2,1)S(1)}, bf16[128,1024]{1,0:T(8,128)(2,1)S(1)}, u32[]{:S(2)}, u32[]{:S(2)}) collective-permute-start(bf16[128,1024]{1,0:T(8,128)(2,1)S(1)} %get-tuple-element.531), channel_id=1, source_target_pairs={{0,8},{8,16},{16,24},{1,9},{9,17},{17,25},{2,10},{10,18},{18,26},{... | collective-permute-start | bytes 786440 | tf_op jit(solution)/shard_map/ppermute | solution.py:621
  152.0 21.2 %collective-permute-start.8 = (bf16[128,1024]{1,0:T(8,128)(2,1)S(1)}, bf16[128,1024]{1,0:T(8,128)(2,1)S(1)}, u32[]{:S(2)}, u32[]{:S(2)}) collective-permute-start(bf16[128,1024]{1,0:T(8,128)(2,1)S(1)} %get-tuple-element.530), channel_id=1, source_target_pairs={{0,8},{8,16},{16,24},{1,9},{9,17},{17,25},{2,10},{10,18},{18,26},{... | collective-permute-start | bytes 786440 | tf_op jit(solution)/shard_map/ppermute | solution.py:621
  171.9 21.6 %collective-permute-start.11 = (bf16[128,1024]{1,0:T(8,128)(2,1)S(1)}, bf16[128,1024]{1,0:T(8,128)(2,1)S(1)}, u32[]{:S(2)}, u32[]{:S(2)}) collective-permute-start(bf16[128,1024]{1,0:T(8,128)(2,1)S(1)} %get-tuple-element.565), channel_id=1, source_target_pairs={{0,8},{8,16},{16,24},{1,9},{9,17},{17,25},{2,10},{10,18},{18,26},{... | collective-permute-start | bytes 786440 | tf_op jit(solution)/shard_map/ppermute | solution.py:621
  192.2 21.6 %collective-permute-start.10 = (bf16[128,1024]{1,0:T(8,128)(2,1)S(1)}, bf16[128,1024]{1,0:T(8,128)(2,1)S(1)}, u32[]{:S(2)}, u32[]{:S(2)}) collective-permute-start(bf16[128,1024]{1,0:T(8,128)(2,1)S(1)} %get-tuple-element.564), channel_id=1, source_target_pairs={{0,8},{8,16},{16,24},{1,9},{9,17},{17,25},{2,10},{10,18},{18,26},{... | collective-permute-start | bytes 786440 | tf_op jit(solution)/shard_map/ppermute | solution.py:621
  212.5 22.1 %collective-permute-start.13 = (bf16[128,1024]{1,0:T(8,128)(2,1)S(1)}, bf16[128,1024]{1,0:T(8,128)(2,1)S(1)}, u32[]{:S(2)}, u32[]{:S(2)}) collective-permute-start(bf16[128,1024]{1,0:T(8,128)(2,1)S(1)} %get-tuple-element.599), channel_id=1, source_target_pairs={{0,8},{8,16},{16,24},{1,9},{9,17},{17,25},{2,10},{10,18},{18,26},{... | collective-permute-start | bytes 786440 | tf_op jit(solution)/shard_map/ppermute | solution.py:621
  233.3 12.1 %collective-permute-start.12 = (bf16[128,1024]{1,0:T(8,128)(2,1)S(1)}, bf16[128,1024]{1,0:T(8,128)(2,1)S(1)}, u32[]{:S(2)}, u32[]{:S(2)}) collective-permute-start(bf16[128,1024]{1,0:T(8,128)(2,1)S(1)} %get-tuple-element.598), channel_id=1, source_target_pairs={{0,8},{8,16},{16,24},{1,9},{9,17},{17,25},{2,10},{10,18},{18,26},{... | collective-permute-start | bytes 786440 | tf_op jit(solution)/shard_map/ppermute | solution.py:621
  240.1 26.8 %collective-permute-start.15 = (bf16[128,1024]{1,0:T(8,128)(2,1)S(1)}, bf16[128,1024]{1,0:T(8,128)(2,1)S(1)}, u32[]{:S(2)}, u32[]{:S(2)}) collective-permute-start(bf16[128,1024]{1,0:T(8,128)(2,1)S(1)} %get-tuple-element.633), channel_id=1, source_target_pairs={{0,8},{8,16},{16,24},{1,9},{9,17},{17,25},{2,10},{10,18},{18,26},{... | collective-permute-start | bytes 786440 | tf_op jit(solution)/shard_map/ppermute | solution.py:621
  259.5 15.0 %collective-permute-start.14 = (bf16[128,1024]{1,0:T(8,128)(2,1)S(1)}, bf16[128,1024]{1,0:T(8,128)(2,1)S(1)}, u32[]{:S(2)}, u32[]{:S(2)}) collective-permute-start(bf16[128,1024]{1,0:T(8,128)(2,1)S(1)} %get-tuple-element.632), channel_id=1, source_target_pairs={{0,8},{8,16},{16,24},{1,9},{9,17},{17,25},{2,10},{10,18},{18,26},{... | collective-permute-start | bytes 786440 | tf_op jit(solution)/shard_map/ppermute | solution.py:621
  272.5 18.0 %collective-permute-start.17 = (bf16[128,1024]{1,0:T(8,128)(2,1)S(1)}, bf16[128,1024]{1,0:T(8,128)(2,1)S(1)}, u32[]{:S(2)}, u32[]{:S(2)}) collective-permute-start(bf16[128,1024]{1,0:T(8,128)(2,1)S(1)} %get-tuple-element.667), channel_id=1, source_target_pairs={{0,8},{8,16},{16,24},{1,9},{9,17},{17,25},{2,10},{10,18},{18,26},{... | collective-permute-start | bytes 786440 | tf_op jit(solution)/shard_map/ppermute | solution.py:621
  343.6 27.2 %collective-permute-start.21 = (bf16[128,1024]{1,0:T(8,128)(2,1)}, bf16[128,1024]{1,0:T(8,128)(2,1)}, u32[]{:S(2)}, u32[]{:S(2)}) collective-permute-start(bf16[128,1024]{1,0:T(8,128)(2,1)} %get-tuple-element.735), channel_id=1, source_target_pairs={{8,0},{16,8},{24,16},{9,1},{17,9},{25,17},{10,2},{18,10},{26,18},{... | collective-permute-start | bytes 786440 | tf_op jit(solution)/shard_map/ppermute | solution.py:621
  369.4 36.2 %collective-permute-start.20 = (bf16[128,1024]{1,0:T(8,128)(2,1)}, bf16[128,1024]{1,0:T(8,128)(2,1)}, u32[]{:S(2)}, u32[]{:S(2)}) collective-permute-start(bf16[128,1024]{1,0:T(8,128)(2,1)} %get-tuple-element.734), channel_id=1, source_target_pairs={{8,0},{16,8},{24,16},{9,1},{17,9},{25,17},{10,2},{18,10},{26,18},{... | collective-permute-start | bytes 786440 | tf_op jit(solution)/shard_map/ppermute | solution.py:621
  404.3 34.7 %collective-permute-start.23 = (bf16[128,1024]{1,0:T(8,128)(2,1)}, bf16[128,1024]{1,0:T(8,128)(2,1)}, u32[]{:S(2)}, u32[]{:S(2)}) collective-permute-start(bf16[128,1024]{1,0:T(8,128)(2,1)} %get-tuple-element.763), channel_id=1, source_target_pairs={{8,0},{16,8},{24,16},{9,1},{17,9},{25,17},{10,2},{18,10},{26,18},{... | collective-permute-start | bytes 786440 | tf_op jit(solution)/shard_map/ppermute | solution.py:621
  437.8 27.6 %collective-permute-start.22 = (bf16[128,1024]{1,0:T(8,128)(2,1)}, bf16[128,1024]{1,0:T(8,128)(2,1)}, u32[]{:S(2)}, u32[]{:S(2)}) collective-permute-start(bf16[128,1024]{1,0:T(8,128)(2,1)} %get-tuple-element.762), channel_id=1, source_target_pairs={{8,0},{16,8},{24,16},{9,1},{17,9},{25,17},{10,2},{18,10},{26,18},{... | collective-permute-start | bytes 786440 | tf_op jit(solution)/shard_map/ppermute | solution.py:621
  464.0 36.3 %collective-permute-start.25 = (bf16[128,1024]{1,0:T(8,128)(2,1)}, bf16[128,1024]{1,0:T(8,128)(2,1)}, u32[]{:S(2)}, u32[]{:S(2)}) collective-permute-start(bf16[128,1024]{1,0:T(8,128)(2,1)} %get-tuple-element.791), channel_id=1, source_target_pairs={{8,0},{16,8},{24,16},{9,1},{17,9},{25,17},{10,2},{18,10},{26,18},{... | collective-permute-start | bytes 786440 | tf_op jit(solution)/shard_map/ppermute | solution.py:621
  499.0 44.8 %collective-permute-start.24 = (bf16[128,1024]{1,0:T(8,128)(2,1)}, bf16[128,1024]{1,0:T(8,128)(2,1)}, u32[]{:S(2)}, u32[]{:S(2)}) collective-permute-start(bf16[128,1024]{1,0:T(8,128)(2,1)} %get-tuple-element.790), channel_id=1, source_target_pairs={{8,0},{16,8},{24,16},{9,1},{17,9},{25,17},{10,2},{18,10},{26,18},{... | collective-permute-start | bytes 786440 | tf_op jit(solution)/shard_map/ppermute | solution.py:621
  542.5 43.9 %collective-permute-start.27 = (bf16[128,1024]{1,0:T(8,128)(2,1)}, bf16[128,1024]{1,0:T(8,128)(2,1)}, u32[]{:S(2)}, u32[]{:S(2)}) collective-permute-start(bf16[128,1024]{1,0:T(8,128)(2,1)} %get-tuple-element.819), channel_id=1, source_target_pairs={{8,0},{16,8},{24,16},{9,1},{17,9},{25,17},{10,2},{18,10},{26,18},{... | collective-permute-start | bytes 786440 | tf_op jit(solution)/shard_map/ppermute | solution.py:621
  585.1 45.4 %collective-permute-start.26 = (bf16[128,1024]{1,0:T(8,128)(2,1)}, bf16[128,1024]{1,0:T(8,128)(2,1)}, u32[]{:S(2)}, u32[]{:S(2)}) collective-permute-start(bf16[128,1024]{1,0:T(8,128)(2,1)} %get-tuple-element.818), channel_id=1, source_target_pairs={{8,0},{16,8},{24,16},{9,1},{17,9},{25,17},{10,2},{18,10},{26,18},{... | collective-permute-start | bytes 786440 | tf_op jit(solution)/shard_map/ppermute | solution.py:621
  629.2 42.9 %collective-permute-start.29 = (bf16[128,1024]{1,0:T(8,128)(2,1)}, bf16[128,1024]{1,0:T(8,128)(2,1)}, u32[]{:S(2)}, u32[]{:S(2)}) collective-permute-start(bf16[128,1024]{1,0:T(8,128)(2,1)} %get-tuple-element.847), channel_id=1, source_target_pairs={{8,0},{16,8},{24,16},{9,1},{17,9},{25,17},{10,2},{18,10},{26,18},{... | collective-permute-start | bytes 786440 | tf_op jit(solution)/shard_map/ppermute | solution.py:621
  670.8 45.5 %collective-permute-start.28 = (bf16[128,1024]{1,0:T(8,128)(2,1)}, bf16[128,1024]{1,0:T(8,128)(2,1)}, u32[]{:S(2)}, u32[]{:S(2)}) collective-permute-start(bf16[128,1024]{1,0:T(8,128)(2,1)} %get-tuple-element.846), channel_id=1, source_target_pairs={{8,0},{16,8},{24,16},{9,1},{17,9},{25,17},{10,2},{18,10},{26,18},{... | collective-permute-start | bytes 786440 | tf_op jit(solution)/shard_map/ppermute | solution.py:621
  710.8 45.9 %collective-permute-start.31 = (bf16[128,1024]{1,0:T(8,128)(2,1)}, bf16[128,1024]{1,0:T(8,128)(2,1)}, u32[]{:S(2)}, u32[]{:S(2)}) collective-permute-start(bf16[128,1024]{1,0:T(8,128)(2,1)} %get-tuple-element.875), channel_id=1, source_target_pairs={{8,0},{16,8},{24,16},{9,1},{17,9},{25,17},{10,2},{18,10},{26,18},{... | collective-permute-start | bytes 786440 | tf_op jit(solution)/shard_map/ppermute | solution.py:621
  753.9 41.6 %collective-permute-start.30 = (bf16[128,1024]{1,0:T(8,128)(2,1)S(1)}, bf16[128,1024]{1,0:T(8,128)(2,1)S(1)}, u32[]{:S(2)}, u32[]{:S(2)}) collective-permute-start(bf16[128,1024]{1,0:T(8,128)(2,1)S(1)} %get-tuple-element.874), channel_id=1, source_target_pairs={{8,0},{16,8},{24,16},{9,1},{17,9},{25,17},{10,2},{18,10},{26,18},{... | collective-permute-start | bytes 786440 | tf_op jit(solution)/shard_map/ppermute | solution.py:621
  814.3 48.9 %collective-permute-start.39 = (bf16[2048,1024]{1,0:T(8,128)(2,1)}, bf16[2048,1024]{1,0:T(8,128)(2,1)}, u32[]{:S(2)}, u32[]{:S(2)}) collective-permute-start(bf16[2048,1024]{1,0:T(8,128)(2,1)} %fusion.13), channel_id=1, source_target_pairs={{0,1},{1,0},{2,3},{3,2},{4,5},{5,4},{6,7},{7,6},{8,9},{9,8},{10,11... | collective-permute-start | bytes 12582920 | tf_op jit(solution)/shard_map/ppermute | solution.py:510
  824.2 47.4 %collective-permute-start.38 = (bf16[1024,2048]{1,0:T(8,128)(2,1)}, bf16[1024,2048]{1,0:T(8,128)(2,1)}, u32[]{:S(2)}, u32[]{:S(2)}) collective-permute-start(bf16[1024,2048]{1,0:T(8,128)(2,1)} %fusion.10), channel_id=1, source_target_pairs={{0,1},{1,0},{2,3},{3,2},{4,5},{5,4},{6,7},{7,6},{8,9},{9,8},{10,11... | collective-permute-start | bytes 12582920 | tf_op jit(solution)/shard_map/ppermute | solution.py:510
  884.6 29.2 %collective-permute-start.32 = (bf16[512,1024]{1,0:T(8,128)(2,1)}, bf16[512,1024]{1,0:T(8,128)(2,1)S(1)}, u32[]{:S(2)}, u32[]{:S(2)}) collective-permute-start(bf16[512,1024]{1,0:T(8,128)(2,1)} %get-tuple-element.927), channel_id=1, source_target_pairs={{0,1},{1,0},{2,3},{3,2},{4,5},{5,4},{6,7},{7,6},{8,9},{9,8},{10,11... | collective-permute-start | bytes 3145736 | tf_op jit(solution)/shard_map/ppermute | solution.py:510
  (244 other events, 2305.3 us)
Sparse Core Ops, SparseCore 0:
  879.5 244.6 all-reduce.2
where the time goes:
time: 1160 us; the launch traced here: 1150 us
  Pallas kernels  415 us (36%)
  local copies, waits for them, and re-layouts  324 us (28%)
  waiting for transfers between devices  239 us (21%)
  matrix products  48.2 us (4%)
  starting transfers between devices  47.6 us (4%)
  other arithmetic  36.2 us (3%)
  blocking collectives  20.3 us (2%)
  between operations  16.7 us (1%)
    pallas_call x56, Pallas kernels, call(): pl.pallas_call(kernel, in_specs=specs + carried_specs, out_specs=carried_...  390 us
    unnamed x473, local copies, waits for them, and re-layouts  303 us
    psum x1, waiting for transfers between devices, local(): output_grad, project_grad = lax.psum((output_grad, project_grad), 'batch')  209 us
    dot_general x12, matrix products, dot_tn(): lax.dot_general(left, right, (((0,), (0,)), ((), ())), preferred_element_...  48.2 us
    ppermute x24, starting transfers between devices, shifted(): return lax.ppermute(value, 'section', route)  42.7 us
    ppermute x24, waiting for transfers between devices, shifted(): return lax.ppermute(value, 'section', route)  29.1 us
    pallas_call x12, Pallas kernels, flipped(): pl.pallas_call(flip_kernel, grid=(rows // size,), in_specs=[pl.BlockSpec(...  24.6 us
  transfers between devices with their start and end apart: 41, of which 6 were waited for; matrix products, arithmetic and copies ran while one was open for 6% of the time, Pallas kernels for 33%

commit v1 on v0

v1 whole, which is shorter than its diff:
```python
from functools import partial

import jax
import jax.numpy as jnp
from jax import lax
from jax.experimental import pallas as pl
from jax.experimental.pallas import tpu as pltpu
from jax.sharding import PartitionSpec as P

EPSILON = 1e-05
CHUNK = 128
KEYS = 256
TILE = 512
HIDE = -1e30
COSTS = (100, 15, 10, 5, 5)
LIMITS = tuple(size * 2**20 for size in (6, 8, 12, 10))
F32 = jnp.float32
BF16 = jnp.bfloat16
VMEM = pl.BlockSpec(memory_space=pltpu.VMEM)
SMEM = pl.BlockSpec(memory_space=pltpu.SMEM)
HBM = pl.BlockSpec(memory_space=pltpu.HBM)
ANY = pl.BlockSpec(memory_space=pl.ANY)


def lasts(microseconds):
    flops = int(microseconds * 1.1e9)
    return pl.CostEstimate(flops=flops, bytes_accessed=1024, transcendentals=0)


def dot_nn(left, right):
    return jnp.dot(left, right, preferred_element_type=F32)


def dot_nt(left, right):
    return lax.dot_general(left, right, (((1,), (1,)), ((), ())), preferred_element_type=F32)


def dot_tn(left, right):
    return lax.dot_general(left, right, (((0,), (0,)), ((), ())), preferred_element_type=F32)


def norm_parts(values):
    centre = values - jnp.mean(values, axis=-1, keepdims=True)
    inv_std = lax.rsqrt(jnp.mean(centre * centre, axis=-1, keepdims=True) + EPSILON)
    return centre * inv_std, inv_std


def norm_back(scaled, normed, inv_std):
    mean_one = jnp.mean(scaled, axis=-1, keepdims=True)
    mean_two = jnp.mean(scaled * normed, axis=-1, keepdims=True)
    return inv_std * (scaled - mean_one - normed * mean_two)


def column_sum(values):
    return jnp.sum(values, axis=0, keepdims=True)


def document_start(starts_ref, place):
    first = jnp.zeros_like(place)
    for k in range(starts_ref.shape[0]):
        start = starts_ref[k]
        first = jnp.maximum(first, jnp.where(place >= start, start, 0))
    return first


def half_masks():
    lane = lax.broadcasted_iota(jnp.int32, (1, 128), 1)
    return (lane < 64).astype(BF16), (lane >= 64).astype(BF16)


def stack_heads(pair):
    even, odd = half_masks()
    return jnp.concatenate([pair * even, pair * odd], axis=0)


def pick_heads(stacked):
    rows = stacked.shape[0] // 2
    lane = lax.broadcasted_iota(jnp.int32, (1, 128), 1)
    return jnp.where(lane < 64, stacked[:rows], stacked[rows:])


def copies_of(pairs, sems):
    return [pltpu.make_async_copy(a, b, sems.at[i]) for i, (a, b) in enumerate(pairs)]


def chunk_rows(place_ref, near_ref, far_ref, first, rows, into, sem):
    half = far_ref.shape[0]
    side = first // half
    inner = first - side * half

    @pl.when(side == place_ref[2])
    def _():
        at = pl.ds(pl.multiple_of(place_ref[3] + inner, rows), rows)
        copy = pltpu.make_async_copy(near_ref.at[at], into, sem)
        copy.start()
        copy.wait()

    @pl.when(side != place_ref[2])
    def _():
        at = pl.ds(pl.multiple_of(inner, rows), rows)
        copy = pltpu.make_async_copy(far_ref.at[at], into, sem)
        copy.start()
        copy.wait()


def row_of(pair, first, size):
    return jnp.concatenate(
        [pair[0][:, first:first + size], pair[1][:, first:first + size]], axis=1
    ).astype(F32)


def attend_kernel(
    tick_ref, section_ref, starts_ref, near_ref, far_ref, inc_ref, wp_a, wp_b, wo_a, wo_b,
    own_ref, other_ref, gain_ref, bias_ref, branch_ref,
    k_in, v_in, x_in, h1_in, q_in, o_in, lse_in, post_in, mid_in,
    k_ref, v_ref, x_buf, h1_buf, q_buf, o_buf, lse_buf, post_buf, mid_buf, mid_ref,
    x_s, h1_s, q_s, o_s, lse_s, post_s, hide_s, sems,
):
    del k_in, v_in, x_in, h1_in, q_in, o_in, lse_in, post_in, mid_in
    rows = mid_ref.shape[0]
    length, width = k_ref.shape
    half = width // 2
    section = section_ref[0]
    chunk = tick_ref[0] - 2 * section
    live = (chunk >= 0) & (chunk < length // rows)

    @pl.when(live)
    def _():
        first = pl.multiple_of(chunk * rows, rows)
        here = pl.ds(first, rows)

        @pl.when(section == 0)
        def _():
            chunk_rows(section_ref, near_ref, far_ref, first, rows, x_s, sems.at[0])

        @pl.when(section != 0)
        def _():
            x_s[...] = inc_ref[...]

        sent = []

        def send(source, target):
            copy = pltpu.make_async_copy(source, target, sems.at[len(sent)])
            copy.start()
            sent.append(copy)

        pair = (own_ref, other_ref)
        layer_in = x_s[...].astype(F32)
        send(x_s, x_buf.at[here])
        normed, _ = norm_parts(layer_in)
        h1 = (normed * gain_ref[0:1].astype(F32) + bias_ref[0:1].astype(F32)).astype(BF16)
        h1_s[...] = h1
        send(h1_s, h1_buf.at[here])
        for side, weight in ((0, wp_a), (1, wp_b)):
            at = slice(side * half, (side + 1) * half)
            q = (dot_nn(h1, weight[0]) + pair[side][:, :half].astype(F32)).astype(BF16)
            q_s[:, at] = q * jnp.asarray(0.125, BF16)
            k_ref[here, at] = dot_nn(h1, weight[1]).astype(BF16)
            value = dot_nn(h1, weight[2]) + pair[side][:, half:width].astype(F32)
            v_ref[here, at] = value.astype(BF16)
        send(q_s, q_buf.at[here])

        def attend(keys):
            place = first + lax.broadcasted_iota(jnp.int32, (rows, 1), 0)
            start = document_start(starts_ref, place)
            key_at = lax.broadcasted_iota(jnp.int32, (rows, keys), 1)
            hide_s[:, :keys] = jnp.where((key_at <= place) & (key_at >= start), 0.0, HIDE)
            lane = lax.broadcasted_iota(jnp.int32, (rows, 128), 1)

            def one_pair(pair, lse):
                at = pl.ds(pl.multiple_of(pair * 128, 128), 128)
                queries = stack_heads(q_s[:, at])
                hide = hide_s[:, :keys]
                scores = dot_nt(queries, k_ref[0:keys, at]) + jnp.concatenate([hide, hide], axis=0)
                top = jnp.max(scores, axis=-1, keepdims=True)
                raised = jnp.exp(scores - top)
                total = jnp.sum(raised, axis=-1, keepdims=True)
                out = dot_nn(raised.astype(BF16), v_ref[0:keys, at]) / total
                o_s[:, at] = pick_heads(out)
                now = top + jnp.log(total)
                lse = jnp.where(lane == 2 * pair, now[:rows], lse)
                return jnp.where(lane == 2 * pair + 1, now[rows:], lse)

            lse = lax.fori_loop(0, width // 128, one_pair, jnp.zeros((rows, 128), F32))
            lse_s[...] = lse.T

        for count in range(length // KEYS):

            @pl.when(first // KEYS == count)
            def _():
                attend((count + 1) * KEYS)

        send(o_s, o_buf.at[here])
        send(lse_s, lse_buf.at[chunk])
        post_normed, _ = norm_parts(o_s[...] * row_of(pair, 2 * half, half))
        post = post_normed * row_of(pair, 3 * half, half) + row_of(pair, 4 * half, half)
        post = post.astype(BF16)
        post_s[...] = post
        send(post_s, post_buf.at[here])
        mid_ref[...] = (
            x_s[...].astype(F32) + dot_nn(post[:, :half], wo_a[...])
            + dot_nn(post[:, half:], wo_b[...]) + branch_ref[0:1].astype(F32)
        )
        send(mid_ref, mid_buf.at[here])
        for copy in sent:
            copy.wait()


def gelu_parts(pre):
    phi = 0.5 + 0.5 * lax.erf(pre * 0.7071067811865476)
    density = jnp.exp(pre * pre * -0.5) * 0.3989422804014327
    return pre * phi, phi + pre * density


def expand_kernel(
    tick_ref, section_ref, mid_ref, we_a, we_b, wr_a, wr_b,
    own_ref, other_ref, gain_ref, bias_ref, branch_ref,
    h2_in, g_in, gp_in, m_in, st_in, keep_in, send_in,
    h2_buf, g_buf, gp_buf, m_buf, st_buf, keep_buf, send_buf, out_ref,
    h2_s, gf_s, g_s, gp_s, m_s, st_s, sems,
):
    del h2_in, g_in, gp_in, m_in, st_in, keep_in, send_in
    rows = mid_ref.shape[0]
    half = we_a.shape[1]
    units = 2 * half
    length = h2_buf.shape[0]
    chunk = tick_ref[0] - 2 * section_ref[0]

    @pl.when((chunk >= 0) & (chunk < length // rows))
    def _():
        here = pl.ds(pl.multiple_of(chunk * rows, rows), rows)
        sent = []

        def send(source, target):
            copy = pltpu.make_async_copy(source, target, sems.at[len(sent)])
            copy.start()
            sent.append(copy)

        def wide(tile, which):
            ref = own_ref if tile * TILE < half else other_ref
            first = 5 * mid_ref.shape[1] // 2 + which * half + tile * TILE % half
            return ref[:, first:first + TILE].astype(F32)

        normed, _ = norm_parts(mid_ref[...])
        h2 = (normed * gain_ref[1:2].astype(F32) + bias_ref[1:2].astype(F32)).astype(BF16)
        h2_s[...] = h2
        send(h2_s, h2_buf.at[here])
        total = jnp.zeros((rows, 1), F32)
        for tile in range(units // TILE):
            weight = we_a if tile * TILE < half else we_b
            inner = tile * TILE % half
            at = slice(tile * TILE, (tile + 1) * TILE)
            pre = dot_nn(h2, weight[:, inner:inner + TILE]) + wide(tile, 0)
            active, slope = gelu_parts(pre)
            gf_s[:, at] = active
            g_s[:, at] = active.astype(BF16)
            gp_s[:, at] = slope.astype(BF16)
            total += jnp.sum(active, axis=-1, keepdims=True)
        send(g_s, g_buf.at[here])
        send(gp_s, gp_buf.at[here])
        mean = total / units
        square = jnp.zeros((rows, 1), F32)
        for tile in range(units // TILE):
            centre = gf_s[:, tile * TILE:(tile + 1) * TILE] - mean
            square += jnp.sum(centre * centre, axis=-1, keepdims=True)
        inv_std = lax.rsqrt(square / units + EPSILON)
        lane = lax.broadcasted_iota(jnp.int32, (rows, 128), 1)
        st_s[...] = jnp.where(lane == 0, mean, inv_std)
        send(st_s, st_buf.at[here])
        out = mid_ref[...] + branch_ref[1:2].astype(F32)
        for tile in range(units // TILE):
            weight = wr_a if tile * TILE < half else wr_b
            inner = tile * TILE % half
            at = slice(tile * TILE, (tile + 1) * TILE)
            active = (gf_s[:, at] - mean) * inv_std * wide(tile, 1) + wide(tile, 2)
            active = active.astype(BF16)
            m_s[:, at] = active
            out += dot_nn(active, weight[inner:inner + TILE, :])
        send(m_s, m_buf.at[here])
        out_ref[...] = out.astype(BF16)
        state = (section_ref, keep_buf, send_buf, chunk * rows, out_ref, sems.at[5])
        store_rows(*state, "start")
        for copy in sent:
            copy.wait()
        store_rows(*state, "wait")


def expand_back_kernel(
    tick_ref, section_ref, near_ref, far_ref, inc_ref, wr_a, wr_b, we_a, we_b,
    own_ref, other_ref, gain_ref,
    g_buf, gp_buf, st_buf, mid_buf,
    sum_in, wsum_in, df_in, dur_in, dmr_in,
    sum_ref, wsum_ref, df_buf, dur_buf, dmr_buf, dmid_ref,
    g_s, gp_s, st_s, mid_s, df_s, z_s, dur_s, dmr_s, in_sems, out_sems,
):
    del sum_in, wsum_in, df_in, dur_in, dmr_in
    rows = dmid_ref.shape[0]
    half = wr_a.shape[1]
    units = 2 * half
    length = g_buf.shape[0]
    count = length // rows
    section = section_ref[0]
    last = section_ref[1] - 1
    chunk = count - 1 - (tick_ref[0] - 2 * (last - section))

    @pl.when((chunk >= 0) & (chunk < count))
    def _():
        here = pl.ds(pl.multiple_of(chunk * rows, rows), rows)
        loads = copies_of(
            (
                (g_buf.at[here], g_s), (gp_buf.at[here], gp_s), (st_buf.at[here], st_s),
                (mid_buf.at[here], mid_s),
            ),
            in_sems,
        )
        for copy in loads:
            copy.start()

        @pl.when(section == last)
        def _():
            chunk_rows(
                section_ref, near_ref, far_ref, chunk * rows, rows, df_s, out_sems.at[0]
            )

        @pl.when(section != last)
        def _():
            df_s[...] = inc_ref[...]

        sent = []

        def send(source, target):
            copy = pltpu.make_async_copy(source, target, out_sems.at[len(sent)])
            copy.start()
            sent.append(copy)

        def gain_of(tile):
            ref = own_ref if tile * TILE < half else other_ref
            first = 5 * dmid_ref.shape[1] // 2 + half + tile * TILE % half
            return ref[:, first:first + TILE].astype(F32)

        grad_low = df_s[...]
        send(df_s, df_buf.at[here])
        sum_ref[0:1] += column_sum(grad_low.astype(F32))
        for copy in loads:
            copy.wait()
        mean = st_s[:, 0:1]
        inv_std = st_s[:, 1:2]
        one = jnp.zeros((rows, 1), F32)
        two = jnp.zeros((rows, 1), F32)
        for tile in range(units // TILE):
            weight = wr_a if tile * TILE < half else wr_b
            inner = tile * TILE % half
            at = slice(tile * TILE, (tile + 1) * TILE)
            grad = dot_nn(grad_low, weight[:, inner:inner + TILE])
            normed = (g_s[:, at].astype(F32) - mean) * inv_std
            wsum_ref[0:1, at] += column_sum(grad * normed)
            wsum_ref[1:2, at] += column_sum(grad)
            scaled = grad * gain_of(tile)
            z_s[:, at] = scaled
            one += jnp.sum(scaled, axis=-1, keepdims=True)
            two += jnp.sum(scaled * normed, axis=-1, keepdims=True)
        one = one / units
        two = two / units
        grad_second = jnp.zeros((rows, dmid_ref.shape[1]), F32)
        for tile in range(units // TILE):
            weight = we_a if tile * TILE < half else we_b
            inner = tile * TILE % half
            at = slice(tile * TILE, (tile + 1) * TILE)
            normed = (g_s[:, at].astype(F32) - mean) * inv_std
            grad = inv_std * (z_s[:, at] - one - normed * two) * gp_s[:, at].astype(F32)
            wsum_ref[2:3, at] += column_sum(grad)
            low = grad.astype(BF16)
            dur_s[:, at] = low
            grad_second += dot_nn(low, weight[inner:inner + TILE, :])
        send(dur_s, dur_buf.at[here])
        normed, inv_std = norm_parts(mid_s[...])
        sum_ref[1:2] += column_sum(grad_second * normed)
        sum_ref[2:3] += column_sum(grad_second)
        grad_mid = grad_low.astype(F32) + norm_back(
            grad_second * gain_ref[1:2].astype(F32), normed, inv_std
        )
        sum_ref[3:4] += column_sum(grad_mid)
        dmid_ref[...] = grad_mid
        dmr_s[...] = grad_mid.astype(BF16)
        send(dmr_s, dmr_buf.at[here])
        for copy in sent:
            copy.wait()


def attend_back_kernel(
    tick_ref, section_ref, starts_ref, after, dmid_ref, wo_a, wo_b, wp_a, wp_b,
    own_ref, other_ref, gain_ref, k_ref, v_ref,
    x_buf, q_buf, o_buf, lse_buf,
    sum_in, dk_in, dv_in, dq_in, dkr_in, dvr_in, keep_in, send_in,
    sum_ref, dk_ref, dv_ref, dq_buf, dkr_buf, dvr_buf, keep_buf, send_buf, out_ref,
    x_s, q_s, o_s, lse_s, do_s, dqf_s, hide_s, dq_s, dkr_s, dvr_s, in_sems, out_sems,
):
    del after, sum_in, dk_in, dv_in, dq_in, dkr_in, dvr_in, keep_in, send_in
    rows = dmid_ref.shape[0]
    length, width = k_ref.shape
    half = width // 2
    count = length // rows
    section = section_ref[0]
    last = section_ref[1] - 1
    chunk = count - 1 - (tick_ref[0] - 2 * (last - section))

    @pl.when((chunk >= 0) & (chunk < count))
    def _():
        first = pl.multiple_of(chunk * rows, rows)
        here = pl.ds(first, rows)
        loads = copies_of(
            (
                (x_buf.at[here], x_s), (q_buf.at[here], q_s), (o_buf.at[here], o_s),
                (lse_buf.at[chunk], lse_s),
            ),
            in_sems,
        )
        for copy in loads:
            copy.start()

        @pl.when(chunk == count - 1)
        def _():
            dk_ref[...] = jnp.zeros_like(dk_ref)
            dv_ref[...] = jnp.zeros_like(dv_ref)

        low = dmid_ref[...].astype(BF16)
        grad_post = jnp.concatenate([dot_nn(low, wo_a[...]), dot_nn(low, wo_b[...])], axis=1)
        for copy in loads:
            copy.wait()
        attended = o_s[...]
        pair_refs = (own_ref, other_ref)
        scale = row_of(pair_refs, 2 * half, half)
        normed, inv_std = norm_parts(attended * scale)
        sum_ref[0:1] += column_sum(grad_post * normed)
        sum_ref[1:2] += column_sum(grad_post)
        grad_mixed = norm_back(grad_post * row_of(pair_refs, 3 * half, half), normed, inv_std)
        sum_ref[2:3] += column_sum(grad_mixed * attended)
        do_s[...] = (grad_mixed * scale).astype(BF16)

        def attend(keys):
            place = first + lax.broadcasted_iota(jnp.int32, (1, rows), 1)
            start = document_start(starts_ref, place)
            key_at = lax.broadcasted_iota(jnp.int32, (keys, rows), 0)
            hide_s[:keys, :] = jnp.where((key_at <= place) & (key_at >= start), 0.0, HIDE)

            def one_pair(pair, carry):
                at = pl.ds(pl.multiple_of(pair * 128, 128), 128)
                queries = stack_heads(q_s[:, at])
                grad_pair = do_s[:, at]
                grads = stack_heads(grad_pair)
                product = (grad_pair.astype(F32) * o_s[:, at]).T
                delta = jnp.concatenate(
                    [column_sum(product[:64]), column_sum(product[64:])], axis=1
                )
                lse = jnp.concatenate(
                    [lse_s[pl.ds(2 * pair, 1), :], lse_s[pl.ds(2 * pair + 1, 1), :]], axis=1
                )
                hide = hide_s[:keys, :]
                key_pair = k_ref[0:keys, at]
                scores = dot_nt(key_pair, queries) + jnp.concatenate([hide, hide], axis=1)
                probs = jnp.exp(scores - lse)
                grad_probs = dot_nt(v_ref[0:keys, at], grads)
                grad_scores = (probs * (grad_probs - delta)).astype(BF16)
                dk_ref[0:keys, at] += dot_nn(grad_scores, queries)
                dv_ref[0:keys, at] += dot_nn(probs.astype(BF16), grads)
                dqf_s[:, at] = pick_heads(dot_tn(grad_scores, key_pair)) * 0.125
                return carry

            lax.fori_loop(0, width // 128, one_pair, 0)

        for number in range(length // KEYS):

            @pl.when(first // KEYS == number)
            def _():
                attend((number + 1) * KEYS)

        sent = []

        def send(source, target):
            copy = pltpu.make_async_copy(source, target, out_sems.at[len(sent)])
            copy.start()
            sent.append(copy)

        grad_query = dqf_s[...]
        grad_value = dv_ref[here, :]
        sum_ref[3:4] += column_sum(grad_query)
        sum_ref[4:5] += column_sum(grad_value)
        dq_s[...] = grad_query.astype(BF16)
        dkr_s[...] = dk_ref[here, :].astype(BF16)
        dvr_s[...] = grad_value.astype(BF16)
        send(dq_s, dq_buf.at[here])
        send(dkr_s, dkr_buf.at[here])
        send(dvr_s, dvr_buf.at[here])
        grad_first = jnp.zeros((rows, width), F32)
        for number, part in enumerate((dq_s, dkr_s, dvr_s)):
            grad_first += dot_nn(part[:, :half], wp_a[number])
            grad_first += dot_nn(part[:, half:], wp_b[number])
        normed, inv_std = norm_parts(x_s[...].astype(F32))
        sum_ref[5:6] += column_sum(grad_first * normed)
        sum_ref[6:7] += column_sum(grad_first)
        out = dmid_ref[...] + norm_back(
            grad_first * gain_ref[0:1].astype(F32), normed, inv_std
        )
        out_ref[...] = out.astype(BF16)
        state = (section_ref, keep_buf, send_buf, first, out_ref, out_sems.at[3])
        store_rows(*state, "start")
        for copy in sent:
            copy.wait()
        store_rows(*state, "wait")


def flip_kernel(first, second, after, first_out, second_out):
    del after
    size = 256
    for source, target in ((first, first_out), (second, second_out)):
        numbers = range(source.shape[0]) if len(source.shape) == 3 else (None,)
        for number in numbers:
            one = source if number is None else source.at[number]
            two = target if number is None else target.at[number]

            def body(step, carry, one=one, two=two):
                at = pl.ds(pl.multiple_of(step * size, size), size)
                two[:, at] = one[at, :].T
                return carry

            lax.fori_loop(0, one.shape[0] // size, body, 0)


def flipped(first, second, after):
    shape = first.shape[:-2] + (first.shape[-1], first.shape[-2])
    return pl.pallas_call(
        flip_kernel,
        in_specs=[VMEM] * 2 + [ANY],
        out_specs=[VMEM] * 2,
        out_shape=[pltpu.VMEM(shape, BF16)] * 2,
        compiler_params=pltpu.CompilerParams(vmem_limit_bytes=2 * 2**20),
    )(first, second, after)


def load_kernel(source, after, target, sem):
    del after
    copy = pltpu.make_async_copy(source, target, sem)
    copy.start()
    copy.wait()


def loaded(value, after):
    return pl.pallas_call(
        load_kernel,
        in_specs=[HBM, ANY],
        out_specs=VMEM,
        out_shape=pltpu.VMEM(value.shape, value.dtype),
        scratch_shapes=[pltpu.SemaphoreType.DMA],
        compiler_params=pltpu.CompilerParams(vmem_limit_bytes=2**20),
    )(pltpu.with_memory_space_constraint(value, pltpu.HBM), after)


def empty_kernel(*refs):
    del refs


def empty(shapes, space, *after):
    return pl.pallas_call(
        empty_kernel,
        in_specs=[ANY] * len(after),
        out_specs=[pl.BlockSpec(memory_space=space)] * len(shapes),
        out_shape=[space(shape, dtype) for shape, dtype in shapes],
        compiler_params=pltpu.CompilerParams(vmem_limit_bytes=2**20),
    )(*after)


def call(kernel, inputs, specs, carried, carried_specs, fresh, fresh_specs, scratch, limit, flops):
    first = len(inputs)
    inputs = [
        pltpu.with_memory_space_constraint(a, pltpu.HBM) if spec is HBM else a
        for a, spec in zip(inputs, specs)
    ]
    shapes = [
        pltpu.HBM(a.shape, a.dtype) if spec is HBM else jax.ShapeDtypeStruct(a.shape, a.dtype)
        for a, spec in zip(carried, carried_specs)
    ] + fresh
    return pl.pallas_call(
        kernel,
        in_specs=specs + carried_specs,
        out_specs=carried_specs + fresh_specs,
        out_shape=shapes,
        scratch_shapes=scratch,
        input_output_aliases={first + i: i for i in range(len(carried))},
        compiler_params=pltpu.CompilerParams(vmem_limit_bytes=limit),
        cost_estimate=pl.CostEstimate(flops=flops, bytes_accessed=2**22, transcendentals=0),
    )(*inputs, *carried)


def settle_kernel(place_ref, *refs):
    pieces, (*outs, wide_s, turn_s, sems) = refs[:8], refs[8:]
    rows = pieces[0].shape[0]
    low, high = place_ref[4], place_ref[5]
    copies = []
    for number, piece in enumerate(pieces):
        half, flips = number // 4, number % 4
        first = (low, high)[half] ^ (flips // 2)
        second = (high, low)[half] ^ (flips % 2)
        slot = number % 2
        if number >= 2:
            for copy in copies[number - 2]:
                copy.wait()
        wide_s[slot] = piece[...].astype(F32)
        at = pl.ds(pl.multiple_of((half * 4 + first * 2 + second) * rows, rows), rows)
        moves = []
        if len(outs) == 1:
            moves.append((wide_s.at[slot], outs[0].at[at]))
        else:
            layers, _, columns = outs[0].shape
            for layer in range(layers):
                source = wide_s.at[slot, :, layer * columns:(layer + 1) * columns]
                moves.append((source, outs[0].at[layer, at]))
            turn_s[slot] = wide_s[slot, :, layers * columns:].T
            moves.append((turn_s.at[slot], outs[1].at[:, at]))
        started = [
            pltpu.make_async_copy(source, target, sems.at[slot, i])
            for i, (source, target) in enumerate(moves)
        ]
        for copy in started:
            copy.start()
        copies.append(started)
    for copy in copies[6] + copies[7]:
        copy.wait()


def settle(place, pieces, shapes, after, cost):
    rows, columns = pieces[0].shape
    turn = (2, shapes[1][0], rows) if len(shapes) > 1 else (2, 8, 128)

    def kernel(place_ref, *refs):
        settle_kernel(place_ref, *refs[:8], *refs[9:])

    return pl.pallas_call(
        kernel,
        grid=(1,),
        in_specs=[SMEM]
        + [pl.BlockSpec((rows, columns), lambda i: (0, 0), pipeline_mode=pl.Buffered(1))] * 8
        + [HBM],
        out_specs=[HBM] * len(shapes),
        out_shape=[pltpu.HBM(shape, F32) for shape in shapes],
        scratch_shapes=[
            pltpu.VMEM((2, rows, columns), F32), pltpu.VMEM(turn, F32),
            pltpu.SemaphoreType.DMA((2, 4)),
        ],
        compiler_params=pltpu.CompilerParams(vmem_limit_bytes=14 * 2**20),
        cost_estimate=lasts(cost),
    )(place, *pieces, *in_hbm([after]))


def crossed(value, bit):
    route = [(i, i ^ bit) for i in range(lax.axis_size("batch"))]
    return lax.ppermute(value, "batch", route)


def in_hbm(values):
    return [pltpu.with_memory_space_constraint(value, pltpu.HBM) for value in values]


def product(lefts, rights, pairs, columns, number):
    left = lefts[pairs[number]][...]
    return slice(number * columns, (number + 1) * columns), dot_tn(left, rights[number][...])


def other_part(lefts, rights, pairs, axis, after, cost=1):
    length = lefts[0].shape[0]
    rows = lefts[0].shape[1] // (2 if axis == 0 else 1)
    columns = rights[0].shape[1] // (1 if axis == 0 else 2)
    tile = rows // 4
    skip = 4 if axis == 0 else 0
    side = 0 if axis == 0 else 1

    def kernel(*refs):
        for number in range(len(rights)):
            at, value = product(
                refs[:len(lefts)], refs[len(lefts):], pairs, columns, number
            )
            refs[-1][:, at] = value.astype(BF16)

    return pl.pallas_call(
        kernel,
        grid=(rows // tile,),
        in_specs=[pl.BlockSpec((length, tile), lambda i: (0, skip + i))] * len(lefts)
        + [pl.BlockSpec((length, columns), lambda i: (0, side), pipeline_mode=pl.Buffered(1))]
        * len(rights)
        + [HBM],
        out_specs=pl.BlockSpec((tile, columns * len(rights)), lambda i: (i, 0)),
        out_shape=pltpu.HBM((rows, columns * len(rights)), BF16),
        compiler_params=pltpu.CompilerParams(vmem_limit_bytes=14 * 2**20),
        cost_estimate=lasts(cost),
    )(*in_hbm(lefts), *in_hbm(rights), *in_hbm([after]))


def own_part(lefts, rights, pairs, come, place, after, cost=1):
    length = lefts[0].shape[0]
    rows, whole = come.shape
    columns = whole // len(rights)
    tile = rows // 4

    def at(i, place):
        low, high = place[4], place[5]
        first = jnp.where(i == 0, 1 - low, 3 - high)
        return jnp.where(i < 2, first, jnp.where(i == 2, low, 2 + high))

    def kernel(place_ref, *refs):
        del place_ref
        come_ref, outs = refs[len(lefts) + len(rights)], refs[-4:]
        for number in range(len(rights)):
            where, value = product(
                refs[:len(lefts)], refs[len(lefts):], pairs, columns, number
            )
            low = (value + come_ref[:, where].astype(F32)).astype(BF16)
            for step, out in enumerate(outs):

                @pl.when(pl.program_id(0) == step)
                def _():
                    out[:, where] = low

    return pl.pallas_call(
        kernel,
        grid_spec=pltpu.PrefetchScalarGridSpec(
            num_scalar_prefetch=1,
            grid=(4,),
            in_specs=[pl.BlockSpec((length, tile), lambda i, place: (0, at(i, place)))]
            * len(lefts)
            + [
                pl.BlockSpec(
                    (length, columns), lambda i, place: (0, 0), pipeline_mode=pl.Buffered(1)
                )
            ]
            * len(rights)
            + [pl.BlockSpec((tile, whole), lambda i, place: (at(i, place), 0)), HBM],
            out_specs=[pl.BlockSpec((tile, whole), lambda i, place: (0, 0))] * 4,
        ),
        out_shape=[pltpu.HBM((tile, whole), BF16)] * 4,
        compiler_params=pltpu.CompilerParams(vmem_limit_bytes=20 * 2**20),
        cost_estimate=lasts(cost),
    )(place, *in_hbm(lefts), *in_hbm(rights), come, *in_hbm([after]))


def add_kernel(split, place_ref, *refs):
    keeps, comes = (refs[0], refs[2]), (refs[1], refs[3])
    outs = refs[5:]
    for half, bit in ((0, 5), (1, 4)):
        keep, come = keeps[half], comes[half]
        if split:
            rows = keep.shape[0] // 2
            side = place_ref[bit]
            for number, where in ((0, 1 - side), (1, side)):
                at = pl.ds(pl.multiple_of(where * rows, rows), rows)
                outs[2 * half + number][...] = (
                    keep[at, :].astype(F32) + come[at, :].astype(F32)
                ).astype(BF16)
        else:
            outs[half][...] = (keep[...].astype(F32) + come[...].astype(F32)).astype(BF16)


def added(keeps, comes, place, split, after, cost):
    rows, columns = keeps[0].shape
    kept = rows // 2 if split else rows
    count = 4 if split else 2
    return pl.pallas_call(
        partial(add_kernel, split),
        grid=(1,),
        in_specs=[SMEM]
        + [pl.BlockSpec((rows, columns), lambda i: (0, 0), pipeline_mode=pl.Buffered(1))] * 4
        + [HBM],
        out_specs=[
            pl.BlockSpec((kept, columns), lambda i: (0, 0), pipeline_mode=pl.Buffered(1))
        ]
        * count,
        out_shape=[pltpu.HBM((kept, columns), BF16)] * count,
        compiler_params=pltpu.CompilerParams(vmem_limit_bytes=12 * 2**20),
        cost_estimate=lasts(cost),
    )(place, keeps[0], comes[0], keeps[1], comes[1], *in_hbm([after]))


class BatchSum:
    def __init__(self, pieces, place):
        send_a, send_b, keep_a, keep_b = pieces
        self.place = place
        self.keeps = keep_a, keep_b
        self.comes = crossed(send_a, 1), crossed(send_b, 2)

    def second(self, after, cost):
        send_a, keep_a, send_b, keep_b = added(self.keeps, self.comes, self.place, True, after, cost)
        self.keeps = keep_a, keep_b
        self.comes = crossed(send_a, 2), crossed(send_b, 1)
        return keep_a

    def third(self, after, cost):
        a, b = added(self.keeps, self.comes, self.place, False, after, cost)
        across_a, across_b = crossed(a, 2), crossed(b, 1)
        self.pieces = [
            a, across_a, crossed(a, 1), crossed(across_a, 1),
            b, across_b, crossed(b, 2), crossed(across_b, 2),
        ]
        return a

    def result(self, shapes, after, cost=1):
        return settle(self.place, self.pieces, shapes, after, cost)


def keep_kernel(place_ref, come_ref, in_ref, out_ref, sem):
    del in_ref
    copy = pltpu.make_async_copy(come_ref, out_ref.at[1 - place_ref[2]], sem)
    copy.start()
    copy.wait()


def with_other_half(kept, come, place, after):
    def kernel(place_ref, come_ref, after_ref, *refs):
        keep_kernel(place_ref, come_ref, *refs)

    return pl.pallas_call(
        kernel,
        in_specs=[SMEM, VMEM, HBM, HBM],
        out_specs=HBM,
        out_shape=pltpu.HBM(kept.shape, kept.dtype),
        scratch_shapes=[pltpu.SemaphoreType.DMA],
        compiler_params=pltpu.CompilerParams(vmem_limit_bytes=4 * 2**20),
        input_output_aliases={3: 0},
        cost_estimate=lasts(3),
    )(place, come, *in_hbm([after]), kept)


def plus_kernel(one, two, after, out):
    del after
    out[...] = one[...] + two[...]


def plus(one, two, after):
    return pl.pallas_call(
        plus_kernel,
        in_specs=[VMEM, VMEM, HBM],
        out_specs=VMEM,
        out_shape=jax.ShapeDtypeStruct(one.shape, one.dtype),
        compiler_params=pltpu.CompilerParams(vmem_limit_bytes=2**20),
        cost_estimate=lasts(1),
    )(one, two, *in_hbm([after]))


def store_rows(place_ref, keep_buf, send_buf, first, source, sem, back):
    rows = source.shape[0]
    half = send_buf.shape[0]
    side = first // half
    at = pl.ds(pl.multiple_of(first - side * half, rows), rows)

    @pl.when(side == place_ref[2])
    def _():
        copy = pltpu.make_async_copy(source, keep_buf.at[side, at], sem)
        getattr(copy, back)()

    @pl.when(side != place_ref[2])
    def _():
        copy = pltpu.make_async_copy(source, send_buf.at[at], sem)
        getattr(copy, back)()


def local(
    tokens, cotangent, document_starts, pre_gain, pre_bias, project_weight, project_bias,
    head_scale, post_gain, post_bias, output_weight, expand_weight, expand_bias, middle_gain,
    middle_bias, reduce_weight, branch_bias,
):
    sections = lax.axis_size("section")
    section = lax.axis_index("section")
    parts = lax.axis_size("mp")
    part = lax.axis_index("mp")
    shard = lax.axis_index("batch")
    micro, rows_here, width = tokens.shape[1:]
    length = rows_here * parts
    chunk = CHUNK
    count = length // chunk
    head = width // (head_scale.shape[1] * parts)
    units = expand_bias.shape[1] * parts
    paired = parts == 2 and micro == 2
    by_links = paired and lax.axis_size("batch") == 4
    block = part * micro // parts
    copies = micro / parts

    def swapped(value):
        return lax.ppermute(value, "mp", [(0, 1), (1, 0)])

    def both(value, axis):
        if paired:
            return value, swapped(value)
        whole = lax.all_gather(value, "mp", axis=axis, tiled=True)
        return tuple(jnp.split(whole, 2, axis=axis))

    def row_source(value):
        if paired:
            theirs = lax.dynamic_index_in_dim(value, 1 - part, 0, keepdims=False)
            return value.reshape(micro * rows_here, width), swapped(theirs)
        whole = lax.all_gather(value, "mp", axis=1, tiled=True)
        whole = lax.dynamic_index_in_dim(whole, block, 0, keepdims=False)
        return whole[:length // 2], whole[length // 2:]

    def spread_rows(kept, sent, after):
        if paired:
            return with_other_half(kept, swapped(sent), place, after)
        whole = lax.all_gather(jnp.concatenate([kept[0], sent]), "mp", axis=0)[:: parts // micro]
        return lax.dynamic_slice_in_dim(whole, part * rows_here, rows_here, 1)

    near_tokens, far_tokens = row_source(tokens[0])
    place = jnp.stack(
        [
            section, jnp.int32(sections), part if paired else jnp.int32(0),
            part * rows_here if paired else jnp.int32(0), shard % 2, shard // 2,
        ]
    ).astype(jnp.int32)
    starts = lax.dynamic_index_in_dim(document_starts[0], block, 0, keepdims=False)[0]
    fields = (
        project_bias[0, 0], project_bias[0, 1], jnp.repeat(head_scale[0], head), post_gain[0],
        post_bias[0], expand_bias[0], middle_gain[0], middle_bias[0],
    )
    if paired:
        own = jnp.concatenate(fields)[None]
        other = swapped(own)
    else:
        sides = [both(field, 0) for field in fields]
        own = jnp.concatenate([a for a, _ in sides])[None]
        other = jnp.concatenate([b for _, b in sides])[None]
    gains, biases, branches = pre_gain[0], pre_bias[0], branch_bias[0]
    wp_a, wp_b = both(project_weight[0], 2)
    wo_a, wo_b = both(output_weight[0], 0)
    we_a, we_b = both(expand_weight[0], 1)
    wr_a, wr_b = both(reduce_weight[0], 0)
    wp_a = loaded(wp_a, place)
    wo_a = loaded(wo_a, wp_a)
    we_a = loaded(we_a, wo_a)
    wr_a = loaded(wr_a, we_a)
    wp_b = loaded(wp_b, wr_a)
    wo_b = loaded(wo_b, wp_b)
    we_b = loaded(we_b, wo_b)
    wr_b = loaded(wr_b, we_b)
    near_cotangent, far_cotangent = row_source(cotangent[0])

    def sized(columns, dtype):
        return ((length, columns), dtype)

    halves = (((2, length // 2, width), BF16), ((length // 2, width), BF16))

    (
        x_buf, h1_buf, q_buf, o_buf, lse_buf, post_buf, mid_buf,
        h2_buf, g_buf, gp_buf, m_buf, st_buf, hid_keep, hid_send,
        df_buf, dur_buf, dmr_buf, dq_buf, dkr_buf, dvr_buf, ig_keep, ig_send,
    ) = empty(
        [
            sized(width, BF16), sized(width, BF16), sized(width, BF16), sized(width, F32),
            ((count, 128, chunk), F32), sized(width, BF16), sized(width, F32),
            sized(width, BF16), sized(units, BF16), sized(units, BF16), sized(units, BF16),
            sized(128, F32), *halves,
            sized(width, BF16), sized(units, BF16), sized(width, BF16), sized(width, BF16),
            sized(width, BF16), sized(width, BF16), *halves,
        ],
        pltpu.HBM,
    )
    k_all = jnp.zeros((length, width), BF16)
    v_all = jnp.zeros((length, width), BF16)
    dma = pltpu.SemaphoreType.DMA
    dense = 2 * chunk * width

    def shifted(value, distance):
        route = [(i, i + distance) for i in range(sections) if 0 <= i + distance < sections]
        return lax.ppermute(value, "section", route)

    ticks = count + 2 * (sections - 1)
    blank = jnp.zeros((chunk, width), BF16)
    incoming = blank
    sent = None
    for tick in range(ticks):
        now = jnp.full((1,), tick, jnp.int32)
        arriving = shifted(sent, 1) if sent is not None and tick + 1 < ticks else blank
        (
            k_all, v_all, x_buf, h1_buf, q_buf, o_buf, lse_buf, post_buf, mid_buf, middle,
        ) = call(
            attend_kernel,
            (
                now, place, starts, near_tokens, far_tokens, incoming, wp_a, wp_b, wo_a, wo_b,
                own, other, gains, biases, branches,
            ),
            [SMEM, SMEM, SMEM, HBM, HBM] + [VMEM] * 10,
            (k_all, v_all, x_buf, h1_buf, q_buf, o_buf, lse_buf, post_buf, mid_buf),
            [VMEM, VMEM] + [HBM] * 7,
            [jax.ShapeDtypeStruct((chunk, width), F32)],
            [VMEM],
            [
                pltpu.VMEM((chunk, width), BF16), pltpu.VMEM((chunk, width), BF16),
                pltpu.VMEM((chunk, width), BF16), pltpu.VMEM((chunk, width), F32),
                pltpu.VMEM((128, chunk), F32), pltpu.VMEM((chunk, width), BF16),
                pltpu.VMEM((chunk, length), F32), dma((7,)),
            ],
            LIMITS[0],
            8 * dense * width,
        )
        h2_buf, g_buf, gp_buf, m_buf, st_buf, hid_keep, hid_send, sent = call(
            expand_kernel,
            (
                now, place, middle, we_a, we_b, wr_a, wr_b, own, other, gains, biases, branches,
            ),
            [SMEM, SMEM] + [VMEM] * 10,
            (h2_buf, g_buf, gp_buf, m_buf, st_buf, hid_keep, hid_send),
            [HBM] * 7,
            [jax.ShapeDtypeStruct((chunk, width), BF16)],
            [VMEM],
            [
                pltpu.VMEM((chunk, width), BF16), pltpu.VMEM((chunk, units), F32),
                pltpu.VMEM((chunk, units), BF16), pltpu.VMEM((chunk, units), BF16),
                pltpu.VMEM((chunk, units), BF16), pltpu.VMEM((chunk, 128), F32), dma((6,)),
            ],
            LIMITS[1],
            2 * dense * units,
        )
        incoming = arriving

    wrt_a, wrt_b = flipped(wr_a, wr_b, sent)
    wet_a, wet_b = flipped(we_a, we_b, wrt_a)
    wot_a, wot_b = flipped(wo_a, wo_b, wet_a)
    wpt_a, wpt_b = flipped(wp_a, wp_b, wot_a)
    dk_acc, dv_acc = empty([sized(width, F32)] * 2, pltpu.VMEM, wpt_a)
    sum_f = jnp.zeros((4, width), F32)
    sum_w = jnp.zeros((3, units), F32)
    sum_a = jnp.zeros((7, width), F32)
    incoming = blank
    sent = None

    def weight_gradient(left, right, axis):
        full = dot_tn(left, right).astype(BF16)
        total = lax.psum_scatter(full, "mp", scatter_dimension=axis, tiled=True)
        return (total.astype(F32) * copies).astype(BF16)

    def attend_back(now, after, grad_mid, carried, cost=10):
        return call(
            attend_back_kernel,
            (
                now, place, starts, after, grad_mid, wot_a, wot_b, wpt_a, wpt_b, own, other, gains,
                k_all, v_all, x_buf, q_buf, o_buf, lse_buf,
            ),
            [SMEM, SMEM, SMEM, HBM] + [VMEM] * 10 + [HBM] * 4,
            carried,
            [VMEM, VMEM, VMEM] + [HBM] * 5,
            [jax.ShapeDtypeStruct((chunk, width), BF16)],
            [VMEM],
            [
                pltpu.VMEM((chunk, width), BF16), pltpu.VMEM((chunk, width), BF16),
                pltpu.VMEM((chunk, width), F32), pltpu.VMEM((128, chunk), F32),
                pltpu.VMEM((chunk, width), BF16), pltpu.VMEM((chunk, width), F32),
                pltpu.VMEM((length, chunk), F32), pltpu.VMEM((chunk, width), BF16),
                pltpu.VMEM((chunk, width), BF16), pltpu.VMEM((chunk, width), BF16),
                dma((4,)), dma((4,)),
            ],
            LIMITS[3],
            cost * 11 * 10**8,
        )

    held = []
    carried = (sum_a, dk_acc, dv_acc, dq_buf, dkr_buf, dvr_buf, ig_keep, ig_send)
    for tick in range(ticks):
        now = jnp.full((1,), tick, jnp.int32)
        arriving = shifted(sent, -1) if sent is not None and tick + 1 < ticks else blank
        sum_f, sum_w, df_buf, dur_buf, dmr_buf, grad_mid = call(
            expand_back_kernel,
            (
                now, place, near_cotangent, far_cotangent, incoming, wrt_a, wrt_b, wet_a, wet_b,
                own, other, gains, g_buf, gp_buf, st_buf, mid_buf,
            ),
            [SMEM, SMEM, HBM, HBM] + [VMEM] * 8 + [HBM] * 4,
            (sum_f, sum_w, df_buf, dur_buf, dmr_buf),
            [VMEM, VMEM] + [HBM] * 3,
            [jax.ShapeDtypeStruct((chunk, width), F32)],
            [VMEM],
            [
                pltpu.VMEM((chunk, units), BF16), pltpu.VMEM((chunk, units), BF16),
                pltpu.VMEM((chunk, 128), F32), pltpu.VMEM((chunk, width), F32),
                pltpu.VMEM((chunk, width), BF16), pltpu.VMEM((chunk, units), F32),
                pltpu.VMEM((chunk, units), BF16), pltpu.VMEM((chunk, width), BF16),
                dma((4,)), dma((3,)),
            ],
            LIMITS[2],
            2 * dense * units,
        )
        held.append((now, grad_mid))
        if tick + 2 < ticks:
            held.clear()
            *carried, sent = attend_back(now, x_buf, grad_mid, carried)
        incoming = arriving
    def gathered(sum_a):
        shared = jnp.stack([sum_a[5], sum_f[1], sum_a[6], sum_f[2], sum_f[3], sum_f[0]])
        narrow = jnp.stack([sum_a[3], sum_a[4], sum_a[2], sum_a[0], sum_a[1]])
        broad = jnp.stack([sum_w[2], sum_w[0], sum_w[1]])
        return shared, narrow, broad

    def packed(side, sum_a):
        shared, narrow, broad = gathered(sum_a)
        cut, wide_cut = width // 2, units // 2
        return jnp.concatenate(
            [
                shared.reshape(-1),
                narrow[:, side * cut:(side + 1) * cut].reshape(-1),
                broad[:, side * wide_cut:(side + 1) * wide_cut].reshape(-1),
            ]
        )

    if by_links:
        reduce_sides = (m_buf,), (df_buf,), (0,)
        expand_sides = (h2_buf,), (dur_buf,), (0,)
        reduce_other = other_part(*reduce_sides, 0, df_buf)
        expand_other = other_part(*expand_sides, 1, reduce_other)
        pieces = own_part(*reduce_sides, swapped(reduce_other), place, expand_other)
        reduce_sum = BatchSum(pieces, place)
        pieces = own_part(*expand_sides, swapped(expand_other), place, pieces[3])
        expand_sum = BatchSum(pieces, place)
        after = pieces[3]
        for number, (now, grad_mid) in enumerate(held):
            *carried, sent = attend_back(now, after, grad_mid, carried, 1)
            after = reduce_sum.second(carried[-1], 1) if number == 0 else carried[-1]
        sum_a, _, _, dq_buf, dkr_buf, dvr_buf, ig_keep, ig_send = carried
        mixed_sides = (h1_buf, dmr_buf), (dq_buf, dkr_buf, dvr_buf, post_buf), (0, 0, 0, 1)
        mixed_other = other_part(*mixed_sides, 1, after)
        after = expand_sum.second(mixed_other, COSTS[0])
        pieces = own_part(*mixed_sides, swapped(mixed_other), place, after)
        mixed_sum = BatchSum(pieces, place)
        after = reduce_sum.third(pieces[3], COSTS[1])
        after = hidden = spread_rows(hid_keep, hid_send, after)
        small_one, small_two = (packed(side, sum_a).reshape(-1, 128) for side in (0, 1))
        small = plus(small_one, swapped(small_two), after)
        after = mixed_sum.second(after, COSTS[2])
        after = expand_sum.third(after, COSTS[3])
        after = mixed_sum.third(after, COSTS[4])
        input_gradient = spread_rows(ig_keep, ig_send, after)
        small = plus(small, crossed(small, 1), input_gradient)
        (reduce_grad,) = reduce_sum.result((reduce_weight.shape[1:],), input_gradient)
        small = plus(small, crossed(small, 2), reduce_grad)
        (expand_grad,) = expand_sum.result((expand_weight.shape[1:],), reduce_grad)
        project_grad, output_grad = mixed_sum.result(
            (project_weight.shape[1:], output_weight.shape[1:]), expand_grad
        )
        project_grad = project_grad[None]
    else:
        for now, grad_mid in held:
            *carried, sent = attend_back(now, x_buf, grad_mid, carried)
        sum_a, _, _, dq_buf, dkr_buf, dvr_buf, ig_keep, ig_send = carried
        hidden = spread_rows(hid_keep, hid_send, sent)
        input_gradient = spread_rows(ig_keep, ig_send, sent)
        reduce_grad, expand_grad, output_grad, *project_grad = (
            total.astype(F32)
            for total in lax.psum(
                (
                    weight_gradient(m_buf, df_buf, 0), weight_gradient(h2_buf, dur_buf, 1),
                    weight_gradient(post_buf, dmr_buf, 0), weight_gradient(h1_buf, dq_buf, 1),
                    weight_gradient(h1_buf, dkr_buf, 1), weight_gradient(h1_buf, dvr_buf, 1),
                ),
                "batch",
            )
        )
        project_grad = jnp.stack(project_grad)[None]

    if paired:
        if not by_links:
            small = lax.psum(packed(0, sum_a) + swapped(packed(1, sum_a)), "batch")
        small = small.reshape(-1)
        here, there = width // 2, units // 2
        shared = small[:6 * width].reshape(6, width)
        narrow = small[6 * width:6 * width + 5 * here].reshape(5, here)
        broad = small[6 * width + 5 * here:].reshape(3, there)
    else:
        shared, narrow, broad = gathered(sum_a)
        small = lax.psum(
            jnp.concatenate([shared.reshape(-1), narrow.reshape(-1), broad.reshape(-1)]),
            ("batch", "mp"),
        ) * copies
        shared = small[:6 * width].reshape(6, width)
        narrow = small[6 * width:11 * width].reshape(5, width)
        broad = small[11 * width:].reshape(3, units)
        narrow = lax.dynamic_slice_in_dim(narrow, part * (width // parts), width // parts, 1)
        broad = lax.dynamic_slice_in_dim(broad, part * (units // parts), units // parts, 1)

    return (
        hidden[None, None],
        input_gradient[None, None],
        shared[0:2][None],
        shared[2:4][None],
        project_grad,
        narrow[0:2][None],
        jnp.sum(narrow[2].reshape(-1, head), axis=1)[None],
        narrow[3][None],
        narrow[4][None],
        output_grad[None],
        expand_grad[None],
        broad[0][None],
        broad[1][None],
        broad[2][None],
        reduce_grad[None],
        shared[4:6][None],
    )


def solution(mesh):
    layered = P("section", None, None)
    split = P("section", "mp")
    rows = P("section", "mp", None)
    columns = P("section", None, "mp")
    projected = P("section", None, None, "mp")
    tokens = P("batch", None, "mp", None)
    states = P("section", "batch", None, "mp", None)
    return jax.shard_map(
        local,
        mesh=mesh,
        in_specs=(
            tokens, tokens, P("batch", None, None, None), layered, layered, projected, columns,
            split, split, split, rows, columns, split, split, split, rows, layered,
        ),
        out_specs=(
            states, states, layered, layered, projected, columns, split, split, split, rows,
            columns, split, split, split, rows, layered,
        ),
        check_vma=False,
    )
```

time: 1160 us -> 772 us (0.67)
  local copies, waits for them, and re-layouts: 324 us -> 28.6 us
  waiting for transfers between devices: 239 us -> 176 us
  Pallas kernels: 415 us -> 464 us
  matrix products: 48.2 us -> 0 us
  starting transfers between devices: 47.6 us -> 88.5 us
  other arithmetic: 36.2 us -> 0.84 us
  blocking collectives: 20.3 us -> 0 us
  between operations: 16.7 us -> 2.78 us
    unnamed x473 -> x123, local copies, waits for them, and re-layouts: 303 us -> 20.3 us
    psum x1 -> x0, waiting for transfers between devices: 209 us -> none  [local(): output_grad, project_grad = lax.psum((output_grad, project_grad), 'batch')]
    pallas_call x13 -> x34, Pallas kernels: 24.6 us -> 122 us  [the longest x3 34.4 us: own_part(): pl.pallas_call(kernel, grid_spec=pltpu.PrefetchScalarGridSpec(num_scalar_...]
    ppermute x0 -> x32, waiting for transfers between devices: none -> 92.1 us  [crossed(): return lax.ppermute(value, 'batch', route)]
    dot_general x12 -> x0, matrix products: 48.2 us -> none  [dot_tn(): lax.dot_general(left, right, (((0,), (0,)), ((), ())), preferred_element_...]
    pallas_call x56, Pallas kernels: 390 us -> 343 us  [call(): pl.pallas_call(kernel, in_specs=specs + carried_specs, out_specs=carried_...]
    ppermute x24, waiting for transfers between devices: 29.1 us -> 72.6 us  [shifted(): return lax.ppermute(value, 'section', route)]
    ppermute x0 -> x32, starting transfers between devices: none -> 37.4 us  [crossed(): return lax.ppermute(value, 'batch', route)]
  transfers between devices with their start and end apart: 41 -> 69, of which waited for: 6 -> 23; matrix products, arithmetic and copies ran while one was open for 6% -> 1% of each run, Pallas kernels for 33% -> 57%
where the time goes in v1:
time: 772 us; the launch traced here: 761 us
  Pallas kernels  464 us (60%)
  waiting for transfers between devices  176 us (23%)
  starting transfers between devices  88.5 us (11%)
  local copies, waits for them, and re-layouts  28.6 us (4%)
    pallas_call x56, Pallas kernels, call(): pl.pallas_call(kernel, in_specs=specs + carried_specs, out_specs=carried_...  343 us
    ppermute x32, waiting for transfers between devices, crossed(): return lax.ppermute(value, 'batch', route)  92.1 us
    ppermute x24, waiting for transfers between devices, shifted(): return lax.ppermute(value, 'section', route)  72.6 us
    ppermute x24, starting transfers between devices, shifted(): return lax.ppermute(value, 'section', route)  47.9 us
    ppermute x32, starting transfers between devices, crossed(): return lax.ppermute(value, 'batch', route)  37.4 us
    pallas_call x3, Pallas kernels, own_part(): pl.pallas_call(kernel, grid_spec=pltpu.PrefetchScalarGridSpec(num_scalar_...  34.4 us
    pallas_call x3, Pallas kernels, other_part(): pl.pallas_call(kernel, grid=(rows // tile,), in_specs=[pl.BlockSpec((leng...  26.5 us
    unnamed x123, local copies, waits for them, and re-layouts  20.3 us
  transfers between devices with their start and end apart: 69, of which 23 were waited for; matrix products, arithmetic and copies ran while one was open for 1% of the time, Pallas kernels for 57%

profile of v1, /device:TPU:0, one launch (start us, length us, event | category | flops | bytes accessed | tf_op | source)
XLA Modules:
  0.0 761.2 jit_solution(13595702372344799660)
XLA Ops:
  7.9 11.0 %collective-permute-done.1.source = bf16[3,1024,512]{2,1,0:T(8,128)(2,1)} collective-permute-done((bf16[3,1024,512]{2,1,0:T(8,128)(2,1)}, bf16[3,1024,512]{2,1,0:T(8,128)(2,1)}, u32[]{:S(2)}, u32[]{:S(2)}) %collective-permute-start.1) | collective-permute-done | bytes 3145760 | tf_op jit(solution)/shard_map/ppermute | solution.py:885
  50.9 10.1 %shard_map.296 = (bf16[1024,1024]{1,0:T(8,128)(2,1)S(1)}, bf16[1024,1024]{1,0:T(8,128)(2,1)S(1)}, bf16[1024,1024]{1,0:T(8,128)(2,1)}, bf16[1024,1024]{1,0:T(8,12...) custom-call(s32[1]{0:T(128)} %constant.87.clone.1.tick_ref, ...), custom_call_target="tpu_custom_call", output_to_operand_aliasing={{0}: (15, {}), {1}: (16, {}), {2}: (17, {}), {3}: (18, {}),... | custom-call | flops 2147483648 | bytes 4194304 | tf_op jit(solution)/shard_map/pallas_call | solution.py:582
  84.6 10.3 %shard_map.302 = (bf16[1024,1024]{1,0:T(8,128)(2,1)S(1)}, bf16[1024,1024]{1,0:T(8,128)(2,1)S(1)}, bf16[1024,1024]{1,0:T(8,128)(2,1)}, bf16[1024,1024]{1,0:T(8,12...) custom-call(s32[1]{0:T(128)} %constant.86.clone.1.tick_ref, ...), custom_call_target="tpu_custom_call", output_to_operand_aliasing={{0}: (15, {}), {1}: (16, {}), {2}: (17, {}), {3}: (18, {}),... | custom-call | flops 2147483648 | bytes 4194304 | tf_op jit(solution)/shard_map/pallas_call | solution.py:582
  102.6 9.5 %shard_map.305 = (bf16[1024,1024]{1,0:T(8,128)(2,1)S(1)}, bf16[1024,1024]{1,0:T(8,128)(2,1)S(1)}, bf16[1024,1024]{1,0:T(8,128)(2,1)}, bf16[1024,1024]{1,0:T(8,12...) custom-call(s32[1]{0:T(128)} %constant.73.clone.1.tick_ref, ...), custom_call_target="tpu_custom_call", output_to_operand_aliasing={{0}: (15, {}), {1}: (16, {}), {2}: (17, {}), {3}: (18, {}),... | custom-call | flops 2147483648 | bytes 4194304 | tf_op jit(solution)/shard_map/pallas_call | solution.py:582
  119.8 10.1 %shard_map.306 = (bf16[1024,1024]{1,0:T(8,128)(2,1)S(1)}, bf16[1024,1024]{1,0:T(8,128)(2,1)S(1)}, bf16[1024,1024]{1,0:T(8,128)(2,1)}, bf16[1024,1024]{1,0:T(8,12...) custom-call(s32[1]{0:T(128)} %constant.85.clone.1.tick_ref, ...), custom_call_target="tpu_custom_call", output_to_operand_aliasing={{0}: (15, {}), {1}: (16, {}), {2}: (17, {}), {3}: (18, {}),... | custom-call | flops 2147483648 | bytes 4194304 | tf_op jit(solution)/shard_map/pallas_call | solution.py:582
  137.6 10.0 %shard_map.309 = (bf16[1024,1024]{1,0:T(8,128)(2,1)S(1)}, bf16[1024,1024]{1,0:T(8,128)(2,1)S(1)}, bf16[1024,1024]{1,0:T(8,128)(2,1)}, bf16[1024,1024]{1,0:T(8,12...) custom-call(s32[1]{0:T(128)} %constant.91.clone.1.tick_ref, ...), custom_call_target="tpu_custom_call", output_to_operand_aliasing={{0}: (15, {}), {1}: (16, {}), {2}: (17, {}), {3}: (18, {}),... | custom-call | flops 2147483648 | bytes 4194304 | tf_op jit(solution)/shard_map/pallas_call | solution.py:582
  155.2 10.6 %shard_map.310 = (bf16[1024,1024]{1,0:T(8,128)(2,1)S(1)}, bf16[1024,1024]{1,0:T(8,128)(2,1)S(1)}, bf16[1024,1024]{1,0:T(8,128)(2,1)}, bf16[1024,1024]{1,0:T(8,12...) custom-call(s32[1]{0:T(128)} %constant.84.clone.1.tick_ref, ...), custom_call_target="tpu_custom_call", output_to_operand_aliasing={{0}: (15, {}), {1}: (16, {}), {2}: (17, {}), {3}: (18, {}),... | custom-call | flops 2147483648 | bytes 4194304 | tf_op jit(solution)/shard_map/pallas_call | solution.py:582
  181.4 9.0 %shard_map.314 = (bf16[1024,1024]{1,0:T(8,128)(2,1)S(1)}, bf16[1024,1024]{1,0:T(8,128)(2,1)S(1)}, bf16[1024,1024]{1,0:T(8,128)(2,1)}, bf16[1024,1024]{1,0:T(8,12...) custom-call(s32[1]{0:T(128)} %constant.83.clone.1.tick_ref, ...), custom_call_target="tpu_custom_call", output_to_operand_aliasing={{0}: (15, {}), {1}: (16, {}), {2}: (17, {}), {3}: (18, {}),... | custom-call | flops 2147483648 | bytes 4194304 | tf_op jit(solution)/shard_map/pallas_call | solution.py:582
  191.0 9.0 %collective-permute-start.14 = (bf16[128,1024]{1,0:T(8,128)(2,1)S(1)}, bf16[128,1024]{1,0:T(8,128)(2,1)S(1)}, u32[]{:S(2)}, u32[]{:S(2)}) collective-permute-start(bf16[128,1024]{1,0:T(8,128)(2,1)S(1)} %get-tuple-element.713), channel_id=1, source_target_pairs={{0,8},{8,16},{16,24},{1,9},{9,17},{17,25},{2,10},{10,18},{18,26},{... | collective-permute-start | bytes 786440 | tf_op jit(solution)/shard_map/ppermute | solution.py:968
  206.7 9.1 %shard_map.318 = (bf16[1024,1024]{1,0:T(8,128)(2,1)S(1)}, bf16[1024,1024]{1,0:T(8,128)(2,1)S(1)}, bf16[1024,1024]{1,0:T(8,128)(2,1)}, bf16[1024,1024]{1,0:T(8,12...) custom-call(s32[1]{0:T(128)} %constant.82.clone.1.tick_ref, ...), custom_call_target="tpu_custom_call", output_to_operand_aliasing={{0}: (15, {}), {1}: (16, {}), {2}: (17, {}), {3}: (18, {}),... | custom-call | flops 2147483648 | bytes 4194304 | tf_op jit(solution)/shard_map/pallas_call | solution.py:582
  224.7 8.9 %shard_map.322 = (bf16[1024,1024]{1,0:T(8,128)(2,1)S(1)}, bf16[1024,1024]{1,0:T(8,128)(2,1)S(1)}, bf16[1024,1024]{1,0:T(8,128)(2,1)}, bf16[1024,1024]{1,0:T(8,12...) custom-call(s32[1]{0:T(128)} %constant.80.clone.1.tick_ref, ...), custom_call_target="tpu_custom_call", output_to_operand_aliasing={{0}: (15, {}), {1}: (16, {}), {2}: (17, {}), {3}: (18, {}),... | custom-call | flops 2147483648 | bytes 4194304 | tf_op jit(solution)/shard_map/pallas_call | solution.py:582
  256.6 11.7 %collective-permute-done.21.inc_ref = bf16[128,1024]{1,0:T(8,128)(2,1)S(1)} collective-permute-done((bf16[128,1024]{1,0:T(8,128)(2,1)S(1)}, bf16[128,1024]{1,0:T(8,128)(2,1)S(1)}, u32[]{:S(2)}, u32[]{:S(2)}) %collective-permute-start.21) | collective-permute-done | bytes 262176 | tf_op jit(solution)/shard_map/ppermute | solution.py:968
  268.2 8.9 %shard_map.334 = (f32[4,1024]{1,0:T(4,128)S(1)}, f32[3,4096]{1,0:T(4,128)S(1)}, bf16[1024,1024]{1,0:T(8,128)(2,1)}, bf16[1024,4096]{1,0:T(8,128)(2,1)}, bf16[102...) custom-call(s32[1]{0:T(128)} %constant.90.clone.1.tick_ref, ...), custom_call_target="tpu_custom_call", output_to_operand_aliasing={{0}: (16, {}), {1}: (17, {}), {2}: (18, {}), {3}: (19, {}),... | custom-call | flops 2147483648 | bytes 4194304 | tf_op jit(solution)/shard_map/pallas_call | solution.py:582
  296.9 8.9 %shard_map.339 = (f32[4,1024]{1,0:T(4,128)S(1)}, f32[3,4096]{1,0:T(4,128)S(1)}, bf16[1024,1024]{1,0:T(8,128)(2,1)}, bf16[1024,4096]{1,0:T(8,128)(2,1)}, bf16[102...) custom-call(s32[1]{0:T(128)} %constant.85.clone.1.tick_ref, ...), custom_call_target="tpu_custom_call", output_to_operand_aliasing={{0}: (16, {}), {1}: (17, {}), {2}: (18, {}), {3}: (19, {}),... | custom-call | flops 2147483648 | bytes 4194304 | tf_op jit(solution)/shard_map/pallas_call | solution.py:582
  307.8 31.0 %collective-permute-done.25.inc_ref = bf16[128,1024]{1,0:T(8,128)(2,1)S(1)} collective-permute-done((bf16[128,1024]{1,0:T(8,128)(2,1)S(1)}, bf16[128,1024]{1,0:T(8,128)(2,1)S(1)}, u32[]{:S(2)}, u32[]{:S(2)}) %collective-permute-start.25) | collective-permute-done | bytes 262176 | tf_op jit(solution)/shard_map/ppermute | solution.py:968
  346.0 12.1 %shard_map.344 = (f32[7,1024]{1,0:T(8,128)S(1)}, f32[1024,1024]{1,0:T(8,128)S(1)}, f32[1024,1024]{1,0:T(8,128)S(1)}, bf16[1024,1024]{1,0:T(8,128)(2,1)}, bf16[10...) custom-call(s32[1]{0:T(128)} %constant.91.clone.1.tick_ref, ...), custom_call_target="tpu_custom_call", output_to_operand_aliasing={{0}: (18, {}), {1}: (19, {}), {2}: (20, {}), {3}: (21, {}),... | custom-call | flops 11000000512 | bytes 4194304 | tf_op jit(solution)/shard_map/pallas_call | solution.py:582
  369.1 11.4 %shard_map.345 = (f32[7,1024]{1,0:T(8,128)S(1)}, f32[1024,1024]{1,0:T(8,128)S(1)}, f32[1024,1024]{1,0:T(8,128)S(1)}, bf16[1024,1024]{1,0:T(8,128)(2,1)}, bf16[10...) custom-call(s32[1]{0:T(128)} %constant.84.clone.1.tick_ref, ...), custom_call_target="tpu_custom_call", output_to_operand_aliasing={{0}: (18, {}), {1}: (19, {}), {2}: (20, {}), {3}: (21, {}),... | custom-call | flops 11000000512 | bytes 4194304 | tf_op jit(solution)/shard_map/pallas_call | solution.py:582
  381.8 9.1 %shard_map.346 = (f32[4,1024]{1,0:T(4,128)S(1)}, f32[3,4096]{1,0:T(4,128)S(1)}, bf16[1024,1024]{1,0:T(8,128)(2,1)}, bf16[1024,4096]{1,0:T(8,128)(2,1)}, bf16[102...) custom-call(s32[1]{0:T(128)} %constant.92.clone.1.tick_ref, ...), custom_call_target="tpu_custom_call", output_to_operand_aliasing={{0}: (16, {}), {1}: (17, {}), {2}: (18, {}), {3}: (19, {}),... | custom-call | flops 2147483648 | bytes 4194304 | tf_op jit(solution)/shard_map/pallas_call | solution.py:582
  391.0 10.0 %shard_map.348 = (f32[7,1024]{1,0:T(8,128)S(1)}, f32[1024,1024]{1,0:T(8,128)S(1)}, f32[1024,1024]{1,0:T(8,128)S(1)}, bf16[1024,1024]{1,0:T(8,128)(2,1)}, bf16[10...) custom-call(s32[1]{0:T(128)} %constant.92.clone.1.tick_ref, ...), custom_call_target="tpu_custom_call", output_to_operand_aliasing={{0}: (18, {}), {1}: (19, {}), {2}: (20, {}), {3}: (21, {}),... | custom-call | flops 11000000512 | bytes 4194304 | tf_op jit(solution)/shard_map/pallas_call | solution.py:582
  409.5 10.6 %shard_map.349 = (f32[7,1024]{1,0:T(8,128)S(1)}, f32[1024,1024]{1,0:T(8,128)S(1)}, f32[1024,1024]{1,0:T(8,128)S(1)}, bf16[1024,1024]{1,0:T(8,128)(2,1)}, bf16[10...) custom-call(s32[1]{0:T(128)} %constant.83.clone.1.tick_ref, ...), custom_call_target="tpu_custom_call", output_to_operand_aliasing={{0}: (18, {}), {1}: (19, {}), {2}: (20, {}), {3}: (21, {}),... | custom-call | flops 11000000512 | bytes 4194304 | tf_op jit(solution)/shard_map/pallas_call | solution.py:582
  454.1 8.9 %shard_map.353 = (f32[7,1024]{1,0:T(8,128)S(1)}, f32[1024,1024]{1,0:T(8,128)S(1)}, f32[1024,1024]{1,0:T(8,128)S(1)}, bf16[1024,1024]{1,0:T(8,128)(2,1)}, bf16[10...) custom-call(s32[1]{0:T(128)} %constant.82.clone.1.tick_ref, ...), custom_call_target="tpu_custom_call", output_to_operand_aliasing={{0}: (18, {}), {1}: (19, {}), {2}: (20, {}), {3}: (21, {}),... | custom-call | flops 11000000512 | bytes 4194304 | tf_op jit(solution)/shard_map/pallas_call | solution.py:582
  473.1 9.1 %collective-permute-done.30.inc_ref = bf16[128,1024]{1,0:T(8,128)(2,1)S(1)} collective-permute-done((bf16[128,1024]{1,0:T(8,128)(2,1)S(1)}, bf16[128,1024]{1,0:T(8,128)(2,1)S(1)}, u32[]{:S(2)}, u32[]{:S(2)}) %collective-permute-start.30) | collective-permute-done | bytes 262176 | tf_op jit(solution)/shard_map/ppermute | solution.py:968
  482.3 9.4 %shard_map.355 = (f32[4,1024]{1,0:T(4,128)S(1)}, f32[3,4096]{1,0:T(4,128)S(1)}, bf16[1024,1024]{1,0:T(8,128)(2,1)}, bf16[1024,4096]{1,0:T(8,128)(2,1)}, bf16[102...) custom-call(s32[1]{0:T(128)} %constant.80.clone.1.tick_ref, ...), custom_call_target="tpu_custom_call", output_to_operand_aliasing={{0}: (16, {}), {1}: (17, {}), {2}: (18, {}), {3}: (19, {}),... | custom-call | flops 2147483648 | bytes 4194304 | tf_op jit(solution)/shard_map/pallas_call | solution.py:582
  509.4 10.2 %shard_map.358 = (bf16[512,1024]{1,0:T(8,128)(2,1)}, bf16[512,1024]{1,0:T(8,128)(2,1)}, bf16[512,1024]{1,0:T(8,128)(2,1)}, bf16[512,1024]{1,0:T(8,128)(2,1)}) custom-call(s32[6]{0:T(128)S(1)} %stack.38.after.section_ref.place_ref, bf16[1024,4096]{1,0:T(8,128)(2,1)} %get-tuple-element.786.refs_0_, bf16[1024,1024]{1,0:T(8,128)(2,1)} %get-tuple-element.993.refs_1_.refs_2_, ...), custom_call_target="tpu_custom_call" | custom-call | flops 1100000000 | bytes 1024 | tf_op jit(solution)/shard_map/pallas_call | solution.py:722
  523.2 10.6 %shard_map.359 = (bf16[256,2048]{1,0:T(8,128)(2,1)}, bf16[256,2048]{1,0:T(8,128)(2,1)}, bf16[256,2048]{1,0:T(8,128)(2,1)}, bf16[256,2048]{1,0:T(8,128)(2,1)}) custom-call(s32[6]{0:T(128)S(1)} %stack.38.after.section_ref.place_ref, bf16[1024,1024]{1,0:T(8,128)(2,1)} %get-tuple-element.994.refs_0_, bf16[1024,4096]{1,0:T(8,128)(2,1)} %get-tuple-element.995.refs_1_, ...), custom_call_target="tpu_custom_call" | custom-call | flops 1100000000 | bytes 1024 | tf_op jit(solution)/shard_map/pallas_call | solution.py:722
  546.5 9.3 %shard_map.360 = (f32[7,1024]{1,0:T(8,128)S(1)}, f32[1024,1024]{1,0:T(8,128)S(1)}, f32[1024,1024]{1,0:T(8,128)S(1)}, bf16[1024,1024]{1,0:T(8,128)(2,1)}, bf16[10...) custom-call(s32[1]{0:T(128)} %constant.94.clone.1.tick_ref, ...), custom_call_target="tpu_custom_call", output_to_operand_aliasing={{0}: (18, {}), {1}: (19, {}), {2}: (20, {}), {3}: (21, {}),... | custom-call | flops 1100000000 | bytes 4194304 | tf_op jit(solution)/shard_map/pallas_call | solution.py:582
  559.3 9.5 %shard_map.362 = (f32[7,1024]{1,0:T(8,128)S(1)}, f32[1024,1024]{1,0:T(8,128)S(1)}, f32[1024,1024]{1,0:T(8,128)S(1)}, bf16[1024,1024]{1,0:T(8,128)(2,1)}, bf16[10...) custom-call(s32[1]{0:T(128)} %constant.80.clone.1.tick_ref, ...), custom_call_target="tpu_custom_call", output_to_operand_aliasing={{0}: (18, {}), {1}: (19, {}), {2}: (20, {}), {3}: (21, {}),... | custom-call | flops 1100000000 | bytes 4194304 | tf_op jit(solution)/shard_map/pallas_call | solution.py:582
  569.4 9.2 %shard_map.363.refs_4_ = bf16[1024,2048]{1,0:T(8,128)(2,1)} custom-call(bf16[1024,1024]{1,0:T(8,128)(2,1)} %get-tuple-element.1015.refs_0_, bf16[1024,1024]{1,0:T(8,128)(2,1)} %get-tuple-element.1016.refs_1_, bf16[1024,1024]{1,0:T(8,128)(2,1)} %get-tuple-element.1025.refs_2_, bf16[1024,1024]{1,0:T(8,128)(2,1)} %get-tuple-element.1026.refs_3_, ...), custom_call_target="tpu_custom_call" | custom-call | flops 1100000000 | bytes 1024 | tf_op jit(solution)/shard_map/pallas_call | solution.py:683
  588.1 13.6 %shard_map.365 = (bf16[256,2048]{1,0:T(8,128)(2,1)}, bf16[256,2048]{1,0:T(8,128)(2,1)}, bf16[256,2048]{1,0:T(8,128)(2,1)}, bf16[256,2048]{1,0:T(8,128)(2,1)}) custom-call(s32[6]{0:T(128)S(1)} %stack.38.after.section_ref.place_ref, bf16[1024,1024]{1,0:T(8,128)(2,1)} %get-tuple-element.1015.refs_0_, bf16[1024,1024]{1,0:T(8,128)(2,1)} %get-tuple-element.1016.refs_1_, ...), custom_call_target="tpu_custom_call" | custom-call | flops 1100000000 | bytes 1024 | tf_op jit(solution)/shard_map/pallas_call | solution.py:722
  608.0 20.0 %collective-permute-done.42.refs_1_ = bf16[256,2048]{1,0:T(8,128)(2,1)S(1)} collective-permute-done((bf16[256,2048]{1,0:T(8,128)(2,1)}, bf16[256,2048]{1,0:T(8,128)(2,1)S(1)}, u32[]{:S(2)}, u32[]{:S(2)}) %collective-permute-start.42) | collective-permute-done | bytes 1048608 | tf_op jit(solution)/shard_map/ppermute | solution.py:656
  653.4 9.6 %collective-permute-done.52.refs_2_ = bf16[256,1024]{1,0:T(8,128)(2,1)S(1)} collective-permute-done((bf16[256,1024]{1,0:T(8,128)(2,1)S(1)}, bf16[256,1024]{1,0:T(8,128)(2,1)S(1)}, u32[]{:S(2)}, u32[]{:S(2)}) %collective-permute-start.52) | collective-permute-done | bytes 524320 | tf_op jit(solution)/shard_map/ppermute | solution.py:656
  718.5 12.0 %collective-permute-done.65.refs_3_ = bf16[128,2048]{1,0:T(8,128)(2,1)S(1)} collective-permute-done((bf16[128,2048]{1,0:T(8,128)(2,1)S(1)}, bf16[128,2048]{1,0:T(8,128)(2,1)S(1)}, u32[]{:S(2)}, u32[]{:S(2)}) %collective-permute-start.65) | collective-permute-done | bytes 524320 | tf_op jit(solution)/shard_map/ppermute | solution.py:656
  (365 shorter events, 405.8 us)
Async XLA Ops:
  0.7 38.1 %collective-permute-start.4 = (bf16[1024,2048]{1,0:T(8,128)(2,1)}, bf16[1024,2048]{1,0:T(8,128)(2,1)}, u32[]{:S(2)}, u32[]{:S(2)}) collective-permute-start(bf16[1024,2048]{1,0:T(8,128)(2,1)} %bitcast.183), channel_id=1, source_target_pairs={{0,1},{1,0},{2,3},{3,2},{4,5},{5,4},{6,7},{7,6},{8,9},{9,8},{10,11... | collective-permute-start | bytes 12582920 | tf_op jit(solution)/shard_map/ppermute | solution.py:885
  1.3 39.8 %collective-permute-start.5 = (bf16[2048,1024]{1,0:T(8,128)(2,1)}, bf16[2048,1024]{1,0:T(8,128)(2,1)}, u32[]{:S(2)}, u32[]{:S(2)}) collective-permute-start(bf16[2048,1024]{1,0:T(8,128)(2,1)} %bitcast.181), channel_id=1, source_target_pairs={{0,1},{1,0},{2,3},{3,2},{4,5},{5,4},{6,7},{7,6},{8,9},{9,8},{10,11... | collective-permute-start | bytes 12582920 | tf_op jit(solution)/shard_map/ppermute | solution.py:885
  1.8 27.1 %collective-permute-start.2 = (bf16[512,1024]{1,0:T(8,128)(2,1)}, bf16[512,1024]{1,0:T(8,128)(2,1)}, u32[]{:S(2)}, u32[]{:S(2)}) collective-permute-start(bf16[512,1024]{1,0:T(8,128)(2,1)} %bitcast.187), channel_id=1, source_target_pairs={{0,1},{1,0},{2,3},{3,2},{4,5},{5,4},{6,7},{7,6},{8,9},{9,8},{10,11... | collective-permute-start | bytes 3145736 | tf_op jit(solution)/shard_map/ppermute | solution.py:885
  4.1 26.2 %collective-permute-start = (bf16[512,1024]{1,0:T(8,128)(2,1)}, bf16[512,1024]{1,0:T(8,128)(2,1)}, u32[]{:S(2)}, u32[]{:S(2)}) collective-permute-start(bf16[512,1024]{1,0:T(8,128)(2,1)} %dynamic-slice_bitcast_fusion.1), channel_id=1, source_target_pairs={{0,1},{1,0},{2,3},{3,2},{4,5},{5,4},{6,7},{7,6},{8,9},{9,8},{10,11... | collective-permute-start | bytes 3145736 | tf_op jit(solution)/shard_map/ppermute | solution.py:885
  28.8 215.4 %collective-permute-start.19 = (bf16[512,1024]{1,0:T(8,128)(2,1)}, bf16[512,1024]{1,0:T(8,128)(2,1)}, u32[]{:S(2)}, u32[]{:S(2)}) collective-permute-start(bf16[512,1024]{1,0:T(8,128)(2,1)} %dynamic-slice_bitcast_fusion), channel_id=1, source_target_pairs={{0,1},{1,0},{2,3},{3,2},{4,5},{5,4},{6,7},{7,6},{8,9},{9,8},{10,11... | collective-permute-start | bytes 3145736 | tf_op jit(solution)/shard_map/ppermute | solution.py:885
  174.8 25.3 %collective-permute-start.15 = (bf16[128,1024]{1,0:T(8,128)(2,1)S(1)}, bf16[128,1024]{1,0:T(8,128)(2,1)S(1)}, u32[]{:S(2)}, u32[]{:S(2)}) collective-permute-start(bf16[128,1024]{1,0:T(8,128)(2,1)S(1)} %get-tuple-element.714), channel_id=1, source_target_pairs={{0,8},{8,16},{16,24},{1,9},{9,17},{17,25},{2,10},{10,18},{18,26},{... | collective-permute-start | bytes 786440 | tf_op jit(solution)/shard_map/ppermute | solution.py:968
  255.3 23.8 %collective-permute-start.20 = (bf16[128,1024]{1,0:T(8,128)(2,1)S(1)}, bf16[128,1024]{1,0:T(8,128)(2,1)S(1)}, u32[]{:S(2)}, u32[]{:S(2)}) collective-permute-start(bf16[128,1024]{1,0:T(8,128)(2,1)S(1)} %get-tuple-element.831), channel_id=1, source_target_pairs={{8,0},{16,8},{24,16},{9,1},{17,9},{25,17},{10,2},{18,10},{26,18},{... | collective-permute-start | bytes 786440 | tf_op jit(solution)/shard_map/ppermute | solution.py:968
  290.2 48.6 %collective-permute-start.25 = (bf16[128,1024]{1,0:T(8,128)(2,1)S(1)}, bf16[128,1024]{1,0:T(8,128)(2,1)S(1)}, u32[]{:S(2)}, u32[]{:S(2)}) collective-permute-start(bf16[128,1024]{1,0:T(8,128)(2,1)S(1)} %get-tuple-element.892), channel_id=1, source_target_pairs={{8,0},{16,8},{24,16},{9,1},{17,9},{25,17},{10,2},{18,10},{26,18},{... | collective-permute-start | bytes 786440 | tf_op jit(solution)/shard_map/ppermute | solution.py:968
  306.5 55.4 %collective-permute-start.24 = (bf16[128,1024]{1,0:T(8,128)(2,1)S(1)}, bf16[128,1024]{1,0:T(8,128)(2,1)S(1)}, u32[]{:S(2)}, u32[]{:S(2)}) collective-permute-start(bf16[128,1024]{1,0:T(8,128)(2,1)S(1)} %get-tuple-element.891), channel_id=1, source_target_pairs={{8,0},{16,8},{24,16},{9,1},{17,9},{25,17},{10,2},{18,10},{26,18},{... | collective-permute-start | bytes 786440 | tf_op jit(solution)/shard_map/ppermute | solution.py:968
  420.1 26.2 %collective-permute-start.28 = (bf16[128,1024]{1,0:T(8,128)(2,1)S(1)}, bf16[128,1024]{1,0:T(8,128)(2,1)S(1)}, u32[]{:S(2)}, u32[]{:S(2)}) collective-permute-start(bf16[128,1024]{1,0:T(8,128)(2,1)S(1)} %get-tuple-element.951), channel_id=1, source_target_pairs={{8,0},{16,8},{24,16},{9,1},{17,9},{25,17},{10,2},{18,10},{26,18},{... | collective-permute-start | bytes 786440 | tf_op jit(solution)/shard_map/ppermute | solution.py:968
  439.0 25.3 %collective-permute-start.31 = (bf16[128,1024]{1,0:T(8,128)(2,1)S(1)}, bf16[128,1024]{1,0:T(8,128)(2,1)S(1)}, u32[]{:S(2)}, u32[]{:S(2)}) collective-permute-start(bf16[128,1024]{1,0:T(8,128)(2,1)S(1)} %get-tuple-element.982), channel_id=1, source_target_pairs={{8,0},{16,8},{24,16},{9,1},{17,9},{25,17},{10,2},{18,10},{26,18},{... | collective-permute-start | bytes 786440 | tf_op jit(solution)/shard_map/ppermute | solution.py:968
  519.6 36.2 %collective-permute-start.33 = (bf16[512,1024]{1,0:T(8,128)(2,1)}, bf16[512,1024]{1,0:T(8,128)(2,1)}, u32[]{:S(2)}, u32[]{:S(2)}) collective-permute-start(bf16[512,1024]{1,0:T(8,128)(2,1)} %get-tuple-element.997), channel_id=1, source_target_pairs={{0,2},{2,0},{4,6},{6,4},{1,3},{3,1},{5,7},{7,5},{8,10},{10,8},{12,... | collective-permute-start | bytes 3145736 | tf_op jit(solution)/shard_map/ppermute | solution.py:656
  521.6 34.2 %collective-permute-start.34 = (bf16[512,1024]{1,0:T(8,128)(2,1)}, bf16[512,1024]{1,0:T(8,128)(2,1)}, u32[]{:S(2)}, u32[]{:S(2)}) collective-permute-start(bf16[512,1024]{1,0:T(8,128)(2,1)} %get-tuple-element.999), channel_id=1, source_target_pairs={{0,4},{2,6},{4,0},{6,2},{1,5},{3,7},{5,1},{7,3},{8,12},{10,14},{12... | collective-permute-start | bytes 3145736 | tf_op jit(solution)/shard_map/ppermute | solution.py:656
  533.9 44.7 %collective-permute-start.39 = (bf16[256,2048]{1,0:T(8,128)(2,1)}, bf16[256,2048]{1,0:T(8,128)(2,1)}, u32[]{:S(2)}, u32[]{:S(2)}) collective-permute-start(bf16[256,2048]{1,0:T(8,128)(2,1)} %get-tuple-element.1031), channel_id=1, source_target_pairs={{0,2},{2,0},{4,6},{6,4},{1,3},{3,1},{5,7},{7,5},{8,10},{10,8},{12,... | collective-permute-start | bytes 3145736 | tf_op jit(solution)/shard_map/ppermute | solution.py:656
  534.3 46.4 %collective-permute-start.40 = (bf16[256,2048]{1,0:T(8,128)(2,1)}, bf16[256,2048]{1,0:T(8,128)(2,1)}, u32[]{:S(2)}, u32[]{:S(2)}) collective-permute-start(bf16[256,2048]{1,0:T(8,128)(2,1)} %get-tuple-element.1032), channel_id=1, source_target_pairs={{0,4},{2,6},{4,0},{6,2},{1,5},{3,7},{5,1},{7,3},{8,12},{10,14},{12... | collective-permute-start | bytes 3145736 | tf_op jit(solution)/shard_map/ppermute | solution.py:656
  534.3 71.2 %collective-permute-start.18 = (bf16[512,1024]{1,0:T(8,128)(2,1)}, bf16[512,1024]{1,0:T(8,128)(2,1)}, u32[]{:S(2)}, u32[]{:S(2)}) collective-permute-start(bf16[512,1024]{1,0:T(8,128)(2,1)} %get-tuple-element.785), channel_id=1, source_target_pairs={{0,1},{1,0},{2,3},{3,2},{4,5},{5,4},{6,7},{7,6},{8,9},{9,8},{10,11... | collective-permute-start | bytes 3145736 | tf_op jit(solution)/shard_map/ppermute | solution.py:885
  568.8 72.1 %collective-permute-start.41 = (bf16[512,1024]{1,0:T(8,128)(2,1)}, bf16[512,1024]{1,0:T(8,128)(2,1)}, u32[]{:S(2)}, u32[]{:S(2)}) collective-permute-start(bf16[512,1024]{1,0:T(8,128)(2,1)} %get-tuple-element.1029.refs_6_), channel_id=1, source_target_pairs={{0,1},{1,0},{2,3},{3,2},{4,5},{5,4},{6,7},{7,6},{8,9},{9,8},{10,11... | collective-permute-start | bytes 3145736 | tf_op jit(solution)/shard_map/ppermute | solution.py:885
  586.1 46.3 %collective-permute-start.46 = (bf16[128,2048]{1,0:T(8,128)(2,1)}, bf16[128,2048]{1,0:T(8,128)(2,1)S(1)}, u32[]{:S(2)}, u32[]{:S(2)}) collective-permute-start(bf16[128,2048]{1,0:T(8,128)(2,1)} %get-tuple-element.1044), channel_id=1, source_target_pairs={{0,4},{2,6},{4,0},{6,2},{1,5},{3,7},{5,1},{7,3},{8,12},{10,14},{12... | collective-permute-start | bytes 1572872 | tf_op jit(solution)/shard_map/ppermute | solution.py:656
  601.7 26.3 %collective-permute-start.42 = (bf16[256,2048]{1,0:T(8,128)(2,1)}, bf16[256,2048]{1,0:T(8,128)(2,1)S(1)}, u32[]{:S(2)}, u32[]{:S(2)}) collective-permute-start(bf16[256,2048]{1,0:T(8,128)(2,1)} %get-tuple-element.1038), channel_id=1, source_target_pairs={{0,2},{2,0},{4,6},{6,4},{1,3},{3,1},{5,7},{7,5},{8,10},{10,8},{12,... | collective-permute-start | bytes 3145736 | tf_op jit(solution)/shard_map/ppermute | solution.py:656
  603.4 24.8 %collective-permute-start.43 = (bf16[256,2048]{1,0:T(8,128)(2,1)}, bf16[256,2048]{1,0:T(8,128)(2,1)S(1)}, u32[]{:S(2)}, u32[]{:S(2)}) collective-permute-start(bf16[256,2048]{1,0:T(8,128)(2,1)} %get-tuple-element.1039), channel_id=1, source_target_pairs={{0,4},{2,6},{4,0},{6,2},{1,5},{3,7},{5,1},{7,3},{8,12},{10,14},{12... | collective-permute-start | bytes 3145736 | tf_op jit(solution)/shard_map/ppermute | solution.py:656
  607.8 31.4 %collective-permute-start.47 = (bf16[128,2048]{1,0:T(8,128)(2,1)S(1)}, bf16[128,2048]{1,0:T(8,128)(2,1)S(1)}, u32[]{:S(2)}, u32[]{:S(2)}) collective-permute-start(bf16[128,2048]{1,0:T(8,128)(2,1)S(1)} %copy-done.55), channel_id=1, source_target_pairs={{0,2},{2,0},{4,6},{6,4},{1,3},{3,1},{5,7},{7,5},{8,10},{10,8},{12,... | collective-permute-start | bytes 1572872 | tf_op jit(solution)/shard_map/ppermute | solution.py:656
  642.9 31.4 %collective-permute-start.45 = (bf16[128,2048]{1,0:T(8,128)(2,1)}, bf16[128,2048]{1,0:T(8,128)(2,1)S(1)}, u32[]{:S(2)}, u32[]{:S(2)}) collective-permute-start(bf16[128,2048]{1,0:T(8,128)(2,1)} %get-tuple-element.1043), channel_id=1, source_target_pairs={{0,2},{2,0},{4,6},{6,4},{1,3},{3,1},{5,7},{7,5},{8,10},{10,8},{12,... | collective-permute-start | bytes 1572872 | tf_op jit(solution)/shard_map/ppermute | solution.py:656
  651.8 33.7 %collective-permute-start.53 = (bf16[256,1024]{1,0:T(8,128)(2,1)S(1)}, bf16[256,1024]{1,0:T(8,128)(2,1)S(1)}, u32[]{:S(2)}, u32[]{:S(2)}) collective-permute-start(bf16[256,1024]{1,0:T(8,128)(2,1)S(1)} %collective-permute-done.51.refs_1_), channel_id=1, source_target_pairs={{0,2},{2,0},{4,6},{6,4},{1,3},{3,1},{5,7},{7,5},{8,10},{10,8},{12,... | collective-permute-start | bytes 1572872 | tf_op jit(solution)/shard_map/ppermute | solution.py:656
  663.1 24.5 %collective-permute-start.63 = (bf16[128,2048]{1,0:T(8,128)(2,1)}, bf16[128,2048]{1,0:T(8,128)(2,1)S(1)}, u32[]{:S(2)}, u32[]{:S(2)}) collective-permute-start(bf16[128,2048]{1,0:T(8,128)(2,1)} %get-tuple-element.1047.refs_4_.refs_0_), channel_id=1, source_target_pairs={{0,4},{2,6},{4,0},{6,2},{1,5},{3,7},{5,1},{7,3},{8,12},{10,14},{12... | collective-permute-start | bytes 1572872 | tf_op jit(solution)/shard_map/ppermute | solution.py:656
  665.1 31.7 %collective-permute-start.66 = (bf16[128,2048]{1,0:T(8,128)(2,1)}, bf16[128,2048]{1,0:T(8,128)(2,1)S(1)}, u32[]{:S(2)}, u32[]{:S(2)}) collective-permute-start(bf16[128,2048]{1,0:T(8,128)(2,1)} %get-tuple-element.1055.refs_4_), channel_id=1, source_target_pairs={{0,2},{2,0},{4,6},{6,4},{1,3},{3,1},{5,7},{7,5},{8,10},{10,8},{12,... | collective-permute-start | bytes 1572872 | tf_op jit(solution)/shard_map/ppermute | solution.py:656
  674.3 33.7 %collective-permute-start.64 = (bf16[128,2048]{1,0:T(8,128)(2,1)}, bf16[128,2048]{1,0:T(8,128)(2,1)S(1)}, u32[]{:S(2)}, u32[]{:S(2)}) collective-permute-start(bf16[128,2048]{1,0:T(8,128)(2,1)} %get-tuple-element.1047.refs_4_.refs_0_), channel_id=1, source_target_pairs={{0,2},{2,0},{4,6},{6,4},{1,3},{3,1},{5,7},{7,5},{8,10},{10,8},{12,... | collective-permute-start | bytes 1572872 | tf_op jit(solution)/shard_map/ppermute | solution.py:656
  685.5 30.5 %collective-permute-start.67 = (bf16[128,2048]{1,0:T(8,128)(2,1)S(1)}, bf16[128,2048]{1,0:T(8,128)(2,1)S(1)}, u32[]{:S(2)}, u32[]{:S(2)}) collective-permute-start(bf16[128,2048]{1,0:T(8,128)(2,1)S(1)} %copy-done.31), channel_id=1, source_target_pairs={{0,4},{2,6},{4,0},{6,2},{1,5},{3,7},{5,1},{7,3},{8,12},{10,14},{12... | collective-permute-start | bytes 1572872 | tf_op jit(solution)/shard_map/ppermute | solution.py:656
  685.5 45.7 %collective-permute-start.57 = (bf16[128,2048]{1,0:T(8,128)(2,1)}, bf16[128,2048]{1,0:T(8,128)(2,1)}, u32[]{:S(2)}, u32[]{:S(2)}) collective-permute-start(bf16[128,2048]{1,0:T(8,128)(2,1)} %get-tuple-element.1048.after_ref.refs_0_), channel_id=1, source_target_pairs={{0,4},{2,6},{4,0},{6,2},{1,5},{3,7},{5,1},{7,3},{8,12},{10,14},{12... | collective-permute-start | bytes 1572872 | tf_op jit(solution)/shard_map/ppermute | solution.py:656
  687.6 45.7 %collective-permute-start.60 = (bf16[128,2048]{1,0:T(8,128)(2,1)}, bf16[128,2048]{1,0:T(8,128)(2,1)}, u32[]{:S(2)}, u32[]{:S(2)}) collective-permute-start(bf16[128,2048]{1,0:T(8,128)(2,1)} %get-tuple-element.1054.refs_4_), channel_id=1, source_target_pairs={{0,2},{2,0},{4,6},{6,4},{1,3},{3,1},{5,7},{7,5},{8,10},{10,8},{12,... | collective-permute-start | bytes 1572872 | tf_op jit(solution)/shard_map/ppermute | solution.py:656
  696.8 33.7 %collective-permute-start.65 = (bf16[128,2048]{1,0:T(8,128)(2,1)S(1)}, bf16[128,2048]{1,0:T(8,128)(2,1)S(1)}, u32[]{:S(2)}, u32[]{:S(2)}) collective-permute-start(bf16[128,2048]{1,0:T(8,128)(2,1)S(1)} %collective-permute-done.63.refs_1_), channel_id=1, source_target_pairs={{0,2},{2,0},{4,6},{6,4},{1,3},{3,1},{5,7},{7,5},{8,10},{10,8},{12,... | collective-permute-start | bytes 1572872 | tf_op jit(solution)/shard_map/ppermute | solution.py:656
  714.0 25.3 %collective-permute-start.68 = (bf16[128,2048]{1,0:T(8,128)(2,1)S(1)}, bf16[128,2048]{1,0:T(8,128)(2,1)}, u32[]{:S(2)}, u32[]{:S(2)}) collective-permute-start(bf16[128,2048]{1,0:T(8,128)(2,1)S(1)} %collective-permute-done.66.refs_5_), channel_id=1, source_target_pairs={{0,4},{2,6},{4,0},{6,2},{1,5},{3,7},{5,1},{7,3},{8,12},{10,14},{12... | collective-permute-start | bytes 1572872 | tf_op jit(solution)/shard_map/ppermute | solution.py:656
  716.9 31.1 %collective-permute-start.58 = (bf16[128,2048]{1,0:T(8,128)(2,1)S(1)}, bf16[128,2048]{1,0:T(8,128)(2,1)}, u32[]{:S(2)}, u32[]{:S(2)}) collective-permute-start(bf16[128,2048]{1,0:T(8,128)(2,1)S(1)} %copy-done.32), channel_id=1, source_target_pairs={{0,2},{2,0},{4,6},{6,4},{1,3},{3,1},{5,7},{7,5},{8,10},{10,8},{12,... | collective-permute-start | bytes 1572872 | tf_op jit(solution)/shard_map/ppermute | solution.py:656
  (95 other events, 1901.8 us)

commit v2 on v1

--- a/solution.py
+++ b/solution.py
@@ -11,9 +11,10 @@
 CHUNK = 128
 KEYS = 256
 TILE = 512
+STRIP = 256
 HIDE = -1e30
 COSTS = (100, 15, 10, 5, 5)
-LIMITS = tuple(size * 2**20 for size in (6, 8, 12, 10))
+LIMITS = tuple(size * 2**20 for size in (7, 8, 11, 10))
 F32 = jnp.float32
 BF16 = jnp.bfloat16
 VMEM = pl.BlockSpec(memory_space=pltpu.VMEM)
@@ -21,6 +22,36 @@
 HBM = pl.BlockSpec(memory_space=pltpu.HBM)
 ANY = pl.BlockSpec(memory_space=pl.ANY)
 
+DMA = pltpu.SemaphoreType.DMA
+SCR = {
+    "af": lambda chunk, width, units, length: [
+        pltpu.VMEM((chunk, width), BF16), pltpu.VMEM((chunk, width), BF16),
+        pltpu.VMEM((chunk, width), BF16), pltpu.VMEM((chunk, width), F32),
+        pltpu.VMEM((128, chunk), F32), pltpu.VMEM((chunk, width), BF16),
+        pltpu.VMEM((chunk, length), F32), pltpu.VMEM((3, chunk, width), BF16), DMA((7,)),
+    ],
+    "ff": lambda chunk, width, units, length: [
+        pltpu.VMEM((chunk, width), BF16), pltpu.VMEM((chunk, units), F32),
+        pltpu.VMEM((chunk, units), BF16), pltpu.VMEM((chunk, units), BF16),
+        pltpu.VMEM((chunk, units), BF16), pltpu.VMEM((chunk, 128), F32), DMA((7,)),
+    ],
+    "fb": lambda chunk, width, units, length: [
+        pltpu.VMEM((chunk, units), BF16), pltpu.VMEM((chunk, units), BF16),
+        pltpu.VMEM((chunk, 128), F32), pltpu.VMEM((chunk, width), F32),
+        pltpu.VMEM((chunk, width), BF16), pltpu.VMEM((chunk, units), F32),
+        pltpu.VMEM((chunk, units), BF16), pltpu.VMEM((chunk, width), F32), DMA((4,)), DMA((2,)),
+    ],
+    "ab": lambda chunk, width, units, length: [
+        pltpu.VMEM((chunk, width), BF16), pltpu.VMEM((chunk, width), BF16),
+        pltpu.VMEM((chunk, width), F32), pltpu.VMEM((128, chunk), F32),
+        pltpu.VMEM((chunk, width), BF16), pltpu.VMEM((chunk, width), F32),
+        pltpu.VMEM((length, chunk), F32), pltpu.VMEM((chunk, width), BF16),
+        pltpu.VMEM((chunk, width), BF16), pltpu.VMEM((chunk, width), BF16),
+        pltpu.VMEM((chunk, width), BF16), pltpu.VMEM((chunk, width), F32),
+        DMA((4,)), DMA((6,)),
+    ],
+}
+
 
 def lasts(microseconds):
     flops = int(microseconds * 1.1e9)
@@ -83,46 +114,95 @@
     return [pltpu.make_async_copy(a, b, sems.at[i]) for i, (a, b) in enumerate(pairs)]
 
 
-def chunk_rows(place_ref, near_ref, far_ref, first, rows, into, sem):
-    half = far_ref.shape[0]
+def in_hbm(values):
+    return [pltpu.with_memory_space_constraint(value, pltpu.HBM) for value in values]
+
+
+def chunk_rows(place_ref, near_ref, far_ref, first, into, sem, step):
+    rows, half = into.shape[0], far_ref.shape[0]
     side = first // half
     inner = first - side * half
 
     @pl.when(side == place_ref[2])
     def _():
         at = pl.ds(pl.multiple_of(place_ref[3] + inner, rows), rows)
-        copy = pltpu.make_async_copy(near_ref.at[at], into, sem)
-        copy.start()
-        copy.wait()
+        getattr(pltpu.make_async_copy(near_ref.at[at], into, sem), step)()
 
     @pl.when(side != place_ref[2])
     def _():
         at = pl.ds(pl.multiple_of(inner, rows), rows)
-        copy = pltpu.make_async_copy(far_ref.at[at], into, sem)
-        copy.start()
-        copy.wait()
-
-
-def row_of(pair, first, size):
+        getattr(pltpu.make_async_copy(far_ref.at[at], into, sem), step)()
+
+
+def first_rows(place, near, far, first, rows, after):
+    def kernel(place_ref, near_ref, far_ref, after_ref, out_ref, sem):
+        del after_ref
+        for step in ("start", "wait"):
+            chunk_rows(place_ref, near_ref, far_ref, jnp.int32(first), out_ref, sem, step)
+
+    return pl.pallas_call(
+        kernel,
+        in_specs=[SMEM, HBM, HBM, ANY],
+        out_specs=VMEM,
+        out_shape=jax.ShapeDtypeStruct((rows, near.shape[1]), near.dtype),
+        scratch_shapes=[pltpu.SemaphoreType.DMA],
+        compiler_params=pltpu.CompilerParams(vmem_limit_bytes=2**20),
+    )(place, *in_hbm([near, far]), after)
+
+
+def last_rows(place, rows, chunk_of, count, keep, send):
+    size = rows.shape[0]
+
+    def kernel(place_ref, rows_ref, keep_in, send_in, keep_buf, send_buf, sem):
+        del keep_in, send_in
+        chunk = chunk_of(place_ref[0], place_ref[1] - 1)
+
+        @pl.when((chunk >= 0) & (chunk < count))
+        def _():
+            for step in ("start", "wait"):
+                store_rows(place_ref, keep_buf, send_buf, chunk * size, rows_ref, sem, step)
+
+    return pl.pallas_call(
+        kernel,
+        in_specs=[SMEM, VMEM, HBM, HBM],
+        out_specs=[HBM, HBM],
+        out_shape=[pltpu.HBM(keep.shape, keep.dtype), pltpu.HBM(send.shape, send.dtype)],
+        scratch_shapes=[pltpu.SemaphoreType.DMA],
+        input_output_aliases={2: 0, 3: 1},
+        compiler_params=pltpu.CompilerParams(vmem_limit_bytes=2**20),
+        cost_estimate=lasts(1),
+    )(place, rows, keep, send)
+
+
+def row_of(vec_ref, first, size):
     return jnp.concatenate(
-        [pair[0][:, first:first + size], pair[1][:, first:first + size]], axis=1
-    ).astype(F32)
+        [vec_ref[0, :, first:first + size], vec_ref[1, :, first:first + size]], axis=1
+    )
+
+
+def aligned(index, size):
+    return pl.ds(pl.multiple_of(index * size, size), size)
 
 
 def attend_kernel(
-    tick_ref, section_ref, starts_ref, near_ref, far_ref, inc_ref, wp_a, wp_b, wo_a, wo_b,
-    own_ref, other_ref, gain_ref, bias_ref, branch_ref,
-    k_in, v_in, x_in, h1_in, q_in, o_in, lse_in, post_in, mid_in,
-    k_ref, v_ref, x_buf, h1_buf, q_buf, o_buf, lse_buf, post_buf, mid_buf, mid_ref,
-    x_s, h1_s, q_s, o_s, lse_s, post_s, hide_s, sems,
+    tick_ref, section_ref, starts_ref, tok_ref, inc_ref, prev_ref, wp_ref, wo_ref,
+    vec_ref, gain_ref, bias_ref, branch_ref,
+    k_in, v_in, x_in, h1_in, q_in, o_in, lse_in, post_in, keep_in, send_in,
+    k_ref, v_ref, x_buf, h1_buf, q_buf, o_buf, lse_buf, post_buf, keep_buf, send_buf, mid_ref,
+    x_s, h1_s, q_s, o_s, lse_s, post_s, hide_s, qkv_s, sems,
 ):
-    del k_in, v_in, x_in, h1_in, q_in, o_in, lse_in, post_in, mid_in
+    del k_in, v_in, x_in, h1_in, q_in, o_in, lse_in, post_in, keep_in, send_in
     rows = mid_ref.shape[0]
     length, width = k_ref.shape
     half = width // 2
     section = section_ref[0]
     chunk = tick_ref[0] - 2 * section
     live = (chunk >= 0) & (chunk < length // rows)
+    state = (section_ref, keep_buf, send_buf, (chunk - 1) * rows, prev_ref, sems.at[6])
+
+    @pl.when((chunk >= 1) & (chunk <= length // rows))
+    def _():
+        store_rows(*state, "start")
 
     @pl.when(live)
     def _():
@@ -131,7 +211,7 @@
 
         @pl.when(section == 0)
         def _():
-            chunk_rows(section_ref, near_ref, far_ref, first, rows, x_s, sems.at[0])
+            x_s[...] = tok_ref[...]
 
         @pl.when(section != 0)
         def _():
@@ -144,20 +224,24 @@
             copy.start()
             sent.append(copy)
 
-        pair = (own_ref, other_ref)
         layer_in = x_s[...].astype(F32)
         send(x_s, x_buf.at[here])
         normed, _ = norm_parts(layer_in)
         h1 = (normed * gain_ref[0:1].astype(F32) + bias_ref[0:1].astype(F32)).astype(BF16)
         h1_s[...] = h1
         send(h1_s, h1_buf.at[here])
-        for side, weight in ((0, wp_a), (1, wp_b)):
-            at = slice(side * half, (side + 1) * half)
-            q = (dot_nn(h1, weight[0]) + pair[side][:, :half].astype(F32)).astype(BF16)
-            q_s[:, at] = q * jnp.asarray(0.125, BF16)
-            k_ref[here, at] = dot_nn(h1, weight[1]).astype(BF16)
-            value = dot_nn(h1, weight[2]) + pair[side][:, half:width].astype(F32)
-            v_ref[here, at] = value.astype(BF16)
+
+        def project(number, carry):
+            side, which = number // 3, number % 3
+            shift = vec_ref[side, :, aligned(which, half)]
+            value = dot_nn(h1_s[...], wp_ref[side, which]) + shift
+            qkv_s[which, :, aligned(side, half)] = value.astype(BF16)
+            return carry
+
+        lax.fori_loop(0, 6, project, 0, unroll=6)
+        q_s[...] = qkv_s[0] * jnp.asarray(0.125, BF16)
+        k_ref[here, :] = qkv_s[1]
+        v_ref[here, :] = qkv_s[2]
         send(q_s, q_buf.at[here])
 
         def attend(keys):
@@ -192,18 +276,25 @@
 
         send(o_s, o_buf.at[here])
         send(lse_s, lse_buf.at[chunk])
-        post_normed, _ = norm_parts(o_s[...] * row_of(pair, 2 * half, half))
-        post = post_normed * row_of(pair, 3 * half, half) + row_of(pair, 4 * half, half)
-        post = post.astype(BF16)
-        post_s[...] = post
+        post_normed, _ = norm_parts(o_s[...] * row_of(vec_ref, 3 * half, half))
+        post = post_normed * row_of(vec_ref, 4 * half, half) + row_of(vec_ref, 5 * half, half)
+        post_s[...] = post.astype(BF16)
         send(post_s, post_buf.at[here])
-        mid_ref[...] = (
-            x_s[...].astype(F32) + dot_nn(post[:, :half], wo_a[...])
-            + dot_nn(post[:, half:], wo_b[...]) + branch_ref[0:1].astype(F32)
-        )
-        send(mid_ref, mid_buf.at[here])
+
+        def mix(number, carry):
+            at = aligned(number, STRIP)
+            total = dot_nn(post_s[:, :half], wo_ref[0, :, at])
+            total += dot_nn(post_s[:, half:], wo_ref[1, :, at])
+            mid_ref[:, at] = x_s[:, at].astype(F32) + total + branch_ref[0:1, at].astype(F32)
+            return carry
+
+        lax.fori_loop(0, width // STRIP, mix, 0, unroll=4)
         for copy in sent:
             copy.wait()
+
+    @pl.when((chunk >= 1) & (chunk <= length // rows))
+    def _():
+        store_rows(*state, "wait")
 
 
 def gelu_parts(pre):
@@ -213,16 +304,18 @@
 
 
 def expand_kernel(
-    tick_ref, section_ref, mid_ref, we_a, we_b, wr_a, wr_b,
-    own_ref, other_ref, gain_ref, bias_ref, branch_ref,
-    h2_in, g_in, gp_in, m_in, st_in, keep_in, send_in,
-    h2_buf, g_buf, gp_buf, m_buf, st_buf, keep_buf, send_buf, out_ref,
+    tick_ref, section_ref, near_ref, far_ref, mid_ref, we_ref, wr_ref, vec_ref, gain_ref,
+    bias_ref, branch_ref,
+    h2_in, g_in, gp_in, m_in, st_in, mid_in,
+    h2_buf, g_buf, gp_buf, m_buf, st_buf, mid_buf, out_ref, next_ref,
     h2_s, gf_s, g_s, gp_s, m_s, st_s, sems,
 ):
-    del h2_in, g_in, gp_in, m_in, st_in, keep_in, send_in
+    del h2_in, g_in, gp_in, m_in, st_in, mid_in
     rows = mid_ref.shape[0]
-    half = we_a.shape[1]
+    width = mid_ref.shape[1]
+    half = we_ref.shape[2]
     units = 2 * half
+    tiles = half // TILE
     length = h2_buf.shape[0]
     chunk = tick_ref[0] - 2 * section_ref[0]
 
@@ -236,67 +329,84 @@
             copy.start()
             sent.append(copy)
 
+        send(mid_ref, mid_buf.at[here])
+        more = (section_ref[0] == 0) & (chunk + 1 < length // rows)
+        fetch = (section_ref, near_ref, far_ref, (chunk + 1) * rows, next_ref, sems.at[6])
+
+        @pl.when(more)
+        def _():
+            chunk_rows(*fetch, "start")
+
         def wide(tile, which):
-            ref = own_ref if tile * TILE < half else other_ref
-            first = 5 * mid_ref.shape[1] // 2 + which * half + tile * TILE % half
-            return ref[:, first:first + TILE].astype(F32)
+            first = 3 * width + which * half + tile % tiles * TILE
+            return vec_ref[tile // tiles, :, pl.ds(pl.multiple_of(first, TILE), TILE)]
 
         normed, _ = norm_parts(mid_ref[...])
         h2 = (normed * gain_ref[1:2].astype(F32) + bias_ref[1:2].astype(F32)).astype(BF16)
         h2_s[...] = h2
         send(h2_s, h2_buf.at[here])
-        total = jnp.zeros((rows, 1), F32)
-        for tile in range(units // TILE):
-            weight = we_a if tile * TILE < half else we_b
-            inner = tile * TILE % half
-            at = slice(tile * TILE, (tile + 1) * TILE)
-            pre = dot_nn(h2, weight[:, inner:inner + TILE]) + wide(tile, 0)
-            active, slope = gelu_parts(pre)
+        def expand(tile, total):
+            at = aligned(tile, TILE)
+            weight = we_ref[tile // tiles, :, aligned(tile % tiles, TILE)]
+            active, slope = gelu_parts(dot_nn(h2_s[...], weight) + wide(tile, 0))
             gf_s[:, at] = active
             g_s[:, at] = active.astype(BF16)
             gp_s[:, at] = slope.astype(BF16)
-            total += jnp.sum(active, axis=-1, keepdims=True)
+            return total + jnp.sum(active, axis=-1, keepdims=True)
+
+        nothing = jnp.zeros((rows, 1), F32)
+        mean = lax.fori_loop(0, 2 * tiles, expand, nothing, unroll=4) / units
         send(g_s, g_buf.at[here])
         send(gp_s, gp_buf.at[here])
-        mean = total / units
-        square = jnp.zeros((rows, 1), F32)
-        for tile in range(units // TILE):
-            centre = gf_s[:, tile * TILE:(tile + 1) * TILE] - mean
-            square += jnp.sum(centre * centre, axis=-1, keepdims=True)
-        inv_std = lax.rsqrt(square / units + EPSILON)
+
+        def spread(tile, total):
+            centre = gf_s[:, aligned(tile, TILE)] - mean
+            return total + jnp.sum(centre * centre, axis=-1, keepdims=True)
+
+        inv_std = lax.rsqrt(lax.fori_loop(0, 2 * tiles, spread, nothing, unroll=8) / units + EPSILON)
         lane = lax.broadcasted_iota(jnp.int32, (rows, 128), 1)
         st_s[...] = jnp.where(lane == 0, mean, inv_std)
         send(st_s, st_buf.at[here])
-        out = mid_ref[...] + branch_ref[1:2].astype(F32)
-        for tile in range(units // TILE):
-            weight = wr_a if tile * TILE < half else wr_b
-            inner = tile * TILE % half
-            at = slice(tile * TILE, (tile + 1) * TILE)
+
+        def normalise(tile, carry):
+            at = aligned(tile, TILE)
             active = (gf_s[:, at] - mean) * inv_std * wide(tile, 1) + wide(tile, 2)
-            active = active.astype(BF16)
-            m_s[:, at] = active
-            out += dot_nn(active, weight[inner:inner + TILE, :])
+            m_s[:, at] = active.astype(BF16)
+            return carry
+
+        lax.fori_loop(0, 2 * tiles, normalise, 0, unroll=4)
         send(m_s, m_buf.at[here])
-        out_ref[...] = out.astype(BF16)
-        state = (section_ref, keep_buf, send_buf, chunk * rows, out_ref, sems.at[5])
-        store_rows(*state, "start")
+
+        def reduce(number, carry):
+            at = aligned(number, STRIP)
+            total = dot_nn(m_s[:, :half], wr_ref[0, :, at])
+            total += dot_nn(m_s[:, half:], wr_ref[1, :, at])
+            total += mid_ref[:, at] + branch_ref[1:2, at].astype(F32)
+            out_ref[:, at] = total.astype(BF16)
+            return carry
+
+        lax.fori_loop(0, width // STRIP, reduce, 0, unroll=2)
         for copy in sent:
             copy.wait()
-        store_rows(*state, "wait")
+
+        @pl.when(more)
+        def _():
+            chunk_rows(*fetch, "wait")
 
 
 def expand_back_kernel(
-    tick_ref, section_ref, near_ref, far_ref, inc_ref, wr_a, wr_b, we_a, we_b,
-    own_ref, other_ref, gain_ref,
+    tick_ref, section_ref, cot_ref, inc_ref, wr_ref, we_ref, vec_ref, gain_ref,
     g_buf, gp_buf, st_buf, mid_buf,
-    sum_in, wsum_in, df_in, dur_in, dmr_in,
-    sum_ref, wsum_ref, df_buf, dur_buf, dmr_buf, dmid_ref,
-    g_s, gp_s, st_s, mid_s, df_s, z_s, dur_s, dmr_s, in_sems, out_sems,
+    sum_in, wsum_in, df_in, dur_in,
+    sum_ref, wsum_ref, df_buf, dur_buf, dmid_ref,
+    g_s, gp_s, st_s, mid_s, df_s, z_s, dur_s, dh_s, in_sems, out_sems,
 ):
-    del sum_in, wsum_in, df_in, dur_in, dmr_in
+    del sum_in, wsum_in, df_in, dur_in
     rows = dmid_ref.shape[0]
-    half = wr_a.shape[1]
+    width = dmid_ref.shape[1]
+    half = wr_ref.shape[2]
     units = 2 * half
+    tiles = half // TILE
     length = g_buf.shape[0]
     count = length // rows
     section = section_ref[0]
@@ -318,9 +428,7 @@
 
         @pl.when(section == last)
         def _():
-            chunk_rows(
-                section_ref, near_ref, far_ref, chunk * rows, rows, df_s, out_sems.at[0]
-            )
+            df_s[...] = cot_ref[...]
 
         @pl.when(section != last)
         def _():
@@ -334,45 +442,56 @@
             sent.append(copy)
 
         def gain_of(tile):
-            ref = own_ref if tile * TILE < half else other_ref
-            first = 5 * dmid_ref.shape[1] // 2 + half + tile * TILE % half
-            return ref[:, first:first + TILE].astype(F32)
+            first = 3 * width + half + tile % tiles * TILE
+            return vec_ref[tile // tiles, :, pl.ds(pl.multiple_of(first, TILE), TILE)]
 
         grad_low = df_s[...]
         send(df_s, df_buf.at[here])
         sum_ref[0:1] += column_sum(grad_low.astype(F32))
-        for copy in loads:
-            copy.wait()
+        loads[0].wait()
+        loads[2].wait()
         mean = st_s[:, 0:1]
         inv_std = st_s[:, 1:2]
-        one = jnp.zeros((rows, 1), F32)
-        two = jnp.zeros((rows, 1), F32)
-        for tile in range(units // TILE):
-            weight = wr_a if tile * TILE < half else wr_b
-            inner = tile * TILE % half
-            at = slice(tile * TILE, (tile + 1) * TILE)
-            grad = dot_nn(grad_low, weight[:, inner:inner + TILE])
+        def reduce_back(tile, sums):
+            at = aligned(tile, TILE)
+            weight = wr_ref[tile // tiles, :, aligned(tile % tiles, TILE)]
+            grad = dot_nn(df_s[...], weight)
             normed = (g_s[:, at].astype(F32) - mean) * inv_std
             wsum_ref[0:1, at] += column_sum(grad * normed)
             wsum_ref[1:2, at] += column_sum(grad)
             scaled = grad * gain_of(tile)
             z_s[:, at] = scaled
-            one += jnp.sum(scaled, axis=-1, keepdims=True)
-            two += jnp.sum(scaled * normed, axis=-1, keepdims=True)
+            return (
+                sums[0] + jnp.sum(scaled, axis=-1, keepdims=True),
+                sums[1] + jnp.sum(scaled * normed, axis=-1, keepdims=True),
+            )
+
+        nothing = jnp.zeros((rows, 1), F32)
+        one, two = lax.fori_loop(0, 2 * tiles, reduce_back, (nothing, nothing), unroll=4)
         one = one / units
         two = two / units
-        grad_second = jnp.zeros((rows, dmid_ref.shape[1]), F32)
-        for tile in range(units // TILE):
-            weight = we_a if tile * TILE < half else we_b
-            inner = tile * TILE % half
-            at = slice(tile * TILE, (tile + 1) * TILE)
+
+        def active_back(tile, carry):
+            at = aligned(tile, TILE)
             normed = (g_s[:, at].astype(F32) - mean) * inv_std
             grad = inv_std * (z_s[:, at] - one - normed * two) * gp_s[:, at].astype(F32)
             wsum_ref[2:3, at] += column_sum(grad)
-            low = grad.astype(BF16)
-            dur_s[:, at] = low
-            grad_second += dot_nn(low, weight[inner:inner + TILE, :])
+            dur_s[:, at] = grad.astype(BF16)
+            return carry
+
+        loads[1].wait()
+        lax.fori_loop(0, 2 * tiles, active_back, 0, unroll=8)
         send(dur_s, dur_buf.at[here])
+
+        def expand_back(number, carry):
+            at = aligned(number, STRIP)
+            total = dot_nn(dur_s[:, :half], we_ref[0, :, at])
+            dh_s[:, at] = total + dot_nn(dur_s[:, half:], we_ref[1, :, at])
+            return carry
+
+        lax.fori_loop(0, width // STRIP, expand_back, 0, unroll=4)
+        grad_second = dh_s[...]
+        loads[3].wait()
         normed, inv_std = norm_parts(mid_s[...])
         sum_ref[1:2] += column_sum(grad_second * normed)
         sum_ref[2:3] += column_sum(grad_second)
@@ -381,21 +500,21 @@
         )
         sum_ref[3:4] += column_sum(grad_mid)
         dmid_ref[...] = grad_mid
-        dmr_s[...] = grad_mid.astype(BF16)
-        send(dmr_s, dmr_buf.at[here])
         for copy in sent:
             copy.wait()
 
 
 def attend_back_kernel(
-    tick_ref, section_ref, starts_ref, after, dmid_ref, wo_a, wo_b, wp_a, wp_b,
-    own_ref, other_ref, gain_ref, k_ref, v_ref,
+    tick_ref, section_ref, starts_ref, after, near_ref, far_ref, prev_ref, dmid_ref, wo_ref,
+    wp_ref, vec_ref, gain_ref, k_ref, v_ref,
     x_buf, q_buf, o_buf, lse_buf,
-    sum_in, dk_in, dv_in, dq_in, dkr_in, dvr_in, keep_in, send_in,
-    sum_ref, dk_ref, dv_ref, dq_buf, dkr_buf, dvr_buf, keep_buf, send_buf, out_ref,
-    x_s, q_s, o_s, lse_s, do_s, dqf_s, hide_s, dq_s, dkr_s, dvr_s, in_sems, out_sems,
+    sum_in, dk_in, dv_in, dq_in, dkr_in, dvr_in, dmr_in, keep_in, send_in,
+    sum_ref, dk_ref, dv_ref, dq_buf, dkr_buf, dvr_buf, dmr_buf, keep_buf, send_buf, out_ref,
+    next_ref,
+    x_s, q_s, o_s, lse_s, do_s, dqf_s, hide_s, dq_s, dkr_s, dvr_s, low_s, wide_s, in_sems,
+    out_sems,
 ):
-    del after, sum_in, dk_in, dv_in, dq_in, dkr_in, dvr_in, keep_in, send_in
+    del after, sum_in, dk_in, dv_in, dq_in, dkr_in, dvr_in, dmr_in, keep_in, send_in
     rows = dmid_ref.shape[0]
     length, width = k_ref.shape
     half = width // 2
@@ -403,6 +522,12 @@
     section = section_ref[0]
     last = section_ref[1] - 1
     chunk = count - 1 - (tick_ref[0] - 2 * (last - section))
+
+    state = (section_ref, keep_buf, send_buf, (chunk + 1) * rows, prev_ref, out_sems.at[4])
+
+    @pl.when((chunk >= -1) & (chunk < count - 1))
+    def _():
+        store_rows(*state, "start")
 
     @pl.when((chunk >= 0) & (chunk < count))
     def _():
@@ -423,19 +548,41 @@
             dk_ref[...] = jnp.zeros_like(dk_ref)
             dv_ref[...] = jnp.zeros_like(dv_ref)
 
-        low = dmid_ref[...].astype(BF16)
-        grad_post = jnp.concatenate([dot_nn(low, wo_a[...]), dot_nn(low, wo_b[...])], axis=1)
-        for copy in loads:
-            copy.wait()
+        more = (section == last) & (chunk >= 1)
+        fetch = (section_ref, near_ref, far_ref, (chunk - 1) * rows, next_ref, out_sems.at[5])
+
+        @pl.when(more)
+        def _():
+            chunk_rows(*fetch, "start")
+
+        sent = []
+
+        def send(source, target):
+            copy = pltpu.make_async_copy(source, target, out_sems.at[len(sent)])
+            copy.start()
+            sent.append(copy)
+
+        low_s[...] = dmid_ref[...].astype(BF16)
+        send(low_s, dmr_buf.at[here])
+
+        def mix_back(side, carry):
+            wide_s[:, aligned(side, half)] = dot_nn(low_s[...], wo_ref[side])
+            return carry
+
+        lax.fori_loop(0, 2, mix_back, 0, unroll=2)
+        grad_post = wide_s[...]
+        loads[2].wait()
         attended = o_s[...]
-        pair_refs = (own_ref, other_ref)
-        scale = row_of(pair_refs, 2 * half, half)
+        scale = row_of(vec_ref, 3 * half, half)
         normed, inv_std = norm_parts(attended * scale)
         sum_ref[0:1] += column_sum(grad_post * normed)
         sum_ref[1:2] += column_sum(grad_post)
-        grad_mixed = norm_back(grad_post * row_of(pair_refs, 3 * half, half), normed, inv_std)
+        grad_mixed = norm_back(grad_post * row_of(vec_ref, 4 * half, half), normed, inv_std)
         sum_ref[2:3] += column_sum(grad_mixed * attended)
         do_s[...] = (grad_mixed * scale).astype(BF16)
+
+        loads[1].wait()
+        loads[3].wait()
 
         def attend(keys):
             place = first + lax.broadcasted_iota(jnp.int32, (1, rows), 1)
@@ -474,13 +621,6 @@
             def _():
                 attend((number + 1) * KEYS)
 
-        sent = []
-
-        def send(source, target):
-            copy = pltpu.make_async_copy(source, target, out_sems.at[len(sent)])
-            copy.start()
-            sent.append(copy)
-
         grad_query = dqf_s[...]
         grad_value = dv_ref[here, :]
         sum_ref[3:4] += column_sum(grad_query)
@@ -491,10 +631,19 @@
         send(dq_s, dq_buf.at[here])
         send(dkr_s, dkr_buf.at[here])
         send(dvr_s, dvr_buf.at[here])
-        grad_first = jnp.zeros((rows, width), F32)
-        for number, part in enumerate((dq_s, dkr_s, dvr_s)):
-            grad_first += dot_nn(part[:, :half], wp_a[number])
-            grad_first += dot_nn(part[:, half:], wp_b[number])
+
+        def project_back(number, carry):
+            at = aligned(number, STRIP)
+            total = jnp.zeros((rows, STRIP), F32)
+            for which, part in enumerate((dq_s, dkr_s, dvr_s)):
+                total += dot_nn(part[:, :half], wp_ref[0, which, :, at])
+                total += dot_nn(part[:, half:], wp_ref[1, which, :, at])
+            wide_s[:, at] = total
+            return carry
+
+        lax.fori_loop(0, width // STRIP, project_back, 0, unroll=4)
+        grad_first = wide_s[...]
+        loads[0].wait()
         normed, inv_std = norm_parts(x_s[...].astype(F32))
         sum_ref[5:6] += column_sum(grad_first * normed)
         sum_ref[6:7] += column_sum(grad_first)
@@ -502,57 +651,71 @@
             grad_first * gain_ref[0:1].astype(F32), normed, inv_std
         )
         out_ref[...] = out.astype(BF16)
-        state = (section_ref, keep_buf, send_buf, first, out_ref, out_sems.at[3])
-        store_rows(*state, "start")
         for copy in sent:
             copy.wait()
+
+        @pl.when(more)
+        def _():
+            chunk_rows(*fetch, "wait")
+
+    @pl.when((chunk >= -1) & (chunk < count - 1))
+    def _():
         store_rows(*state, "wait")
 
 
-def flip_kernel(first, second, after, first_out, second_out):
+def flip_kernel(source, after, target):
     del after
     size = 256
-    for source, target in ((first, first_out), (second, second_out)):
-        numbers = range(source.shape[0]) if len(source.shape) == 3 else (None,)
-        for number in numbers:
-            one = source if number is None else source.at[number]
-            two = target if number is None else target.at[number]
-
-            def body(step, carry, one=one, two=two):
-                at = pl.ds(pl.multiple_of(step * size, size), size)
-                two[:, at] = one[at, :].T
-                return carry
-
-            lax.fori_loop(0, one.shape[0] // size, body, 0)
-
-
-def flipped(first, second, after):
-    shape = first.shape[:-2] + (first.shape[-1], first.shape[-2])
+
+    def flip(one, two):
+        def body(step, carry):
+            at = aligned(step, size)
+            two[:, at] = one[at, :].T
+            return carry
+
+        lax.fori_loop(0, one.shape[0] // size, body, 0)
+
+    def each(index, carry):
+        if len(source.shape) == 3:
+            flip(source.at[index], target.at[index])
+        else:
+            deep = source.shape[1]
+            flip(source.at[index // deep, index % deep], target.at[index // deep, index % deep])
+        return carry
+
+    count = source.shape[0] * (source.shape[1] if len(source.shape) == 4 else 1)
+    lax.fori_loop(0, count, each, 0)
+
+
+def flipped(weight, after):
+    shape = weight.shape[:-2] + (weight.shape[-1], weight.shape[-2])
     return pl.pallas_call(
         flip_kernel,
-        in_specs=[VMEM] * 2 + [ANY],
-        out_specs=[VMEM] * 2,
-        out_shape=[pltpu.VMEM(shape, BF16)] * 2,
+        in_specs=[VMEM, ANY],
+        out_specs=VMEM,
+        out_shape=pltpu.VMEM(shape, BF16),
         compiler_params=pltpu.CompilerParams(vmem_limit_bytes=2 * 2**20),
-    )(first, second, after)
-
-
-def load_kernel(source, after, target, sem):
+    )(weight, after)
+
+
+def load_kernel(side, source, after, *refs):
     del after
-    copy = pltpu.make_async_copy(source, target, sem)
+    copy = pltpu.make_async_copy(source, refs[-2].at[side], refs[-1])
     copy.start()
     copy.wait()
 
 
-def loaded(value, after):
+def loaded(side, value, both, after):
+    known = [] if both is None else [both]
     return pl.pallas_call(
-        load_kernel,
-        in_specs=[HBM, ANY],
+        partial(load_kernel, side),
+        in_specs=[HBM, ANY] + [VMEM] * len(known),
         out_specs=VMEM,
-        out_shape=pltpu.VMEM(value.shape, value.dtype),
+        out_shape=pltpu.VMEM((2, *value.shape), value.dtype),
         scratch_shapes=[pltpu.SemaphoreType.DMA],
+        input_output_aliases={2: 0} if known else {},
         compiler_params=pltpu.CompilerParams(vmem_limit_bytes=2**20),
-    )(pltpu.with_memory_space_constraint(value, pltpu.HBM), after)
+    )(*in_hbm([value]), after, *known)
 
 
 def empty_kernel(*refs):
@@ -646,7 +809,7 @@
             pltpu.VMEM((2, rows, columns), F32), pltpu.VMEM(turn, F32),
             pltpu.SemaphoreType.DMA((2, 4)),
         ],
-        compiler_params=pltpu.CompilerParams(vmem_limit_bytes=14 * 2**20),
+        compiler_params=pltpu.CompilerParams(vmem_limit_bytes=12 * 2**20),
         cost_estimate=lasts(cost),
     )(place, *pieces, *in_hbm([after]))
 
@@ -654,10 +817,6 @@
 def crossed(value, bit):
     route = [(i, i ^ bit) for i in range(lax.axis_size("batch"))]
     return lax.ppermute(value, "batch", route)
-
-
-def in_hbm(values):
-    return [pltpu.with_memory_space_constraint(value, pltpu.HBM) for value in values]
 
 
 def product(lefts, rights, pairs, columns, number):
@@ -689,7 +848,7 @@
         + [HBM],
         out_specs=pl.BlockSpec((tile, columns * len(rights)), lambda i: (i, 0)),
         out_shape=pltpu.HBM((rows, columns * len(rights)), BF16),
-        compiler_params=pltpu.CompilerParams(vmem_limit_bytes=14 * 2**20),
+        compiler_params=pltpu.CompilerParams(vmem_limit_bytes=12 * 2**20),
         cost_estimate=lasts(cost),
     )(*in_hbm(lefts), *in_hbm(rights), *in_hbm([after]))
 
@@ -707,17 +866,37 @@
 
     def kernel(place_ref, *refs):
         del place_ref
-        come_ref, outs = refs[len(lefts) + len(rights)], refs[-4:]
+        come_ref = refs[len(lefts) + len(rights)]
+        *outs, low_s, sems = refs[-6:]
+        step = pl.program_id(0)
+        slot = step % 2
+
+        def store(number):
+            return pltpu.make_async_copy(
+                low_s.at[number % 2], outs[number], sems.at[number % 2]
+            )
+
+        for number in (2, 3):
+
+            @pl.when(step == number)
+            def _():
+                store(number - 2).wait()
+
         for number in range(len(rights)):
             where, value = product(
                 refs[:len(lefts)], refs[len(lefts):], pairs, columns, number
             )
-            low = (value + come_ref[:, where].astype(F32)).astype(BF16)
-            for step, out in enumerate(outs):
-
-                @pl.when(pl.program_id(0) == step)
-                def _():
-                    out[:, where] = low
+            low_s[slot, :, where] = (value + come_ref[:, where].astype(F32)).astype(BF16)
+        for number in range(4):
+
+            @pl.when(step == number)
+            def _():
+                store(number).start()
+
+        @pl.when(step == 3)
+        def _():
+            store(2).wait()
+            store(3).wait()
 
     return pl.pallas_call(
         kernel,
@@ -733,10 +912,13 @@
             ]
             * len(rights)
             + [pl.BlockSpec((tile, whole), lambda i, place: (at(i, place), 0)), HBM],
-            out_specs=[pl.BlockSpec((tile, whole), lambda i, place: (0, 0))] * 4,
+            out_specs=[HBM] * 4,
+            scratch_shapes=[
+                pltpu.VMEM((2, tile, whole), BF16), pltpu.SemaphoreType.DMA((2,))
+            ],
         ),
         out_shape=[pltpu.HBM((tile, whole), BF16)] * 4,
-        compiler_params=pltpu.CompilerParams(vmem_limit_bytes=20 * 2**20),
+        compiler_params=pltpu.CompilerParams(vmem_limit_bytes=12 * 2**20),
         cost_estimate=lasts(cost),
     )(place, *in_hbm(lefts), *in_hbm(rights), come, *in_hbm([after]))
 
@@ -913,7 +1095,8 @@
     ).astype(jnp.int32)
     starts = lax.dynamic_index_in_dim(document_starts[0], block, 0, keepdims=False)[0]
     fields = (
-        project_bias[0, 0], project_bias[0, 1], jnp.repeat(head_scale[0], head), post_gain[0],
+        project_bias[0, 0], jnp.zeros_like(project_bias[0, 0]), project_bias[0, 1],
+        jnp.repeat(head_scale[0], head), post_gain[0],
         post_bias[0], expand_bias[0], middle_gain[0], middle_bias[0],
     )
     if paired:
@@ -928,14 +1111,16 @@
     wo_a, wo_b = both(output_weight[0], 0)
     we_a, we_b = both(expand_weight[0], 1)
     wr_a, wr_b = both(reduce_weight[0], 0)
-    wp_a = loaded(wp_a, place)
-    wo_a = loaded(wo_a, wp_a)
-    we_a = loaded(we_a, wo_a)
-    wr_a = loaded(wr_a, we_a)
-    wp_b = loaded(wp_b, wr_a)
-    wo_b = loaded(wo_b, wp_b)
-    we_b = loaded(we_b, wo_b)
-    wr_b = loaded(wr_b, we_b)
+    wp = loaded(0, wp_a, None, place)
+    wo = loaded(0, wo_a, None, wp)
+    we = loaded(0, we_a, None, wo)
+    wr = loaded(0, wr_a, None, we)
+    wr_own = wr
+    wp = loaded(1, wp_b, wp, wr)
+    wo = loaded(1, wo_b, wo, wp)
+    we = loaded(1, we_b, we, wo)
+    wr = loaded(1, wr_b, wr, we)
+    vectors = jnp.stack([own, other]).astype(F32)
     near_cotangent, far_cotangent = row_source(cotangent[0])
 
     def sized(columns, dtype):
@@ -960,7 +1145,6 @@
     )
     k_all = jnp.zeros((length, width), BF16)
     v_all = jnp.zeros((length, width), BF16)
-    dma = pltpu.SemaphoreType.DMA
     dense = 2 * chunk * width
 
     def shifted(value, distance):
@@ -971,56 +1155,50 @@
     blank = jnp.zeros((chunk, width), BF16)
     incoming = blank
     sent = None
+    rows_in = first_rows(place, near_tokens, far_tokens, 0, chunk, wr_own)
     for tick in range(ticks):
         now = jnp.full((1,), tick, jnp.int32)
         arriving = shifted(sent, 1) if sent is not None and tick + 1 < ticks else blank
         (
-            k_all, v_all, x_buf, h1_buf, q_buf, o_buf, lse_buf, post_buf, mid_buf, middle,
+            k_all, v_all, x_buf, h1_buf, q_buf, o_buf, lse_buf, post_buf, hid_keep, hid_send,
+            middle,
         ) = call(
             attend_kernel,
             (
-                now, place, starts, near_tokens, far_tokens, incoming, wp_a, wp_b, wo_a, wo_b,
-                own, other, gains, biases, branches,
+                now, place, starts, rows_in, incoming, blank if sent is None else sent, wp, wo,
+                vectors, gains, biases, branches,
             ),
-            [SMEM, SMEM, SMEM, HBM, HBM] + [VMEM] * 10,
-            (k_all, v_all, x_buf, h1_buf, q_buf, o_buf, lse_buf, post_buf, mid_buf),
-            [VMEM, VMEM] + [HBM] * 7,
+            [SMEM] * 3 + [VMEM] * 9,
+            (
+                k_all, v_all, x_buf, h1_buf, q_buf, o_buf, lse_buf, post_buf, hid_keep, hid_send,
+            ),
+            [VMEM, VMEM] + [HBM] * 8,
             [jax.ShapeDtypeStruct((chunk, width), F32)],
             [VMEM],
-            [
-                pltpu.VMEM((chunk, width), BF16), pltpu.VMEM((chunk, width), BF16),
-                pltpu.VMEM((chunk, width), BF16), pltpu.VMEM((chunk, width), F32),
-                pltpu.VMEM((128, chunk), F32), pltpu.VMEM((chunk, width), BF16),
-                pltpu.VMEM((chunk, length), F32), dma((7,)),
-            ],
+            SCR["af"](chunk, width, units, length),
             LIMITS[0],
             8 * dense * width,
         )
-        h2_buf, g_buf, gp_buf, m_buf, st_buf, hid_keep, hid_send, sent = call(
+        h2_buf, g_buf, gp_buf, m_buf, st_buf, mid_buf, sent, rows_in = call(
             expand_kernel,
-            (
-                now, place, middle, we_a, we_b, wr_a, wr_b, own, other, gains, biases, branches,
-            ),
-            [SMEM, SMEM] + [VMEM] * 10,
-            (h2_buf, g_buf, gp_buf, m_buf, st_buf, hid_keep, hid_send),
-            [HBM] * 7,
-            [jax.ShapeDtypeStruct((chunk, width), BF16)],
-            [VMEM],
-            [
-                pltpu.VMEM((chunk, width), BF16), pltpu.VMEM((chunk, units), F32),
-                pltpu.VMEM((chunk, units), BF16), pltpu.VMEM((chunk, units), BF16),
-                pltpu.VMEM((chunk, units), BF16), pltpu.VMEM((chunk, 128), F32), dma((6,)),
-            ],
+            (now, place, near_tokens, far_tokens, middle, we, wr, vectors, gains, biases, branches),
+            [SMEM, SMEM, HBM, HBM] + [VMEM] * 7,
+            (h2_buf, g_buf, gp_buf, m_buf, st_buf, mid_buf),
+            [HBM] * 6,
+            [jax.ShapeDtypeStruct((chunk, width), BF16)] * 2,
+            [VMEM] * 2,
+            SCR["ff"](chunk, width, units, length),
             LIMITS[1],
             2 * dense * units,
         )
         incoming = arriving
 
-    wrt_a, wrt_b = flipped(wr_a, wr_b, sent)
-    wet_a, wet_b = flipped(we_a, we_b, wrt_a)
-    wot_a, wot_b = flipped(wo_a, wo_b, wet_a)
-    wpt_a, wpt_b = flipped(wp_a, wp_b, wot_a)
-    dk_acc, dv_acc = empty([sized(width, F32)] * 2, pltpu.VMEM, wpt_a)
+    last_out = sent
+    wrt = flipped(wr, sent)
+    wet = flipped(we, wrt)
+    wot = flipped(wo, wet)
+    wpt = flipped(wp, wot)
+    dk_acc, dv_acc = empty([sized(width, F32)] * 2, pltpu.VMEM, wpt)
     sum_f = jnp.zeros((4, width), F32)
     sum_w = jnp.zeros((3, units), F32)
     sum_a = jnp.zeros((7, width), F32)
@@ -1032,61 +1210,51 @@
         total = lax.psum_scatter(full, "mp", scatter_dimension=axis, tiled=True)
         return (total.astype(F32) * copies).astype(BF16)
 
-    def attend_back(now, after, grad_mid, carried, cost=10):
+    def attend_back(now, after, prev, grad_mid, carried, cost=10):
         return call(
             attend_back_kernel,
             (
-                now, place, starts, after, grad_mid, wot_a, wot_b, wpt_a, wpt_b, own, other, gains,
-                k_all, v_all, x_buf, q_buf, o_buf, lse_buf,
+                now, place, starts, after, near_cotangent, far_cotangent, prev, grad_mid, wot,
+                wpt, vectors, gains, k_all, v_all, x_buf, q_buf, o_buf, lse_buf,
             ),
-            [SMEM, SMEM, SMEM, HBM] + [VMEM] * 10 + [HBM] * 4,
+            [SMEM, SMEM, SMEM, HBM, HBM, HBM] + [VMEM] * 8 + [HBM] * 4,
             carried,
-            [VMEM, VMEM, VMEM] + [HBM] * 5,
-            [jax.ShapeDtypeStruct((chunk, width), BF16)],
-            [VMEM],
-            [
-                pltpu.VMEM((chunk, width), BF16), pltpu.VMEM((chunk, width), BF16),
-                pltpu.VMEM((chunk, width), F32), pltpu.VMEM((128, chunk), F32),
-                pltpu.VMEM((chunk, width), BF16), pltpu.VMEM((chunk, width), F32),
-                pltpu.VMEM((length, chunk), F32), pltpu.VMEM((chunk, width), BF16),
-                pltpu.VMEM((chunk, width), BF16), pltpu.VMEM((chunk, width), BF16),
-                dma((4,)), dma((4,)),
-            ],
+            [VMEM, VMEM, VMEM] + [HBM] * 6,
+            [jax.ShapeDtypeStruct((chunk, width), BF16)] * 2,
+            [VMEM] * 2,
+            SCR["ab"](chunk, width, units, length),
             LIMITS[3],
             cost * 11 * 10**8,
         )
 
     held = []
-    carried = (sum_a, dk_acc, dv_acc, dq_buf, dkr_buf, dvr_buf, ig_keep, ig_send)
+    carried = (sum_a, dk_acc, dv_acc, dq_buf, dkr_buf, dvr_buf, dmr_buf, ig_keep, ig_send)
+    rows_in = first_rows(place, near_cotangent, far_cotangent, length - chunk, chunk, wpt)
     for tick in range(ticks):
         now = jnp.full((1,), tick, jnp.int32)
         arriving = shifted(sent, -1) if sent is not None and tick + 1 < ticks else blank
-        sum_f, sum_w, df_buf, dur_buf, dmr_buf, grad_mid = call(
+        sum_f, sum_w, df_buf, dur_buf, grad_mid = call(
             expand_back_kernel,
             (
-                now, place, near_cotangent, far_cotangent, incoming, wrt_a, wrt_b, wet_a, wet_b,
-                own, other, gains, g_buf, gp_buf, st_buf, mid_buf,
+                now, place, rows_in, incoming, wrt, wet, vectors, gains, g_buf, gp_buf, st_buf,
+                mid_buf,
             ),
-            [SMEM, SMEM, HBM, HBM] + [VMEM] * 8 + [HBM] * 4,
-            (sum_f, sum_w, df_buf, dur_buf, dmr_buf),
-            [VMEM, VMEM] + [HBM] * 3,
+            [SMEM, SMEM] + [VMEM] * 6 + [HBM] * 4,
+            (sum_f, sum_w, df_buf, dur_buf),
+            [VMEM, VMEM] + [HBM] * 2,
             [jax.ShapeDtypeStruct((chunk, width), F32)],
             [VMEM],
-            [
-                pltpu.VMEM((chunk, units), BF16), pltpu.VMEM((chunk, units), BF16),
-                pltpu.VMEM((chunk, 128), F32), pltpu.VMEM((chunk, width), F32),
-                pltpu.VMEM((chunk, width), BF16), pltpu.VMEM((chunk, units), F32),
-                pltpu.VMEM((chunk, units), BF16), pltpu.VMEM((chunk, width), BF16),
-                dma((4,)), dma((3,)),
-            ],
+            SCR["fb"](chunk, width, units, length),
             LIMITS[2],
             2 * dense * units,
         )
         held.append((now, grad_mid))
         if tick + 2 < ticks:
             held.clear()
-            *carried, sent = attend_back(now, x_buf, grad_mid, carried)
+            prev = blank if sent is None else sent
+            *carried, sent, rows_in = attend_back(now, x_buf, prev, grad_mid, carried)
         incoming = arriving
+
     def gathered(sum_a):
         shared = jnp.stack([sum_a[5], sum_f[1], sum_a[6], sum_f[2], sum_f[3], sum_f[0]])
         narrow = jnp.stack([sum_a[3], sum_a[4], sum_a[2], sum_a[0], sum_a[1]])
@@ -1103,6 +1271,15 @@
                 broad[:, side * wide_cut:(side + 1) * wide_cut].reshape(-1),
             ]
         )
+
+    def forward_chunk(section, last):
+        return ticks - 1 - 2 * section
+
+    def backward_chunk(section, last):
+        return count - 1 - (ticks - 1 - 2 * (last - section))
+
+    def finished(rows, chunk_of, keep, send):
+        return last_rows(place, rows, chunk_of, count, keep, send)
 
     if by_links:
         reduce_sides = (m_buf,), (df_buf,), (0,)
@@ -1115,22 +1292,24 @@
         expand_sum = BatchSum(pieces, place)
         after = pieces[3]
         for number, (now, grad_mid) in enumerate(held):
-            *carried, sent = attend_back(now, after, grad_mid, carried, 1)
+            *carried, sent, _ = attend_back(now, after, sent, grad_mid, carried, 1)
             after = reduce_sum.second(carried[-1], 1) if number == 0 else carried[-1]
-        sum_a, _, _, dq_buf, dkr_buf, dvr_buf, ig_keep, ig_send = carried
+        sum_a, _, _, dq_buf, dkr_buf, dvr_buf, dmr_buf, ig_keep, ig_send = carried
         mixed_sides = (h1_buf, dmr_buf), (dq_buf, dkr_buf, dvr_buf, post_buf), (0, 0, 0, 1)
         mixed_other = other_part(*mixed_sides, 1, after)
         after = expand_sum.second(mixed_other, COSTS[0])
         pieces = own_part(*mixed_sides, swapped(mixed_other), place, after)
         mixed_sum = BatchSum(pieces, place)
         after = reduce_sum.third(pieces[3], COSTS[1])
-        after = hidden = spread_rows(hid_keep, hid_send, after)
+        kept = finished(last_out, forward_chunk, hid_keep, hid_send)
+        after = hidden = spread_rows(*kept, after)
         small_one, small_two = (packed(side, sum_a).reshape(-1, 128) for side in (0, 1))
         small = plus(small_one, swapped(small_two), after)
         after = mixed_sum.second(after, COSTS[2])
         after = expand_sum.third(after, COSTS[3])
         after = mixed_sum.third(after, COSTS[4])
-        input_gradient = spread_rows(ig_keep, ig_send, after)
+        kept = finished(sent, backward_chunk, ig_keep, ig_send)
+        input_gradient = spread_rows(*kept, after)
         small = plus(small, crossed(small, 1), input_gradient)
         (reduce_grad,) = reduce_sum.result((reduce_weight.shape[1:],), input_gradient)
         small = plus(small, crossed(small, 2), reduce_grad)
@@ -1141,10 +1320,12 @@
         project_grad = project_grad[None]
     else:
         for now, grad_mid in held:
-            *carried, sent = attend_back(now, x_buf, grad_mid, carried)
-        sum_a, _, _, dq_buf, dkr_buf, dvr_buf, ig_keep, ig_send = carried
-        hidden = spread_rows(hid_keep, hid_send, sent)
-        input_gradient = spread_rows(ig_keep, ig_send, sent)
+            *carried, sent, _ = attend_back(now, x_buf, sent, grad_mid, carried)
+        sum_a, _, _, dq_buf, dkr_buf, dvr_buf, dmr_buf, ig_keep, ig_send = carried
+        kept = finished(last_out, forward_chunk, hid_keep, hid_send)
+        hidden = spread_rows(*kept, sent)
+        kept = finished(sent, backward_chunk, ig_keep, ig_send)
+        input_gradient = spread_rows(*kept, sent)
         reduce_grad, expand_grad, output_grad, *project_grad = (
             total.astype(F32)
             for total in lax.psum(

time: 772 us -> 734 us (0.951)
  Pallas kernels: 464 us -> 398 us
  local copies, waits for them, and re-layouts: 28.6 us -> 41.7 us
    pallas_call x56, Pallas kernels: 343 us -> 277 us  [call(): pl.pallas_call(kernel, in_specs=specs + carried_specs, out_specs=carried_...]
    unnamed x123 -> x190, local copies, waits for them, and re-layouts: 20.3 us -> 33.2 us
    ppermute x24, waiting for transfers between devices: 72.6 us -> 84.7 us  [shifted(): return lax.ppermute(value, 'section', route)]
    ppermute x24, starting transfers between devices: 47.9 us -> 56.3 us  [shifted(): return lax.ppermute(value, 'section', route)]
    ppermute x13, waiting for transfers between devices: 11.4 us -> 2.96 us  [swapped(): return lax.ppermute(value, 'mp', [(0, 1), (1, 0)])]
    pallas_call x12 -> x16, Pallas kernels: 24.9 us -> 30 us  [the longest x8 15.1 us: loaded(): pl.pallas_call(partial(load_kernel, side), in_specs=[HBM, ANY] + [VMEM] *...]
  transfers between devices with their start and end apart: 69 -> 69, of which waited for: 23 -> 21; matrix products, arithmetic and copies ran while one was open for 1% -> 2% of each run, Pallas kernels for 57% -> 51%
where the time goes in v2:
time: 734 us; the launch traced here: 722 us
  Pallas kernels  398 us (54%)
  waiting for transfers between devices  181 us (25%)
  starting transfers between devices  93.5 us (13%)
  local copies, waits for them, and re-layouts  41.7 us (6%)
    pallas_call x56, Pallas kernels, call(): pl.pallas_call(kernel, in_specs=specs + carried_specs, out_specs=carried_...  277 us
    ppermute x32, waiting for transfers between devices, crossed(): return lax.ppermute(value, 'batch', route)  93.4 us
    ppermute x24, waiting for transfers between devices, shifted(): return lax.ppermute(value, 'section', route)  84.7 us
    ppermute x24, starting transfers between devices, shifted(): return lax.ppermute(value, 'section', route)  56.3 us
    ppermute x32, starting transfers between devices, crossed(): return lax.ppermute(value, 'batch', route)  33.8 us
    unnamed x190, local copies, waits for them, and re-layouts  33.2 us
    pallas_call x3, Pallas kernels, own_part(): pl.pallas_call(kernel, grid_spec=pltpu.PrefetchScalarGridSpec(num_scalar_...  28.8 us
    pallas_call x3, Pallas kernels, other_part(): pl.pallas_call(kernel, grid=(rows // tile,), in_specs=[pl.BlockSpec((leng...  26.3 us
  transfers between devices with their start and end apart: 69, of which 21 were waited for; matrix products, arithmetic and copies ran while one was open for 2% of the time, Pallas kernels for 51%

profile of v2, /device:TPU:0, one launch (start us, length us, event | category | flops | bytes accessed | tf_op | source)
XLA Modules:
  0.0 721.7 jit_solution(2903074610704033638)
XLA Ops:
  88.4 8.2 %shard_map.306 = (bf16[1024,1024]{1,0:T(8,128)(2,1)S(1)}, bf16[1024,1024]{1,0:T(8,128)(2,1)S(1)}, bf16[1024,1024]{1,0:T(8,128)(2,1)}, bf16[1024,1024]{1,0:T(8,12...) custom-call(s32[1]{0:T(128)} %constant.74.clone.1.tick_ref, ...), custom_call_target="tpu_custom_call", output_to_operand_aliasing={{0}: (12, {}), {1}: (13, {}), {2}: (14, {}), {3}: (15, {}),... | custom-call | flops 2147483648 | bytes 4194304 | tf_op jit(solution)/shard_map/pallas_call | solution.py:745
  103.5 8.6 %shard_map.308 = (bf16[1024,1024]{1,0:T(8,128)(2,1)S(1)}, bf16[1024,1024]{1,0:T(8,128)(2,1)S(1)}, bf16[1024,1024]{1,0:T(8,128)(2,1)}, bf16[1024,1024]{1,0:T(8,12...) custom-call(s32[1]{0:T(128)} %constant.90.clone.1.tick_ref, ...), custom_call_target="tpu_custom_call", output_to_operand_aliasing={{0}: (12, {}), {1}: (13, {}), {2}: (14, {}), {3}: (15, {}),... | custom-call | flops 2147483648 | bytes 4194304 | tf_op jit(solution)/shard_map/pallas_call | solution.py:745
  119.0 8.6 %shard_map.310 = (bf16[1024,1024]{1,0:T(8,128)(2,1)S(1)}, bf16[1024,1024]{1,0:T(8,128)(2,1)S(1)}, bf16[1024,1024]{1,0:T(8,128)(2,1)}, bf16[1024,1024]{1,0:T(8,12...) custom-call(s32[1]{0:T(128)} %constant.89.clone.1.tick_ref, ...), custom_call_target="tpu_custom_call", output_to_operand_aliasing={{0}: (12, {}), {1}: (13, {}), {2}: (14, {}), {3}: (15, {}),... | custom-call | flops 2147483648 | bytes 4194304 | tf_op jit(solution)/shard_map/pallas_call | solution.py:745
  134.6 8.8 %shard_map.312 = (bf16[1024,1024]{1,0:T(8,128)(2,1)S(1)}, bf16[1024,1024]{1,0:T(8,128)(2,1)S(1)}, bf16[1024,1024]{1,0:T(8,128)(2,1)}, bf16[1024,1024]{1,0:T(8,12...) custom-call(s32[1]{0:T(128)} %constant.88.clone.1.tick_ref, ...), custom_call_target="tpu_custom_call", output_to_operand_aliasing={{0}: (12, {}), {1}: (13, {}), {2}: (14, {}), {3}: (15, {}),... | custom-call | flops 2147483648 | bytes 4194304 | tf_op jit(solution)/shard_map/pallas_call | solution.py:745
  152.3 8.4 %collective-permute-start.14 = (bf16[128,1024]{1,0:T(8,128)(2,1)S(1)}, bf16[128,1024]{1,0:T(8,128)(2,1)S(1)}, u32[]{:S(2)}, u32[]{:S(2)}) collective-permute-start(bf16[128,1024]{1,0:T(8,128)(2,1)S(1)} %get-tuple-element.729.prev_ref), channel_id=1, source_target_pairs={{0,8},{8,16},{16,24},{1,9},{9,17},{17,25},{2,10},{10,18},{18,26},{... | collective-permute-start | bytes 786440 | tf_op jit(solution)/shard_map/ppermute | solution.py:1152
  162.4 14.8 %collective-permute-start.15 = (bf16[128,1024]{1,0:T(8,128)(2,1)S(1)}, bf16[128,1024]{1,0:T(8,128)(2,1)S(1)}, u32[]{:S(2)}, u32[]{:S(2)}) collective-permute-start(bf16[128,1024]{1,0:T(8,128)(2,1)S(1)} %get-tuple-element.748.prev_ref), channel_id=1, source_target_pairs={{0,8},{8,16},{16,24},{1,9},{9,17},{17,25},{2,10},{10,18},{18,26},{... | collective-permute-start | bytes 786440 | tf_op jit(solution)/shard_map/ppermute | solution.py:1152
  216.4 17.1 %collective-permute-done.20.inc_ref = bf16[128,1024]{1,0:T(8,128)(2,1)S(1)} collective-permute-done((bf16[128,1024]{1,0:T(8,128)(2,1)S(1)}, bf16[128,1024]{1,0:T(8,128)(2,1)S(1)}, u32[]{:S(2)}, u32[]{:S(2)}) %collective-permute-start.20) | collective-permute-done | bytes 262176 | tf_op jit(solution)/shard_map/ppermute | solution.py:1152
  253.2 10.5 %shard_map.343 = (f32[4,1024]{1,0:T(4,128)S(1)}, f32[3,4096]{1,0:T(4,128)S(1)}, bf16[1024,1024]{1,0:T(8,128)(2,1)}, bf16[1024,4096]{1,0:T(8,128)(2,1)}, f32[128,1024]{1,0:T(8,128)S(1)}) custom-call(s32[1]{0:T(128)} %constant.90.clone.1.tick_ref, ...), custom_call_target="tpu_custom_call", output_to_operand_aliasing={{0}: (12, {}), {1}: (13, {}), {2}: (14, {}), {3}: (15, {})} | custom-call | flops 2147483648 | bytes 4194304 | tf_op jit(solution)/shard_map/pallas_call | solution.py:745
  265.8 43.9 %collective-permute-done.24.inc_ref = bf16[128,1024]{1,0:T(8,128)(2,1)S(1)} collective-permute-done((bf16[128,1024]{1,0:T(8,128)(2,1)S(1)}, bf16[128,1024]{1,0:T(8,128)(2,1)S(1)}, u32[]{:S(2)}, u32[]{:S(2)}) %collective-permute-start.24) | collective-permute-done | bytes 262176 | tf_op jit(solution)/shard_map/ppermute | solution.py:1152
  316.7 11.3 %shard_map.346 = (f32[7,1024]{1,0:T(8,128)S(1)}, f32[1024,1024]{1,0:T(8,128)S(1)}, f32[1024,1024]{1,0:T(8,128)S(1)}, bf16[1024,1024]{1,0:T(8,128)(2,1)}, bf16[10...) custom-call(s32[1]{0:T(128)} %constant.89.clone.1.tick_ref, ...), custom_call_target="tpu_custom_call", output_to_operand_aliasing={{0}: (18, {}), {1}: (19, {}), {2}: (20, {}), {3}: (21, {}),... | custom-call | flops 11000000512 | bytes 4194304 | tf_op jit(solution)/shard_map/pallas_call | solution.py:745
  341.2 11.2 %shard_map.348 = (f32[7,1024]{1,0:T(8,128)S(1)}, f32[1024,1024]{1,0:T(8,128)S(1)}, f32[1024,1024]{1,0:T(8,128)S(1)}, bf16[1024,1024]{1,0:T(8,128)(2,1)}, bf16[10...) custom-call(s32[1]{0:T(128)} %constant.88.clone.1.tick_ref, ...), custom_call_target="tpu_custom_call", output_to_operand_aliasing={{0}: (18, {}), {1}: (19, {}), {2}: (20, {}), {3}: (21, {}),... | custom-call | flops 11000000512 | bytes 4194304 | tf_op jit(solution)/shard_map/pallas_call | solution.py:745
  353.8 10.9 %shard_map.349 = (f32[4,1024]{1,0:T(4,128)S(1)}, f32[3,4096]{1,0:T(4,128)S(1)}, bf16[1024,1024]{1,0:T(8,128)(2,1)}, bf16[1024,4096]{1,0:T(8,128)(2,1)}, f32[128,1024]{1,0:T(8,128)S(1)}) custom-call(s32[1]{0:T(128)} %constant.87.clone.1.tick_ref, ...), custom_call_target="tpu_custom_call", output_to_operand_aliasing={{0}: (12, {}), {1}: (13, {}), {2}: (14, {}), {3}: (15, {})} | custom-call | flops 2147483648 | bytes 4194304 | tf_op jit(solution)/shard_map/pallas_call | solution.py:745
  364.8 9.8 %shard_map.350 = (f32[7,1024]{1,0:T(8,128)S(1)}, f32[1024,1024]{1,0:T(8,128)S(1)}, f32[1024,1024]{1,0:T(8,128)S(1)}, bf16[1024,1024]{1,0:T(8,128)(2,1)}, bf16[10...) custom-call(s32[1]{0:T(128)} %constant.87.clone.1.tick_ref, ...), custom_call_target="tpu_custom_call", output_to_operand_aliasing={{0}: (18, {}), {1}: (19, {}), {2}: (20, {}), {3}: (21, {}),... | custom-call | flops 11000000512 | bytes 4194304 | tf_op jit(solution)/shard_map/pallas_call | solution.py:745
  383.0 10.1 %shard_map.352 = (f32[7,1024]{1,0:T(8,128)S(1)}, f32[1024,1024]{1,0:T(8,128)S(1)}, f32[1024,1024]{1,0:T(8,128)S(1)}, bf16[1024,1024]{1,0:T(8,128)(2,1)}, bf16[10...) custom-call(s32[1]{0:T(128)} %constant.86.clone.1.tick_ref, ...), custom_call_target="tpu_custom_call", output_to_operand_aliasing={{0}: (18, {}), {1}: (19, {}), {2}: (20, {}), {3}: (21, {}),... | custom-call | flops 11000000512 | bytes 4194304 | tf_op jit(solution)/shard_map/pallas_call | solution.py:745
  401.3 8.7 %shard_map.354 = (f32[7,1024]{1,0:T(8,128)S(1)}, f32[1024,1024]{1,0:T(8,128)S(1)}, f32[1024,1024]{1,0:T(8,128)S(1)}, bf16[1024,1024]{1,0:T(8,128)(2,1)}, bf16[10...) custom-call(s32[1]{0:T(128)} %constant.85.clone.1.tick_ref, ...), custom_call_target="tpu_custom_call", output_to_operand_aliasing={{0}: (18, {}), {1}: (19, {}), {2}: (20, {}), {3}: (21, {}),... | custom-call | flops 11000000512 | bytes 4194304 | tf_op jit(solution)/shard_map/pallas_call | solution.py:745
  413.5 7.7 %shard_map.355 = (f32[4,1024]{1,0:T(4,128)S(1)}, f32[3,4096]{1,0:T(4,128)S(1)}, bf16[1024,1024]{1,0:T(8,128)(2,1)}, bf16[1024,4096]{1,0:T(8,128)(2,1)}, f32[128,1024]{1,0:T(8,128)S(1)}) custom-call(s32[1]{0:T(128)} %constant.84.clone.1.tick_ref, ...), custom_call_target="tpu_custom_call", output_to_operand_aliasing={{0}: (12, {}), {1}: (13, {}), {2}: (14, {}), {3}: (15, {})} | custom-call | flops 2147483648 | bytes 4194304 | tf_op jit(solution)/shard_map/pallas_call | solution.py:745
  421.2 8.7 %shard_map.356 = (f32[7,1024]{1,0:T(8,128)S(1)}, f32[1024,1024]{1,0:T(8,128)S(1)}, f32[1024,1024]{1,0:T(8,128)S(1)}, bf16[1024,1024]{1,0:T(8,128)(2,1)}, bf16[10...) custom-call(s32[1]{0:T(128)} %constant.84.clone.1.tick_ref, ...), custom_call_target="tpu_custom_call", output_to_operand_aliasing={{0}: (18, {}), {1}: (19, {}), {2}: (20, {}), {3}: (21, {}),... | custom-call | flops 11000000512 | bytes 4194304 | tf_op jit(solution)/shard_map/pallas_call | solution.py:745
  438.9 10.3 %collective-permute-done.30.inc_ref = bf16[128,1024]{1,0:T(8,128)(2,1)S(1)} collective-permute-done((bf16[128,1024]{1,0:T(8,128)(2,1)S(1)}, bf16[128,1024]{1,0:T(8,128)(2,1)S(1)}, u32[]{:S(2)}, u32[]{:S(2)}) %collective-permute-start.30) | collective-permute-done | bytes 262176 | tf_op jit(solution)/shard_map/ppermute | solution.py:1152
  449.2 9.2 %shard_map.358 = (f32[4,1024]{1,0:T(4,128)S(1)}, f32[3,4096]{1,0:T(4,128)S(1)}, bf16[1024,1024]{1,0:T(8,128)(2,1)}, bf16[1024,4096]{1,0:T(8,128)(2,1)}, f32[128,1024]{1,0:T(8,128)S(1)}) custom-call(s32[1]{0:T(128)} %constant.81.clone.1.tick_ref, ...), custom_call_target="tpu_custom_call", output_to_operand_aliasing={{0}: (12, {}), {1}: (13, {}), {2}: (14, {}), {3}: (15, {})} | custom-call | flops 2147483648 | bytes 4194304 | tf_op jit(solution)/shard_map/pallas_call | solution.py:745
  458.4 8.5 %shard_map.359.refs_2_ = bf16[2048,1024]{1,0:T(8,128)(2,1)} custom-call(bf16[1024,4096]{1,0:T(8,128)(2,1)} %get-tuple-element.827.refs_0_, bf16[1024,1024]{1,0:T(8,128)(2,1)} %get-tuple-element.1035.refs_1_.refs_2_, bf16[1024,1024]{1,0:T(8,128)(2,1)} %get-tuple-element.1035.refs_1_.refs_2_), custom_call_target="tpu_custom_call" | custom-call | flops 1100000000 | bytes 1024 | tf_op jit(solution)/shard_map/pallas_call | solution.py:842
  466.9 8.7 %shard_map.360.refs_3_ = bf16[1024,2048]{1,0:T(8,128)(2,1)} custom-call(bf16[1024,1024]{1,0:T(8,128)(2,1)} %get-tuple-element.1036.refs_0_, bf16[1024,4096]{1,0:T(8,128)(2,1)} %get-tuple-element.1037.refs_1_, bf16[2048,1024]{1,0:T(8,128)(2,1)} %shard_map.359.refs_2_), custom_call_target="tpu_custom_call" | custom-call | flops 1100000000 | bytes 1024 | tf_op jit(solution)/shard_map/pallas_call | solution.py:842
  476.1 9.0 %shard_map.361 = (bf16[512,1024]{1,0:T(8,128)(2,1)}, bf16[512,1024]{1,0:T(8,128)(2,1)}, bf16[512,1024]{1,0:T(8,128)(2,1)}, bf16[512,1024]{1,0:T(8,128)(2,1)}) custom-call(s32[6]{0:T(128)S(1)} %stack.46.after.place_ref.section_ref, bf16[1024,4096]{1,0:T(8,128)(2,1)} %get-tuple-element.827.refs_0_, bf16[1024,1024]{1,0:T(8,128)(2,1)} %get-tuple-element.1035.refs_1_.refs_2_, ...), custom_call_target="tpu_custom_call" | custom-call | flops 1100000000 | bytes 1024 | tf_op jit(solution)/shard_map/pallas_call | solution.py:901
  490.1 9.2 %shard_map.362 = (bf16[256,2048]{1,0:T(8,128)(2,1)}, bf16[256,2048]{1,0:T(8,128)(2,1)}, bf16[256,2048]{1,0:T(8,128)(2,1)}, bf16[256,2048]{1,0:T(8,128)(2,1)}) custom-call(s32[6]{0:T(128)S(1)} %stack.46.after.place_ref.section_ref, bf16[1024,1024]{1,0:T(8,128)(2,1)} %get-tuple-element.1036.refs_0_, bf16[1024,4096]{1,0:T(8,128)(2,1)} %get-tuple-element.1037.refs_1_, ...), custom_call_target="tpu_custom_call" | custom-call | flops 1100000000 | bytes 1024 | tf_op jit(solution)/shard_map/pallas_call | solution.py:901
  513.0 9.1 %shard_map.363 = (f32[7,1024]{1,0:T(8,128)S(1)}, f32[1024,1024]{1,0:T(8,128)S(1)}, f32[1024,1024]{1,0:T(8,128)S(1)}, bf16[1024,1024]{1,0:T(8,128)(2,1)}, bf16[10...) custom-call(s32[1]{0:T(128)} %constant.83.clone.1.tick_ref, ...), custom_call_target="tpu_custom_call", output_to_operand_aliasing={{0}: (18, {}), {1}: (19, {}), {2}: (20, {}), {3}: (21, {}),... | custom-call | flops 1100000000 | bytes 4194304 | tf_op jit(solution)/shard_map/pallas_call | solution.py:745
  525.5 10.4 %shard_map.365 = (f32[7,1024]{1,0:T(8,128)S(1)}, f32[1024,1024]{1,0:T(8,128)S(1)}, f32[1024,1024]{1,0:T(8,128)S(1)}, bf16[1024,1024]{1,0:T(8,128)(2,1)}, bf16[10...) custom-call(s32[1]{0:T(128)} %constant.81.clone.1.tick_ref, ...), custom_call_target="tpu_custom_call", output_to_operand_aliasing={{0}: (18, {}), {1}: (19, {}), {2}: (20, {}), {3}: (21, {}),... | custom-call | flops 1100000000 | bytes 4194304 | tf_op jit(solution)/shard_map/pallas_call | solution.py:745
  535.9 9.2 %shard_map.366.refs_4_ = bf16[1024,2048]{1,0:T(8,128)(2,1)} custom-call(bf16[1024,1024]{1,0:T(8,128)(2,1)} %get-tuple-element.1058.refs_0_, bf16[1024,1024]{1,0:T(8,128)(2,1)} %get-tuple-element.1069.refs_1_, bf16[1024,1024]{1,0:T(8,128)(2,1)} %get-tuple-element.1070.refs_2_, bf16[1024,1024]{1,0:T(8,128)(2,1)} %get-tuple-element.1071.refs_3_, ...), custom_call_target="tpu_custom_call" | custom-call | flops 1100000000 | bytes 1024 | tf_op jit(solution)/shard_map/pallas_call | solution.py:842
  554.6 10.5 %shard_map.368 = (bf16[256,2048]{1,0:T(8,128)(2,1)}, bf16[256,2048]{1,0:T(8,128)(2,1)}, bf16[256,2048]{1,0:T(8,128)(2,1)}, bf16[256,2048]{1,0:T(8,128)(2,1)}) custom-call(s32[6]{0:T(128)S(1)} %stack.46.after.place_ref.section_ref, bf16[1024,1024]{1,0:T(8,128)(2,1)} %get-tuple-element.1058.refs_0_, bf16[1024,1024]{1,0:T(8,128)(2,1)} %get-tuple-element.1069.refs_1_, ...), custom_call_target="tpu_custom_call" | custom-call | flops 1100000000 | bytes 1024 | tf_op jit(solution)/shard_map/pallas_call | solution.py:901
  572.8 22.3 %collective-permute-done.42.refs_1_ = bf16[256,2048]{1,0:T(8,128)(2,1)S(1)} collective-permute-done((bf16[256,2048]{1,0:T(8,128)(2,1)}, bf16[256,2048]{1,0:T(8,128)(2,1)S(1)}, u32[]{:S(2)}, u32[]{:S(2)}) %collective-permute-start.42) | collective-permute-done | bytes 1048608 | tf_op jit(solution)/shard_map/ppermute | solution.py:819
  614.6 10.9 %collective-permute-done.52.refs_2_ = bf16[256,1024]{1,0:T(8,128)(2,1)S(1)} collective-permute-done((bf16[256,1024]{1,0:T(8,128)(2,1)S(1)}, bf16[256,1024]{1,0:T(8,128)(2,1)S(1)}, u32[]{:S(2)}, u32[]{:S(2)}) %collective-permute-start.52) | collective-permute-done | bytes 524320 | tf_op jit(solution)/shard_map/ppermute | solution.py:819
  638.7 9.2 %collective-permute-done.53.refs_3_ = bf16[256,1024]{1,0:T(8,128)(2,1)S(1)} collective-permute-done((bf16[256,1024]{1,0:T(8,128)(2,1)S(1)}, bf16[256,1024]{1,0:T(8,128)(2,1)S(1)}, u32[]{:S(2)}, u32[]{:S(2)}) %collective-permute-start.53) | collective-permute-done | bytes 524320 | tf_op jit(solution)/shard_map/ppermute | solution.py:819
  661.1 9.4 %collective-permute-done.64.refs_2_ = bf16[128,2048]{1,0:T(8,128)(2,1)S(1)} collective-permute-done((bf16[128,2048]{1,0:T(8,128)(2,1)}, bf16[128,2048]{1,0:T(8,128)(2,1)S(1)}, u32[]{:S(2)}, u32[]{:S(2)}) %collective-permute-start.64) | collective-permute-done | bytes 524320 | tf_op jit(solution)/shard_map/ppermute | solution.py:819
  679.9 13.0 %collective-permute-done.65.refs_3_ = bf16[128,2048]{1,0:T(8,128)(2,1)S(1)} collective-permute-done((bf16[128,2048]{1,0:T(8,128)(2,1)S(1)}, bf16[128,2048]{1,0:T(8,128)(2,1)S(1)}, u32[]{:S(2)}, u32[]{:S(2)}) %collective-permute-start.65) | collective-permute-done | bytes 524320 | tf_op jit(solution)/shard_map/ppermute | solution.py:819
  (449 shorter events, 352.0 us)
Async XLA Ops:
  0.7 34.6 %collective-permute-start.4 = (bf16[1024,2048]{1,0:T(8,128)(2,1)}, bf16[1024,2048]{1,0:T(8,128)(2,1)}, u32[]{:S(2)}, u32[]{:S(2)}) collective-permute-start(bf16[1024,2048]{1,0:T(8,128)(2,1)} %bitcast.204), channel_id=1, source_target_pairs={{0,1},{1,0},{2,3},{3,2},{4,5},{5,4},{6,7},{7,6},{8,9},{9,8},{10,11... | collective-permute-start | bytes 12582920 | tf_op jit(solution)/shard_map/ppermute | solution.py:1067
  1.2 36.3 %collective-permute-start.5 = (bf16[2048,1024]{1,0:T(8,128)(2,1)}, bf16[2048,1024]{1,0:T(8,128)(2,1)}, u32[]{:S(2)}, u32[]{:S(2)}) collective-permute-start(bf16[2048,1024]{1,0:T(8,128)(2,1)} %bitcast.206), channel_id=1, source_target_pairs={{0,1},{1,0},{2,3},{3,2},{4,5},{5,4},{6,7},{7,6},{8,9},{9,8},{10,11... | collective-permute-start | bytes 12582920 | tf_op jit(solution)/shard_map/ppermute | solution.py:1067
  1.7 25.0 %collective-permute-start.2 = (bf16[512,1024]{1,0:T(8,128)(2,1)}, bf16[512,1024]{1,0:T(8,128)(2,1)}, u32[]{:S(2)}, u32[]{:S(2)}) collective-permute-start(bf16[512,1024]{1,0:T(8,128)(2,1)} %bitcast.210), channel_id=1, source_target_pairs={{0,1},{1,0},{2,3},{3,2},{4,5},{5,4},{6,7},{7,6},{8,9},{9,8},{10,11... | collective-permute-start | bytes 3145736 | tf_op jit(solution)/shard_map/ppermute | solution.py:1067
  22.3 184.7 %collective-permute-start.19 = (bf16[512,1024]{1,0:T(8,128)(2,1)}, bf16[512,1024]{1,0:T(8,128)(2,1)}, u32[]{:S(2)}, u32[]{:S(2)}) collective-permute-start(bf16[512,1024]{1,0:T(8,128)(2,1)} %dynamic-slice_bitcast_fusion), channel_id=1, source_target_pairs={{0,1},{1,0},{2,3},{3,2},{4,5},{5,4},{6,7},{7,6},{8,9},{9,8},{10,11... | collective-permute-start | bytes 3145736 | tf_op jit(solution)/shard_map/ppermute | solution.py:1067
  152.3 24.9 %collective-permute-start.14 = (bf16[128,1024]{1,0:T(8,128)(2,1)S(1)}, bf16[128,1024]{1,0:T(8,128)(2,1)S(1)}, u32[]{:S(2)}, u32[]{:S(2)}) collective-permute-start(bf16[128,1024]{1,0:T(8,128)(2,1)S(1)} %get-tuple-element.729.prev_ref), channel_id=1, source_target_pairs={{0,8},{8,16},{16,24},{1,9},{9,17},{17,25},{2,10},{10,18},{18,26},{... | collective-permute-start | bytes 786440 | tf_op jit(solution)/shard_map/ppermute | solution.py:1152
  251.8 57.9 %collective-permute-start.24 = (bf16[128,1024]{1,0:T(8,128)(2,1)S(1)}, bf16[128,1024]{1,0:T(8,128)(2,1)S(1)}, u32[]{:S(2)}, u32[]{:S(2)}) collective-permute-start(bf16[128,1024]{1,0:T(8,128)(2,1)S(1)} %get-tuple-element.913.prev_ref), channel_id=1, source_target_pairs={{8,0},{16,8},{24,16},{9,1},{17,9},{25,17},{10,2},{18,10},{26,18},{... | collective-permute-start | bytes 786440 | tf_op jit(solution)/shard_map/ppermute | solution.py:1152
  264.5 69.8 %collective-permute-start.25 = (bf16[128,1024]{1,0:T(8,128)(2,1)S(1)}, bf16[128,1024]{1,0:T(8,128)(2,1)S(1)}, u32[]{:S(2)}, u32[]{:S(2)}) collective-permute-start(bf16[128,1024]{1,0:T(8,128)(2,1)S(1)} %get-tuple-element.929.prev_ref), channel_id=1, source_target_pairs={{8,0},{16,8},{24,16},{9,1},{17,9},{25,17},{10,2},{18,10},{26,18},{... | collective-permute-start | bytes 786440 | tf_op jit(solution)/shard_map/ppermute | solution.py:1152
  328.0 25.8 %collective-permute-start.26 = (bf16[128,1024]{1,0:T(8,128)(2,1)S(1)}, bf16[128,1024]{1,0:T(8,128)(2,1)S(1)}, u32[]{:S(2)}, u32[]{:S(2)}) collective-permute-start(bf16[128,1024]{1,0:T(8,128)(2,1)S(1)} %get-tuple-element.945.prev_ref), channel_id=1, source_target_pairs={{8,0},{16,8},{24,16},{9,1},{17,9},{25,17},{10,2},{18,10},{26,18},{... | collective-permute-start | bytes 786440 | tf_op jit(solution)/shard_map/ppermute | solution.py:1152
  485.1 36.9 %collective-permute-start.33 = (bf16[512,1024]{1,0:T(8,128)(2,1)}, bf16[512,1024]{1,0:T(8,128)(2,1)}, u32[]{:S(2)}, u32[]{:S(2)}) collective-permute-start(bf16[512,1024]{1,0:T(8,128)(2,1)} %get-tuple-element.1039), channel_id=1, source_target_pairs={{0,2},{2,0},{4,6},{6,4},{1,3},{3,1},{5,7},{7,5},{8,10},{10,8},{12,... | collective-permute-start | bytes 3145736 | tf_op jit(solution)/shard_map/ppermute | solution.py:819
  488.6 33.5 %collective-permute-start.34 = (bf16[512,1024]{1,0:T(8,128)(2,1)}, bf16[512,1024]{1,0:T(8,128)(2,1)}, u32[]{:S(2)}, u32[]{:S(2)}) collective-permute-start(bf16[512,1024]{1,0:T(8,128)(2,1)} %get-tuple-element.1041), channel_id=1, source_target_pairs={{0,4},{2,6},{4,0},{6,2},{1,5},{3,7},{5,1},{7,3},{8,12},{10,14},{12... | collective-permute-start | bytes 3145736 | tf_op jit(solution)/shard_map/ppermute | solution.py:819
  499.4 47.7 %collective-permute-start.39 = (bf16[256,2048]{1,0:T(8,128)(2,1)}, bf16[256,2048]{1,0:T(8,128)(2,1)}, u32[]{:S(2)}, u32[]{:S(2)}) collective-permute-start(bf16[256,2048]{1,0:T(8,128)(2,1)} %get-tuple-element.1076), channel_id=1, source_target_pairs={{0,2},{2,0},{4,6},{6,4},{1,3},{3,1},{5,7},{7,5},{8,10},{10,8},{12,... | collective-permute-start | bytes 3145736 | tf_op jit(solution)/shard_map/ppermute | solution.py:819
  500.0 48.6 %collective-permute-start.40 = (bf16[256,2048]{1,0:T(8,128)(2,1)}, bf16[256,2048]{1,0:T(8,128)(2,1)}, u32[]{:S(2)}, u32[]{:S(2)}) collective-permute-start(bf16[256,2048]{1,0:T(8,128)(2,1)} %get-tuple-element.1077), channel_id=1, source_target_pairs={{0,4},{2,6},{4,0},{6,2},{1,5},{3,7},{5,1},{7,3},{8,12},{10,14},{12... | collective-permute-start | bytes 3145736 | tf_op jit(solution)/shard_map/ppermute | solution.py:819
  500.6 69.2 %collective-permute-start.18 = (bf16[512,1024]{1,0:T(8,128)(2,1)}, bf16[512,1024]{1,0:T(8,128)(2,1)}, u32[]{:S(2)}, u32[]{:S(2)}) collective-permute-start(bf16[512,1024]{1,0:T(8,128)(2,1)} %get-tuple-element.826), channel_id=1, source_target_pairs={{0,1},{1,0},{2,3},{3,2},{4,5},{5,4},{6,7},{7,6},{8,9},{9,8},{10,11... | collective-permute-start | bytes 3145736 | tf_op jit(solution)/shard_map/ppermute | solution.py:1067
  551.9 47.5 %collective-permute-start.46 = (bf16[128,2048]{1,0:T(8,128)(2,1)}, bf16[128,2048]{1,0:T(8,128)(2,1)S(1)}, u32[]{:S(2)}, u32[]{:S(2)}) collective-permute-start(bf16[128,2048]{1,0:T(8,128)(2,1)} %get-tuple-element.1092), channel_id=1, source_target_pairs={{0,4},{2,6},{4,0},{6,2},{1,5},{3,7},{5,1},{7,3},{8,12},{10,14},{12... | collective-permute-start | bytes 1572872 | tf_op jit(solution)/shard_map/ppermute | solution.py:819
  553.9 45.9 %collective-permute-start.47 = (bf16[128,2048]{1,0:T(8,128)(2,1)S(1)}, bf16[128,2048]{1,0:T(8,128)(2,1)S(1)}, u32[]{:S(2)}, u32[]{:S(2)}) collective-permute-start(bf16[128,2048]{1,0:T(8,128)(2,1)S(1)} %copy-done.70), channel_id=1, source_target_pairs={{0,2},{2,0},{4,6},{6,4},{1,3},{3,1},{5,7},{7,5},{8,10},{10,8},{12,... | collective-permute-start | bytes 1572872 | tf_op jit(solution)/shard_map/ppermute | solution.py:819
  565.1 29.9 %collective-permute-start.42 = (bf16[256,2048]{1,0:T(8,128)(2,1)}, bf16[256,2048]{1,0:T(8,128)(2,1)S(1)}, u32[]{:S(2)}, u32[]{:S(2)}) collective-permute-start(bf16[256,2048]{1,0:T(8,128)(2,1)} %get-tuple-element.1086), channel_id=1, source_target_pairs={{0,2},{2,0},{4,6},{6,4},{1,3},{3,1},{5,7},{7,5},{8,10},{10,8},{12,... | collective-permute-start | bytes 3145736 | tf_op jit(solution)/shard_map/ppermute | solution.py:819
  566.6 28.8 %collective-permute-start.43 = (bf16[256,2048]{1,0:T(8,128)(2,1)}, bf16[256,2048]{1,0:T(8,128)(2,1)S(1)}, u32[]{:S(2)}, u32[]{:S(2)}) collective-permute-start(bf16[256,2048]{1,0:T(8,128)(2,1)} %get-tuple-element.1087), channel_id=1, source_target_pairs={{0,4},{2,6},{4,0},{6,2},{1,5},{3,7},{5,1},{7,3},{8,12},{10,14},{12... | collective-permute-start | bytes 3145736 | tf_op jit(solution)/shard_map/ppermute | solution.py:819
  572.2 29.2 %collective-permute-start.41 = (bf16[512,1024]{1,0:T(8,128)(2,1)S(1)}, bf16[512,1024]{1,0:T(8,128)(2,1)S(1)}, u32[]{:S(2)}, u32[]{:S(2)}) collective-permute-start(bf16[512,1024]{1,0:T(8,128)(2,1)S(1)} %copy-done.68), channel_id=1, source_target_pairs={{0,1},{1,0},{2,3},{3,2},{4,5},{5,4},{6,7},{7,6},{8,9},{9,8},{10,11... | collective-permute-start | bytes 3145736 | tf_op jit(solution)/shard_map/ppermute | solution.py:1067
  599.7 25.8 %collective-permute-start.52 = (bf16[256,1024]{1,0:T(8,128)(2,1)S(1)}, bf16[256,1024]{1,0:T(8,128)(2,1)S(1)}, u32[]{:S(2)}, u32[]{:S(2)}) collective-permute-start(bf16[256,1024]{1,0:T(8,128)(2,1)S(1)} %copy-done.44), channel_id=1, source_target_pairs={{0,2},{2,0},{4,6},{6,4},{1,3},{3,1},{5,7},{7,5},{8,10},{10,8},{12,... | collective-permute-start | bytes 1572872 | tf_op jit(solution)/shard_map/ppermute | solution.py:819
  601.4 25.6 %collective-permute-start.55 = (bf16[256,1024]{1,0:T(8,128)(2,1)S(1)}, bf16[256,1024]{1,0:T(8,128)(2,1)S(1)}, u32[]{:S(2)}, u32[]{:S(2)}) collective-permute-start(bf16[256,1024]{1,0:T(8,128)(2,1)S(1)} %copy-done.45), channel_id=1, source_target_pairs={{0,4},{2,6},{4,0},{6,2},{1,5},{3,7},{5,1},{7,3},{8,12},{10,14},{12... | collective-permute-start | bytes 1572872 | tf_op jit(solution)/shard_map/ppermute | solution.py:819
  602.9 29.5 %collective-permute-start.44 = (bf16[128,2048]{1,0:T(8,128)(2,1)}, bf16[128,2048]{1,0:T(8,128)(2,1)S(1)}, u32[]{:S(2)}, u32[]{:S(2)}) collective-permute-start(bf16[128,2048]{1,0:T(8,128)(2,1)} %get-tuple-element.1089), channel_id=1, source_target_pairs={{0,4},{2,6},{4,0},{6,2},{1,5},{3,7},{5,1},{7,3},{8,12},{10,14},{12... | collective-permute-start | bytes 1572872 | tf_op jit(solution)/shard_map/ppermute | solution.py:819
  609.9 26.8 %collective-permute-start.45 = (bf16[128,2048]{1,0:T(8,128)(2,1)}, bf16[128,2048]{1,0:T(8,128)(2,1)S(1)}, u32[]{:S(2)}, u32[]{:S(2)}) collective-permute-start(bf16[128,2048]{1,0:T(8,128)(2,1)} %get-tuple-element.1091), channel_id=1, source_target_pairs={{0,2},{2,0},{4,6},{6,4},{1,3},{3,1},{5,7},{7,5},{8,10},{10,8},{12,... | collective-permute-start | bytes 1572872 | tf_op jit(solution)/shard_map/ppermute | solution.py:819
  614.2 33.7 %collective-permute-start.53 = (bf16[256,1024]{1,0:T(8,128)(2,1)S(1)}, bf16[256,1024]{1,0:T(8,128)(2,1)S(1)}, u32[]{:S(2)}, u32[]{:S(2)}) collective-permute-start(bf16[256,1024]{1,0:T(8,128)(2,1)S(1)} %collective-permute-done.51.refs_1_), channel_id=1, source_target_pairs={{0,2},{2,0},{4,6},{6,4},{1,3},{3,1},{5,7},{7,5},{8,10},{10,8},{12,... | collective-permute-start | bytes 1572872 | tf_op jit(solution)/shard_map/ppermute | solution.py:819
  625.5 24.0 %collective-permute-start.56 = (bf16[256,1024]{1,0:T(8,128)(2,1)S(1)}, bf16[256,1024]{1,0:T(8,128)(2,1)S(1)}, u32[]{:S(2)}, u32[]{:S(2)}) collective-permute-start(bf16[256,1024]{1,0:T(8,128)(2,1)S(1)} %collective-permute-done.54.refs_5_), channel_id=1, source_target_pairs={{0,4},{2,6},{4,0},{6,2},{1,5},{3,7},{5,1},{7,3},{8,12},{10,14},{12... | collective-permute-start | bytes 1572872 | tf_op jit(solution)/shard_map/ppermute | solution.py:819
  627.0 27.9 %collective-permute-start.63 = (bf16[128,2048]{1,0:T(8,128)(2,1)}, bf16[128,2048]{1,0:T(8,128)(2,1)S(1)}, u32[]{:S(2)}, u32[]{:S(2)}) collective-permute-start(bf16[128,2048]{1,0:T(8,128)(2,1)} %get-tuple-element.1095.refs_4_.refs_0_), channel_id=1, source_target_pairs={{0,4},{2,6},{4,0},{6,2},{1,5},{3,7},{5,1},{7,3},{8,12},{10,14},{12... | collective-permute-start | bytes 1572872 | tf_op jit(solution)/shard_map/ppermute | solution.py:819
  632.4 26.8 %collective-permute-start.66 = (bf16[128,2048]{1,0:T(8,128)(2,1)}, bf16[128,2048]{1,0:T(8,128)(2,1)S(1)}, u32[]{:S(2)}, u32[]{:S(2)}) collective-permute-start(bf16[128,2048]{1,0:T(8,128)(2,1)} %get-tuple-element.1103.refs_4_), channel_id=1, source_target_pairs={{0,2},{2,0},{4,6},{6,4},{1,3},{3,1},{5,7},{7,5},{8,10},{10,8},{12,... | collective-permute-start | bytes 1572872 | tf_op jit(solution)/shard_map/ppermute | solution.py:819
  636.7 33.7 %collective-permute-start.64 = (bf16[128,2048]{1,0:T(8,128)(2,1)}, bf16[128,2048]{1,0:T(8,128)(2,1)S(1)}, u32[]{:S(2)}, u32[]{:S(2)}) collective-permute-start(bf16[128,2048]{1,0:T(8,128)(2,1)} %get-tuple-element.1095.refs_4_.refs_0_), channel_id=1, source_target_pairs={{0,2},{2,0},{4,6},{6,4},{1,3},{3,1},{5,7},{7,5},{8,10},{10,8},{12,... | collective-permute-start | bytes 1572872 | tf_op jit(solution)/shard_map/ppermute | solution.py:819
  648.0 30.5 %collective-permute-start.67 = (bf16[128,2048]{1,0:T(8,128)(2,1)S(1)}, bf16[128,2048]{1,0:T(8,128)(2,1)S(1)}, u32[]{:S(2)}, u32[]{:S(2)}) collective-permute-start(bf16[128,2048]{1,0:T(8,128)(2,1)S(1)} %copy-done.47), channel_id=1, source_target_pairs={{0,4},{2,6},{4,0},{6,2},{1,5},{3,7},{5,1},{7,3},{8,12},{10,14},{12... | collective-permute-start | bytes 1572872 | tf_op jit(solution)/shard_map/ppermute | solution.py:819
  649.5 45.8 %collective-permute-start.57 = (bf16[128,2048]{1,0:T(8,128)(2,1)}, bf16[128,2048]{1,0:T(8,128)(2,1)}, u32[]{:S(2)}, u32[]{:S(2)}) collective-permute-start(bf16[128,2048]{1,0:T(8,128)(2,1)} %get-tuple-element.1096.after_ref.refs_0_), channel_id=1, source_target_pairs={{0,4},{2,6},{4,0},{6,2},{1,5},{3,7},{5,1},{7,3},{8,12},{10,14},{12... | collective-permute-start | bytes 1572872 | tf_op jit(solution)/shard_map/ppermute | solution.py:819
  654.9 40.9 %collective-permute-start.60 = (bf16[128,2048]{1,0:T(8,128)(2,1)}, bf16[128,2048]{1,0:T(8,128)(2,1)}, u32[]{:S(2)}, u32[]{:S(2)}) collective-permute-start(bf16[128,2048]{1,0:T(8,128)(2,1)} %get-tuple-element.1102.refs_4_), channel_id=1, source_target_pairs={{0,2},{2,0},{4,6},{6,4},{1,3},{3,1},{5,7},{7,5},{8,10},{10,8},{12,... | collective-permute-start | bytes 1572872 | tf_op jit(solution)/shard_map/ppermute | solution.py:819
  659.2 33.7 %collective-permute-start.65 = (bf16[128,2048]{1,0:T(8,128)(2,1)S(1)}, bf16[128,2048]{1,0:T(8,128)(2,1)S(1)}, u32[]{:S(2)}, u32[]{:S(2)}) collective-permute-start(bf16[128,2048]{1,0:T(8,128)(2,1)S(1)} %collective-permute-done.63.refs_1_), channel_id=1, source_target_pairs={{0,2},{2,0},{4,6},{6,4},{1,3},{3,1},{5,7},{7,5},{8,10},{10,8},{12,... | collective-permute-start | bytes 1572872 | tf_op jit(solution)/shard_map/ppermute | solution.py:819
  679.4 29.8 %collective-permute-start.58 = (bf16[128,2048]{1,0:T(8,128)(2,1)S(1)}, bf16[128,2048]{1,0:T(8,128)(2,1)}, u32[]{:S(2)}, u32[]{:S(2)}) collective-permute-start(bf16[128,2048]{1,0:T(8,128)(2,1)S(1)} %copy-done.48), channel_id=1, source_target_pairs={{0,2},{2,0},{4,6},{6,4},{1,3},{3,1},{5,7},{7,5},{8,10},{10,8},{12,... | collective-permute-start | bytes 1572872 | tf_op jit(solution)/shard_map/ppermute | solution.py:819
  (128 other events, 1385.1 us)

commit v3 on v2

--- a/solution.py
+++ b/solution.py
@@ -9,12 +9,13 @@
 
 EPSILON = 1e-05
 CHUNK = 128
-KEYS = 256
+KEYS = 512
 TILE = 512
 STRIP = 256
+PART = 512
 HIDE = -1e30
 COSTS = (100, 15, 10, 5, 5)
-LIMITS = tuple(size * 2**20 for size in (7, 8, 11, 10))
+LIMITS = tuple(size * 2**20 for size in (14, 11, 10))
 F32 = jnp.float32
 BF16 = jnp.bfloat16
 VMEM = pl.BlockSpec(memory_space=pltpu.VMEM)
@@ -39,7 +40,8 @@
         pltpu.VMEM((chunk, units), BF16), pltpu.VMEM((chunk, units), BF16),
         pltpu.VMEM((chunk, 128), F32), pltpu.VMEM((chunk, width), F32),
         pltpu.VMEM((chunk, width), BF16), pltpu.VMEM((chunk, units), F32),
-        pltpu.VMEM((chunk, units), BF16), pltpu.VMEM((chunk, width), F32), DMA((4,)), DMA((2,)),
+        pltpu.VMEM((chunk, units), BF16), pltpu.VMEM((chunk, width), F32),
+        DMA((4,)), DMA((2,)),
     ],
     "ab": lambda chunk, width, units, length: [
         pltpu.VMEM((chunk, width), BF16), pltpu.VMEM((chunk, width), BF16),
@@ -189,7 +191,7 @@
     vec_ref, gain_ref, bias_ref, branch_ref,
     k_in, v_in, x_in, h1_in, q_in, o_in, lse_in, post_in, keep_in, send_in,
     k_ref, v_ref, x_buf, h1_buf, q_buf, o_buf, lse_buf, post_buf, keep_buf, send_buf, mid_ref,
-    x_s, h1_s, q_s, o_s, lse_s, post_s, hide_s, qkv_s, sems,
+    x_s, h1_s, q_s, o_s, lse_s, post_s, hide_s, qkv_s, sems, finish=True,
 ):
     del k_in, v_in, x_in, h1_in, q_in, o_in, lse_in, post_in, keep_in, send_in
     rows = mid_ref.shape[0]
@@ -204,6 +206,16 @@
     def _():
         store_rows(*state, "start")
 
+    def saves():
+        here = pl.ds(pl.multiple_of(chunk * rows, rows), rows)
+        return copies_of(
+            (
+                (x_s, x_buf.at[here]), (h1_s, h1_buf.at[here]), (q_s, q_buf.at[here]),
+                (o_s, o_buf.at[here]), (lse_s, lse_buf.at[chunk]), (post_s, post_buf.at[here]),
+            ),
+            sems,
+        )
+
     @pl.when(live)
     def _():
         first = pl.multiple_of(chunk * rows, rows)
@@ -217,19 +229,13 @@
         def _():
             x_s[...] = inc_ref[...]
 
-        sent = []
-
-        def send(source, target):
-            copy = pltpu.make_async_copy(source, target, sems.at[len(sent)])
-            copy.start()
-            sent.append(copy)
-
+        stores = saves()
         layer_in = x_s[...].astype(F32)
-        send(x_s, x_buf.at[here])
+        stores[0].start()
         normed, _ = norm_parts(layer_in)
         h1 = (normed * gain_ref[0:1].astype(F32) + bias_ref[0:1].astype(F32)).astype(BF16)
         h1_s[...] = h1
-        send(h1_s, h1_buf.at[here])
+        stores[1].start()
 
         def project(number, carry):
             side, which = number // 3, number % 3
@@ -242,7 +248,7 @@
         q_s[...] = qkv_s[0] * jnp.asarray(0.125, BF16)
         k_ref[here, :] = qkv_s[1]
         v_ref[here, :] = qkv_s[2]
-        send(q_s, q_buf.at[here])
+        stores[2].start()
 
         def attend(keys):
             place = first + lax.broadcasted_iota(jnp.int32, (rows, 1), 0)
@@ -265,7 +271,8 @@
                 lse = jnp.where(lane == 2 * pair, now[:rows], lse)
                 return jnp.where(lane == 2 * pair + 1, now[rows:], lse)
 
-            lse = lax.fori_loop(0, width // 128, one_pair, jnp.zeros((rows, 128), F32))
+            nothing = jnp.zeros((rows, 128), F32)
+            lse = lax.fori_loop(0, width // 128, one_pair, nothing, unroll=2)
             lse_s[...] = lse.T
 
         for count in range(length // KEYS):
@@ -274,12 +281,12 @@
             def _():
                 attend((count + 1) * KEYS)
 
-        send(o_s, o_buf.at[here])
-        send(lse_s, lse_buf.at[chunk])
+        stores[3].start()
+        stores[4].start()
         post_normed, _ = norm_parts(o_s[...] * row_of(vec_ref, 3 * half, half))
         post = post_normed * row_of(vec_ref, 4 * half, half) + row_of(vec_ref, 5 * half, half)
         post_s[...] = post.astype(BF16)
-        send(post_s, post_buf.at[here])
+        stores[5].start()
 
         def mix(number, carry):
             at = aligned(number, STRIP)
@@ -289,12 +296,20 @@
             return carry
 
         lax.fori_loop(0, width // STRIP, mix, 0, unroll=4)
-        for copy in sent:
-            copy.wait()
-
-    @pl.when((chunk >= 1) & (chunk <= length // rows))
-    def _():
-        store_rows(*state, "wait")
+
+    def done():
+        @pl.when(live)
+        def _():
+            for copy in saves():
+                copy.wait()
+
+        @pl.when((chunk >= 1) & (chunk <= length // rows))
+        def _():
+            store_rows(*state, "wait")
+
+    if finish:
+        done()
+    return done
 
 
 def gelu_parts(pre):
@@ -304,8 +319,8 @@
 
 
 def expand_kernel(
-    tick_ref, section_ref, near_ref, far_ref, mid_ref, we_ref, wr_ref, vec_ref, gain_ref,
-    bias_ref, branch_ref,
+    tick_ref, section_ref, near_ref, far_ref, near_back, far_back, mid_ref, we_ref, wr_ref,
+    vec_ref, gain_ref, bias_ref, branch_ref,
     h2_in, g_in, gp_in, m_in, st_in, mid_in,
     h2_buf, g_buf, gp_buf, m_buf, st_buf, mid_buf, out_ref, next_ref,
     h2_s, gf_s, g_s, gp_s, m_s, st_s, sems,
@@ -333,9 +348,16 @@
         more = (section_ref[0] == 0) & (chunk + 1 < length // rows)
         fetch = (section_ref, near_ref, far_ref, (chunk + 1) * rows, next_ref, sems.at[6])
 
+        turn = (section_ref[0] == section_ref[1] - 1) & (chunk == length // rows - 1)
+        back = (section_ref, near_back, far_back, chunk * rows, next_ref, sems.at[6])
+
         @pl.when(more)
         def _():
             chunk_rows(*fetch, "start")
+
+        @pl.when(turn)
+        def _():
+            chunk_rows(*back, "start")
 
         def wide(tile, which):
             first = 3 * width + which * half + tile % tiles * TILE
@@ -392,6 +414,10 @@
         @pl.when(more)
         def _():
             chunk_rows(*fetch, "wait")
+
+        @pl.when(turn)
+        def _():
+            chunk_rows(*back, "wait")
 
 
 def expand_back_kernel(
@@ -418,13 +444,13 @@
         here = pl.ds(pl.multiple_of(chunk * rows, rows), rows)
         loads = copies_of(
             (
-                (g_buf.at[here], g_s), (gp_buf.at[here], gp_s), (st_buf.at[here], st_s),
+                (g_buf.at[here], g_s), (st_buf.at[here], st_s), (gp_buf.at[here], gp_s),
                 (mid_buf.at[here], mid_s),
             ),
             in_sems,
         )
-        for copy in loads:
-            copy.start()
+        loads[0].start()
+        loads[1].start()
 
         @pl.when(section == last)
         def _():
@@ -449,7 +475,9 @@
         send(df_s, df_buf.at[here])
         sum_ref[0:1] += column_sum(grad_low.astype(F32))
         loads[0].wait()
-        loads[2].wait()
+        loads[1].wait()
+        loads[2].start()
+        loads[3].start()
         mean = st_s[:, 0:1]
         inv_std = st_s[:, 1:2]
         def reduce_back(tile, sums):
@@ -479,7 +507,7 @@
             dur_s[:, at] = grad.astype(BF16)
             return carry
 
-        loads[1].wait()
+        loads[2].wait()
         lax.fori_loop(0, 2 * tiles, active_back, 0, unroll=8)
         send(dur_s, dur_buf.at[here])
 
@@ -523,6 +551,21 @@
     last = section_ref[1] - 1
     chunk = count - 1 - (tick_ref[0] - 2 * (last - section))
 
+    def fetches():
+        here = pl.ds(pl.multiple_of(chunk * rows, rows), rows)
+        return copies_of(
+            (
+                (o_buf.at[here], o_s), (q_buf.at[here], q_s), (lse_buf.at[chunk], lse_s),
+                (x_buf.at[here], x_s),
+            ),
+            in_sems,
+        )
+
+    @pl.when((chunk >= 0) & (chunk < count))
+    def _():
+        for copy in fetches():
+            copy.start()
+
     state = (section_ref, keep_buf, send_buf, (chunk + 1) * rows, prev_ref, out_sems.at[4])
 
     @pl.when((chunk >= -1) & (chunk < count - 1))
@@ -533,15 +576,7 @@
     def _():
         first = pl.multiple_of(chunk * rows, rows)
         here = pl.ds(first, rows)
-        loads = copies_of(
-            (
-                (x_buf.at[here], x_s), (q_buf.at[here], q_s), (o_buf.at[here], o_s),
-                (lse_buf.at[chunk], lse_s),
-            ),
-            in_sems,
-        )
-        for copy in loads:
-            copy.start()
+        loads = fetches()
 
         @pl.when(chunk == count - 1)
         def _():
@@ -571,7 +606,7 @@
 
         lax.fori_loop(0, 2, mix_back, 0, unroll=2)
         grad_post = wide_s[...]
-        loads[2].wait()
+        loads[0].wait()
         attended = o_s[...]
         scale = row_of(vec_ref, 3 * half, half)
         normed, inv_std = norm_parts(attended * scale)
@@ -582,7 +617,7 @@
         do_s[...] = (grad_mixed * scale).astype(BF16)
 
         loads[1].wait()
-        loads[3].wait()
+        loads[2].wait()
 
         def attend(keys):
             place = first + lax.broadcasted_iota(jnp.int32, (1, rows), 1)
@@ -613,7 +648,7 @@
                 dqf_s[:, at] = pick_heads(dot_tn(grad_scores, key_pair)) * 0.125
                 return carry
 
-            lax.fori_loop(0, width // 128, one_pair, 0)
+            lax.fori_loop(0, width // 128, one_pair, 0, unroll=2)
 
         for number in range(length // KEYS):
 
@@ -643,7 +678,7 @@
 
         lax.fori_loop(0, width // STRIP, project_back, 0, unroll=4)
         grad_first = wide_s[...]
-        loads[0].wait()
+        loads[3].wait()
         normed, inv_std = norm_parts(x_s[...].astype(F32))
         sum_ref[5:6] += column_sum(grad_first * normed)
         sum_ref[6:7] += column_sum(grad_first)
@@ -661,6 +696,24 @@
     @pl.when((chunk >= -1) & (chunk < count - 1))
     def _():
         store_rows(*state, "wait")
+
+
+def forward_kernel(
+    tick_ref, section_ref, starts_ref, near_ref, far_ref, near_back, far_back, tok_ref, inc_ref,
+    prev_ref, wp_ref, wo_ref, we_ref, wr_ref, vec_ref, gain_ref, bias_ref, branch_ref, *refs,
+):
+    ins, outs, (out_ref, next_ref, mid_s), scratch = refs[:16], refs[16:32], refs[32:35], refs[35:]
+    shared = vec_ref, gain_ref, bias_ref, branch_ref
+    done = attend_kernel(
+        tick_ref, section_ref, starts_ref, tok_ref, inc_ref, prev_ref, wp_ref, wo_ref, *shared,
+        *ins[:10], *outs[:10], mid_s, *scratch[:9], finish=False,
+    )
+    expand_kernel(
+        tick_ref, section_ref, near_ref, far_ref, near_back, far_back, mid_s, we_ref, wr_ref,
+        *shared,
+        *ins[10:], *outs[10:], out_ref, next_ref, *scratch[9:],
+    )
+    done()
 
 
 def flip_kernel(source, after, target):
@@ -819,9 +872,20 @@
     return lax.ppermute(value, "batch", route)
 
 
-def product(lefts, rights, pairs, columns, number):
-    left = lefts[pairs[number]][...]
-    return slice(number * columns, (number + 1) * columns), dot_tn(left, rights[number][...])
+def products(lefts, rights, pairs, columns, tile, store):
+    part = min(tile, PART)
+
+    def body(index, carry):
+        at = aligned(index, part)
+        for number, right in enumerate(rights):
+            where = slice(number * columns, (number + 1) * columns)
+            store(at, where, dot_tn(lefts[pairs[number]][:, at], right[...]))
+        return carry
+
+    if tile == part:
+        body(0, 0)
+    else:
+        lax.fori_loop(0, tile // part, body, 0)
 
 
 def other_part(lefts, rights, pairs, axis, after, cost=1):
@@ -833,11 +897,11 @@
     side = 0 if axis == 0 else 1
 
     def kernel(*refs):
-        for number in range(len(rights)):
-            at, value = product(
-                refs[:len(lefts)], refs[len(lefts):], pairs, columns, number
-            )
-            refs[-1][:, at] = value.astype(BF16)
+        def store(at, where, value):
+            refs[-1][at, where] = value.astype(BF16)
+
+        inputs = refs[:len(lefts)], refs[len(lefts):len(lefts) + len(rights)]
+        products(*inputs, pairs, columns, tile, store)
 
     return pl.pallas_call(
         kernel,
@@ -882,11 +946,11 @@
             def _():
                 store(number - 2).wait()
 
-        for number in range(len(rights)):
-            where, value = product(
-                refs[:len(lefts)], refs[len(lefts):], pairs, columns, number
-            )
-            low_s[slot, :, where] = (value + come_ref[:, where].astype(F32)).astype(BF16)
+        def keep(at, where, value):
+            low_s[slot, at, where] = (value + come_ref[at, where].astype(F32)).astype(BF16)
+
+        inputs = refs[:len(lefts)], refs[len(lefts):len(lefts) + len(rights)]
+        products(*inputs, pairs, columns, tile, keep)
         for number in range(4):
 
             @pl.when(step == number)
@@ -1156,48 +1220,42 @@
     incoming = blank
     sent = None
     rows_in = first_rows(place, near_tokens, far_tokens, 0, chunk, wr_own)
+    kept = (
+        k_all, v_all, x_buf, h1_buf, q_buf, o_buf, lse_buf, post_buf, hid_keep, hid_send,
+        h2_buf, g_buf, gp_buf, m_buf, st_buf, mid_buf,
+    )
     for tick in range(ticks):
         now = jnp.full((1,), tick, jnp.int32)
         arriving = shifted(sent, 1) if sent is not None and tick + 1 < ticks else blank
-        (
-            k_all, v_all, x_buf, h1_buf, q_buf, o_buf, lse_buf, post_buf, hid_keep, hid_send,
-            middle,
-        ) = call(
-            attend_kernel,
+        *kept, sent, rows_in = call(
+            forward_kernel,
             (
-                now, place, starts, rows_in, incoming, blank if sent is None else sent, wp, wo,
-                vectors, gains, biases, branches,
+                now, place, starts, near_tokens, far_tokens, near_cotangent, far_cotangent,
+                rows_in, incoming, blank if sent is None else sent, wp, wo, we, wr, vectors, gains, biases, branches,
             ),
-            [SMEM] * 3 + [VMEM] * 9,
-            (
-                k_all, v_all, x_buf, h1_buf, q_buf, o_buf, lse_buf, post_buf, hid_keep, hid_send,
-            ),
-            [VMEM, VMEM] + [HBM] * 8,
-            [jax.ShapeDtypeStruct((chunk, width), F32)],
-            [VMEM],
-            SCR["af"](chunk, width, units, length),
-            LIMITS[0],
-            8 * dense * width,
-        )
-        h2_buf, g_buf, gp_buf, m_buf, st_buf, mid_buf, sent, rows_in = call(
-            expand_kernel,
-            (now, place, near_tokens, far_tokens, middle, we, wr, vectors, gains, biases, branches),
-            [SMEM, SMEM, HBM, HBM] + [VMEM] * 7,
-            (h2_buf, g_buf, gp_buf, m_buf, st_buf, mid_buf),
-            [HBM] * 6,
+            [SMEM, SMEM, SMEM] + [HBM] * 4 + [VMEM] * 11,
+            kept,
+            [VMEM, VMEM] + [HBM] * 14,
             [jax.ShapeDtypeStruct((chunk, width), BF16)] * 2,
             [VMEM] * 2,
-            SCR["ff"](chunk, width, units, length),
-            LIMITS[1],
-            2 * dense * units,
+            [
+                pltpu.VMEM((chunk, width), F32), *SCR["af"](chunk, width, units, length),
+                *SCR["ff"](chunk, width, units, length),
+            ],
+            LIMITS[0],
+            4 * dense * units,
         )
         incoming = arriving
 
+    (
+        k_all, v_all, x_buf, h1_buf, q_buf, o_buf, lse_buf, post_buf, hid_keep, hid_send,
+        h2_buf, g_buf, gp_buf, m_buf, st_buf, mid_buf,
+    ) = kept
     last_out = sent
     wrt = flipped(wr, sent)
-    wet = flipped(we, wrt)
+    wpt = flipped(wp, wrt)
+    wet = flipped(we, wpt)
     wot = flipped(wo, wet)
-    wpt = flipped(wp, wot)
     dk_acc, dv_acc = empty([sized(width, F32)] * 2, pltpu.VMEM, wpt)
     sum_f = jnp.zeros((4, width), F32)
     sum_w = jnp.zeros((3, units), F32)
@@ -1223,13 +1281,12 @@
             [jax.ShapeDtypeStruct((chunk, width), BF16)] * 2,
             [VMEM] * 2,
             SCR["ab"](chunk, width, units, length),
-            LIMITS[3],
+            LIMITS[2],
             cost * 11 * 10**8,
         )
 
     held = []
     carried = (sum_a, dk_acc, dv_acc, dq_buf, dkr_buf, dvr_buf, dmr_buf, ig_keep, ig_send)
-    rows_in = first_rows(place, near_cotangent, far_cotangent, length - chunk, chunk, wpt)
     for tick in range(ticks):
         now = jnp.full((1,), tick, jnp.int32)
         arriving = shifted(sent, -1) if sent is not None and tick + 1 < ticks else blank
@@ -1245,7 +1302,7 @@
             [jax.ShapeDtypeStruct((chunk, width), F32)],
             [VMEM],
             SCR["fb"](chunk, width, units, length),
-            LIMITS[2],
+            LIMITS[1],
             2 * dense * units,
         )
         held.append((now, grad_mid))

time: 734 us -> 716 us (0.975)
  waiting for transfers between devices: 181 us -> 169 us
    ppermute x24, waiting for transfers between devices: 84.7 us -> 71.8 us  [shifted(): return lax.ppermute(value, 'section', route)]
    pallas_call x56 -> x42, Pallas kernels: 277 us -> 279 us  [call(): pl.pallas_call(kernel, in_specs=specs + carried_specs, out_specs=carried_...]
    unnamed x190 -> x188, local copies, waits for them, and re-layouts: 33.2 us -> 31.9 us
  transfers between devices with their start and end apart: 69 -> 69, of which waited for: 21 -> 25; matrix products, arithmetic and copies ran while one was open for 2% -> 1% of each run, Pallas kernels for 51% -> 50%
where the time goes in v3:
time: 716 us; the launch traced here: 704 us
  Pallas kernels  398 us (56%)
  waiting for transfers between devices  169 us (24%)
  starting transfers between devices  93.2 us (13%)
  local copies, waits for them, and re-layouts  40 us (6%)
    pallas_call x42, Pallas kernels, call(): pl.pallas_call(kernel, in_specs=specs + carried_specs, out_specs=carried_...  279 us
    ppermute x32, waiting for transfers between devices, crossed(): return lax.ppermute(value, 'batch', route)  92.1 us
    ppermute x24, waiting for transfers between devices, shifted(): return lax.ppermute(value, 'section', route)  71.8 us
    ppermute x24, starting transfers between devices, shifted(): return lax.ppermute(value, 'section', route)  57.1 us
    ppermute x32, starting transfers between devices, crossed(): return lax.ppermute(value, 'batch', route)  32.2 us
    unnamed x188, local copies, waits for them, and re-layouts  31.9 us
    pallas_call x3, Pallas kernels, own_part(): pl.pallas_call(kernel, grid_spec=pltpu.PrefetchScalarGridSpec(num_scalar_...  29 us
    pallas_call x3, Pallas kernels, other_part(): pl.pallas_call(kernel, grid=(rows // tile,), in_specs=[pl.BlockSpec((leng...  26.3 us
  transfers between devices with their start and end apart: 69, of which 25 were waited for; matrix products, arithmetic and copies ran while one was open for 1% of the time, Pallas kernels for 50%

profile of v3, /device:TPU:0, one launch (start us, length us, event | category | flops | bytes accessed | tf_op | source)
XLA Modules:
  0.0 704.2 jit_solution(2255841382487877809)
XLA Ops:
  33.9 10.9 %shard_map.298 = (bf16[1024,1024]{1,0:T(8,128)(2,1)S(1)}, bf16[1024,1024]{1,0:T(8,128)(2,1)S(1)}, bf16[1024,1024]{1,0:T(8,128)(2,1)}, bf16[1024,1024]{1,0:T(8,12...) custom-call(s32[1]{0:T(128)} %constant.94.clone.1.tick_ref, ...), custom_call_target="tpu_custom_call", output_to_operand_aliasing={{0}: (18, {}), {1}: (19, {}), {2}: (20, {}), {3}: (21, {}),... | custom-call | flops 4294967296 | bytes 4194304 | tf_op jit(solution)/shard_map/pallas_call | solution.py:798
  46.2 11.2 %shard_map.299 = (bf16[1024,1024]{1,0:T(8,128)(2,1)S(1)}, bf16[1024,1024]{1,0:T(8,128)(2,1)S(1)}, bf16[1024,1024]{1,0:T(8,128)(2,1)}, bf16[1024,1024]{1,0:T(8,12...) custom-call(s32[1]{0:T(128)} %constant.93.clone.1.tick_ref, ...), custom_call_target="tpu_custom_call", output_to_operand_aliasing={{0}: (18, {}), {1}: (19, {}), {2}: (20, {}), {3}: (21, {}),... | custom-call | flops 4294967296 | bytes 4194304 | tf_op jit(solution)/shard_map/pallas_call | solution.py:798
  58.7 11.0 %shard_map.300 = (bf16[1024,1024]{1,0:T(8,128)(2,1)S(1)}, bf16[1024,1024]{1,0:T(8,128)(2,1)S(1)}, bf16[1024,1024]{1,0:T(8,128)(2,1)}, bf16[1024,1024]{1,0:T(8,12...) custom-call(s32[1]{0:T(128)} %constant.92.clone.1.tick_ref, ...), custom_call_target="tpu_custom_call", output_to_operand_aliasing={{0}: (18, {}), {1}: (19, {}), {2}: (20, {}), {3}: (21, {}),... | custom-call | flops 4294967296 | bytes 4194304 | tf_op jit(solution)/shard_map/pallas_call | solution.py:798
  71.0 11.4 %shard_map.301 = (bf16[1024,1024]{1,0:T(8,128)(2,1)S(1)}, bf16[1024,1024]{1,0:T(8,128)(2,1)S(1)}, bf16[1024,1024]{1,0:T(8,128)(2,1)}, bf16[1024,1024]{1,0:T(8,12...) custom-call(s32[1]{0:T(128)} %constant.91.clone.1.tick_ref, ...), custom_call_target="tpu_custom_call", output_to_operand_aliasing={{0}: (18, {}), {1}: (19, {}), {2}: (20, {}), {3}: (21, {}),... | custom-call | flops 4294967296 | bytes 4194304 | tf_op jit(solution)/shard_map/pallas_call | solution.py:798
  83.8 12.7 %shard_map.302 = (bf16[1024,1024]{1,0:T(8,128)(2,1)S(1)}, bf16[1024,1024]{1,0:T(8,128)(2,1)S(1)}, bf16[1024,1024]{1,0:T(8,128)(2,1)}, bf16[1024,1024]{1,0:T(8,12...) custom-call(s32[1]{0:T(128)} %constant.74.clone.1.tick_ref, ...), custom_call_target="tpu_custom_call", output_to_operand_aliasing={{0}: (18, {}), {1}: (19, {}), {2}: (20, {}), {3}: (21, {}),... | custom-call | flops 4294967296 | bytes 4194304 | tf_op jit(solution)/shard_map/pallas_call | solution.py:798
  97.8 12.8 %shard_map.303 = (bf16[1024,1024]{1,0:T(8,128)(2,1)S(1)}, bf16[1024,1024]{1,0:T(8,128)(2,1)S(1)}, bf16[1024,1024]{1,0:T(8,128)(2,1)}, bf16[1024,1024]{1,0:T(8,12...) custom-call(s32[1]{0:T(128)} %constant.90.clone.1.tick_ref, ...), custom_call_target="tpu_custom_call", output_to_operand_aliasing={{0}: (18, {}), {1}: (19, {}), {2}: (20, {}), {3}: (21, {}),... | custom-call | flops 4294967296 | bytes 4194304 | tf_op jit(solution)/shard_map/pallas_call | solution.py:798
  111.9 12.7 %shard_map.304 = (bf16[1024,1024]{1,0:T(8,128)(2,1)S(1)}, bf16[1024,1024]{1,0:T(8,128)(2,1)S(1)}, bf16[1024,1024]{1,0:T(8,128)(2,1)}, bf16[1024,1024]{1,0:T(8,12...) custom-call(s32[1]{0:T(128)} %constant.89.clone.1.tick_ref, ...), custom_call_target="tpu_custom_call", output_to_operand_aliasing={{0}: (18, {}), {1}: (19, {}), {2}: (20, {}), {3}: (21, {}),... | custom-call | flops 4294967296 | bytes 4194304 | tf_op jit(solution)/shard_map/pallas_call | solution.py:798
  126.0 13.1 %shard_map.305 = (bf16[1024,1024]{1,0:T(8,128)(2,1)S(1)}, bf16[1024,1024]{1,0:T(8,128)(2,1)S(1)}, bf16[1024,1024]{1,0:T(8,128)(2,1)}, bf16[1024,1024]{1,0:T(8,12...) custom-call(s32[1]{0:T(128)} %constant.88.clone.1.tick_ref, ...), custom_call_target="tpu_custom_call", output_to_operand_aliasing={{0}: (18, {}), {1}: (19, {}), {2}: (20, {}), {3}: (21, {}),... | custom-call | flops 4294967296 | bytes 4194304 | tf_op jit(solution)/shard_map/pallas_call | solution.py:798
  141.8 9.8 %collective-permute-start.15 = (bf16[128,1024]{1,0:T(8,128)(2,1)S(1)}, bf16[128,1024]{1,0:T(8,128)(2,1)S(1)}, u32[]{:S(2)}, u32[]{:S(2)}) collective-permute-start(bf16[128,1024]{1,0:T(8,128)(2,1)S(1)} %get-tuple-element.707.prev_ref), channel_id=1, source_target_pairs={{0,8},{8,16},{16,24},{1,9},{9,17},{17,25},{2,10},{10,18},{18,26},{... | collective-permute-start | bytes 786440 | tf_op jit(solution)/shard_map/ppermute | solution.py:1216
  152.6 13.8 %collective-permute-start.16 = (bf16[128,1024]{1,0:T(8,128)(2,1)S(1)}, bf16[128,1024]{1,0:T(8,128)(2,1)S(1)}, u32[]{:S(2)}, u32[]{:S(2)}) collective-permute-start(bf16[128,1024]{1,0:T(8,128)(2,1)S(1)} %get-tuple-element.725.prev_ref), channel_id=1, source_target_pairs={{0,8},{8,16},{16,24},{1,9},{9,17},{17,25},{2,10},{10,18},{18,26},{... | collective-permute-start | bytes 786440 | tf_op jit(solution)/shard_map/ppermute | solution.py:1216
  201.8 8.7 %shard_map.320 = (f32[4,1024]{1,0:T(4,128)S(1)}, f32[3,4096]{1,0:T(4,128)S(1)}, bf16[1024,1024]{1,0:T(8,128)(2,1)}, bf16[1024,4096]{1,0:T(8,128)(2,1)}, f32[128,1024]{1,0:T(8,128)S(1)}) custom-call(s32[1]{0:T(128)} %constant.93.clone.1.tick_ref, ...), custom_call_target="tpu_custom_call", output_to_operand_aliasing={{0}: (12, {}), {1}: (13, {}), {2}: (14, {}), {3}: (15, {})} | custom-call | flops 2147483648 | bytes 4194304 | tf_op jit(solution)/shard_map/pallas_call | solution.py:798
  233.3 10.8 %collective-permute-done.22.inc_ref = bf16[128,1024]{1,0:T(8,128)(2,1)S(1)} collective-permute-done((bf16[128,1024]{1,0:T(8,128)(2,1)S(1)}, bf16[128,1024]{1,0:T(8,128)(2,1)S(1)}, u32[]{:S(2)}, u32[]{:S(2)}) %collective-permute-start.22) | collective-permute-done | bytes 262176 | tf_op jit(solution)/shard_map/ppermute | solution.py:1216
  244.2 8.6 %shard_map.326 = (f32[4,1024]{1,0:T(4,128)S(1)}, f32[3,4096]{1,0:T(4,128)S(1)}, bf16[1024,1024]{1,0:T(8,128)(2,1)}, bf16[1024,4096]{1,0:T(8,128)(2,1)}, f32[128,1024]{1,0:T(8,128)S(1)}) custom-call(s32[1]{0:T(128)} %constant.74.clone.1.tick_ref, ...), custom_call_target="tpu_custom_call", output_to_operand_aliasing={{0}: (12, {}), {1}: (13, {}), {2}: (14, {}), {3}: (15, {})} | custom-call | flops 2147483648 | bytes 4194304 | tf_op jit(solution)/shard_map/pallas_call | solution.py:798
  265.9 30.2 %collective-permute-done.24.inc_ref = bf16[128,1024]{1,0:T(8,128)(2,1)S(1)} collective-permute-done((bf16[128,1024]{1,0:T(8,128)(2,1)S(1)}, bf16[128,1024]{1,0:T(8,128)(2,1)S(1)}, u32[]{:S(2)}, u32[]{:S(2)}) %collective-permute-start.24) | collective-permute-done | bytes 262176 | tf_op jit(solution)/shard_map/ppermute | solution.py:1216
  302.5 10.4 %shard_map.331 = (f32[7,1024]{1,0:T(8,128)S(1)}, f32[1024,1024]{1,0:T(8,128)S(1)}, f32[1024,1024]{1,0:T(8,128)S(1)}, bf16[1024,1024]{1,0:T(8,128)(2,1)}, bf16[10...) custom-call(s32[1]{0:T(128)} %constant.89.clone.1.tick_ref, ...), custom_call_target="tpu_custom_call", output_to_operand_aliasing={{0}: (18, {}), {1}: (19, {}), {2}: (20, {}), {3}: (21, {}),... | custom-call | flops 11000000512 | bytes 4194304 | tf_op jit(solution)/shard_map/pallas_call | solution.py:798
  315.9 8.8 %shard_map.332 = (f32[4,1024]{1,0:T(4,128)S(1)}, f32[3,4096]{1,0:T(4,128)S(1)}, bf16[1024,1024]{1,0:T(8,128)(2,1)}, bf16[1024,4096]{1,0:T(8,128)(2,1)}, f32[128,1024]{1,0:T(8,128)S(1)}) custom-call(s32[1]{0:T(128)} %constant.88.clone.1.tick_ref, ...), custom_call_target="tpu_custom_call", output_to_operand_aliasing={{0}: (12, {}), {1}: (13, {}), {2}: (14, {}), {3}: (15, {})} | custom-call | flops 2147483648 | bytes 4194304 | tf_op jit(solution)/shard_map/pallas_call | solution.py:798
  324.7 10.5 %shard_map.333 = (f32[7,1024]{1,0:T(8,128)S(1)}, f32[1024,1024]{1,0:T(8,128)S(1)}, f32[1024,1024]{1,0:T(8,128)S(1)}, bf16[1024,1024]{1,0:T(8,128)(2,1)}, bf16[10...) custom-call(s32[1]{0:T(128)} %constant.88.clone.1.tick_ref, ...), custom_call_target="tpu_custom_call", output_to_operand_aliasing={{0}: (18, {}), {1}: (19, {}), {2}: (20, {}), {3}: (21, {}),... | custom-call | flops 11000000512 | bytes 4194304 | tf_op jit(solution)/shard_map/pallas_call | solution.py:798
  343.0 11.1 %shard_map.335 = (f32[7,1024]{1,0:T(8,128)S(1)}, f32[1024,1024]{1,0:T(8,128)S(1)}, f32[1024,1024]{1,0:T(8,128)S(1)}, bf16[1024,1024]{1,0:T(8,128)(2,1)}, bf16[10...) custom-call(s32[1]{0:T(128)} %constant.87.clone.1.tick_ref, ...), custom_call_target="tpu_custom_call", output_to_operand_aliasing={{0}: (18, {}), {1}: (19, {}), {2}: (20, {}), {3}: (21, {}),... | custom-call | flops 11000000512 | bytes 4194304 | tf_op jit(solution)/shard_map/pallas_call | solution.py:798
  363.8 10.6 %shard_map.337 = (f32[7,1024]{1,0:T(8,128)S(1)}, f32[1024,1024]{1,0:T(8,128)S(1)}, f32[1024,1024]{1,0:T(8,128)S(1)}, bf16[1024,1024]{1,0:T(8,128)(2,1)}, bf16[10...) custom-call(s32[1]{0:T(128)} %constant.86.clone.1.tick_ref, ...), custom_call_target="tpu_custom_call", output_to_operand_aliasing={{0}: (18, {}), {1}: (19, {}), {2}: (20, {}), {3}: (21, {}),... | custom-call | flops 11000000512 | bytes 4194304 | tf_op jit(solution)/shard_map/pallas_call | solution.py:798
  379.2 9.1 %shard_map.338 = (f32[4,1024]{1,0:T(4,128)S(1)}, f32[3,4096]{1,0:T(4,128)S(1)}, bf16[1024,1024]{1,0:T(8,128)(2,1)}, bf16[1024,4096]{1,0:T(8,128)(2,1)}, f32[128,1024]{1,0:T(8,128)S(1)}) custom-call(s32[1]{0:T(128)} %constant.85.clone.1.tick_ref, ...), custom_call_target="tpu_custom_call", output_to_operand_aliasing={{0}: (12, {}), {1}: (13, {}), {2}: (14, {}), {3}: (15, {})} | custom-call | flops 2147483648 | bytes 4194304 | tf_op jit(solution)/shard_map/pallas_call | solution.py:798
  404.1 15.2 %shard_map.341 = (f32[7,1024]{1,0:T(8,128)S(1)}, f32[1024,1024]{1,0:T(8,128)S(1)}, f32[1024,1024]{1,0:T(8,128)S(1)}, bf16[1024,1024]{1,0:T(8,128)(2,1)}, bf16[10...) custom-call(s32[1]{0:T(128)} %constant.84.clone.1.tick_ref, ...), custom_call_target="tpu_custom_call", output_to_operand_aliasing={{0}: (18, {}), {1}: (19, {}), {2}: (20, {}), {3}: (21, {}),... | custom-call | flops 11000000512 | bytes 4194304 | tf_op jit(solution)/shard_map/pallas_call | solution.py:798
  427.8 10.6 %collective-permute-done.30.inc_ref = bf16[128,1024]{1,0:T(8,128)(2,1)S(1)} collective-permute-done((bf16[128,1024]{1,0:T(8,128)(2,1)S(1)}, bf16[128,1024]{1,0:T(8,128)(2,1)S(1)}, u32[]{:S(2)}, u32[]{:S(2)}) %collective-permute-start.30) | collective-permute-done | bytes 262176 | tf_op jit(solution)/shard_map/ppermute | solution.py:1216
  453.2 8.7 %shard_map.345.refs_3_ = bf16[1024,2048]{1,0:T(8,128)(2,1)} custom-call(bf16[1024,1024]{1,0:T(8,128)(2,1)} %get-tuple-element.1010.refs_0_, bf16[1024,4096]{1,0:T(8,128)(2,1)} %get-tuple-element.1011.refs_1_, bf16[2048,1024]{1,0:T(8,128)(2,1)} %shard_map.344.refs_2_), custom_call_target="tpu_custom_call" | custom-call | flops 1100000000 | bytes 1024 | tf_op jit(solution)/shard_map/pallas_call | solution.py:906
  462.4 9.1 %shard_map.346 = (bf16[512,1024]{1,0:T(8,128)(2,1)}, bf16[512,1024]{1,0:T(8,128)(2,1)}, bf16[512,1024]{1,0:T(8,128)(2,1)}, bf16[512,1024]{1,0:T(8,128)(2,1)}) custom-call(s32[6]{0:T(128)S(1)} %stack.46.after.place_ref.section_ref, bf16[1024,4096]{1,0:T(8,128)(2,1)} %get-tuple-element.800.refs_0_, bf16[1024,1024]{1,0:T(8,128)(2,1)} %get-tuple-element.1009.refs_1_.refs_2_, ...), custom_call_target="tpu_custom_call" | custom-call | flops 1100000000 | bytes 1024 | tf_op jit(solution)/shard_map/pallas_call | solution.py:965
  475.0 9.4 %shard_map.347 = (bf16[256,2048]{1,0:T(8,128)(2,1)}, bf16[256,2048]{1,0:T(8,128)(2,1)}, bf16[256,2048]{1,0:T(8,128)(2,1)}, bf16[256,2048]{1,0:T(8,128)(2,1)}) custom-call(s32[6]{0:T(128)S(1)} %stack.46.after.place_ref.section_ref, bf16[1024,1024]{1,0:T(8,128)(2,1)} %get-tuple-element.1010.refs_0_, bf16[1024,4096]{1,0:T(8,128)(2,1)} %get-tuple-element.1011.refs_1_, ...), custom_call_target="tpu_custom_call" | custom-call | flops 1100000000 | bytes 1024 | tf_op jit(solution)/shard_map/pallas_call | solution.py:965
  519.6 9.2 %shard_map.351.refs_4_ = bf16[1024,2048]{1,0:T(8,128)(2,1)} custom-call(bf16[1024,1024]{1,0:T(8,128)(2,1)} %get-tuple-element.1032.refs_0_, bf16[1024,1024]{1,0:T(8,128)(2,1)} %get-tuple-element.1043.refs_1_, bf16[1024,1024]{1,0:T(8,128)(2,1)} %get-tuple-element.1044.refs_2_, bf16[1024,1024]{1,0:T(8,128)(2,1)} %get-tuple-element.1045.refs_3_, ...), custom_call_target="tpu_custom_call" | custom-call | flops 1100000000 | bytes 1024 | tf_op jit(solution)/shard_map/pallas_call | solution.py:906
  538.4 10.5 %shard_map.353 = (bf16[256,2048]{1,0:T(8,128)(2,1)}, bf16[256,2048]{1,0:T(8,128)(2,1)}, bf16[256,2048]{1,0:T(8,128)(2,1)}, bf16[256,2048]{1,0:T(8,128)(2,1)}) custom-call(s32[6]{0:T(128)S(1)} %stack.46.after.place_ref.section_ref, bf16[1024,1024]{1,0:T(8,128)(2,1)} %get-tuple-element.1032.refs_0_, bf16[1024,1024]{1,0:T(8,128)(2,1)} %get-tuple-element.1043.refs_1_, ...), custom_call_target="tpu_custom_call" | custom-call | flops 1100000000 | bytes 1024 | tf_op jit(solution)/shard_map/pallas_call | solution.py:965
  556.8 22.0 %collective-permute-done.42.refs_1_ = bf16[256,2048]{1,0:T(8,128)(2,1)S(1)} collective-permute-done((bf16[256,2048]{1,0:T(8,128)(2,1)}, bf16[256,2048]{1,0:T(8,128)(2,1)S(1)}, u32[]{:S(2)}, u32[]{:S(2)}) %collective-permute-start.42) | collective-permute-done | bytes 1048608 | tf_op jit(solution)/shard_map/ppermute | solution.py:872
  598.4 10.8 %collective-permute-done.52.refs_2_ = bf16[256,1024]{1,0:T(8,128)(2,1)S(1)} collective-permute-done((bf16[256,1024]{1,0:T(8,128)(2,1)S(1)}, bf16[256,1024]{1,0:T(8,128)(2,1)S(1)}, u32[]{:S(2)}, u32[]{:S(2)}) %collective-permute-start.52) | collective-permute-done | bytes 524320 | tf_op jit(solution)/shard_map/ppermute | solution.py:872
  622.5 9.1 %collective-permute-done.53.refs_3_ = bf16[256,1024]{1,0:T(8,128)(2,1)S(1)} collective-permute-done((bf16[256,1024]{1,0:T(8,128)(2,1)S(1)}, bf16[256,1024]{1,0:T(8,128)(2,1)S(1)}, u32[]{:S(2)}, u32[]{:S(2)}) %collective-permute-start.53) | collective-permute-done | bytes 524320 | tf_op jit(solution)/shard_map/ppermute | solution.py:872
  645.0 9.2 %collective-permute-done.64.refs_2_ = bf16[128,2048]{1,0:T(8,128)(2,1)S(1)} collective-permute-done((bf16[128,2048]{1,0:T(8,128)(2,1)}, bf16[128,2048]{1,0:T(8,128)(2,1)S(1)}, u32[]{:S(2)}, u32[]{:S(2)}) %collective-permute-start.64) | collective-permute-done | bytes 524320 | tf_op jit(solution)/shard_map/ppermute | solution.py:872
  663.5 13.1 %collective-permute-done.65.refs_3_ = bf16[128,2048]{1,0:T(8,128)(2,1)S(1)} collective-permute-done((bf16[128,2048]{1,0:T(8,128)(2,1)S(1)}, bf16[128,2048]{1,0:T(8,128)(2,1)S(1)}, u32[]{:S(2)}, u32[]{:S(2)}) %collective-permute-start.65) | collective-permute-done | bytes 524320 | tf_op jit(solution)/shard_map/ppermute | solution.py:872
  (435 shorter events, 326.3 us)
Async XLA Ops:
  0.7 26.9 %collective-permute-start.4 = (bf16[1024,2048]{1,0:T(8,128)(2,1)}, bf16[1024,2048]{1,0:T(8,128)(2,1)}, u32[]{:S(2)}, u32[]{:S(2)}) collective-permute-start(bf16[1024,2048]{1,0:T(8,128)(2,1)} %bitcast.181), channel_id=1, source_target_pairs={{0,1},{1,0},{2,3},{3,2},{4,5},{5,4},{6,7},{7,6},{8,9},{9,8},{10,11... | collective-permute-start | bytes 12582920 | tf_op jit(solution)/shard_map/ppermute | solution.py:1131
  1.3 28.6 %collective-permute-start.5 = (bf16[2048,1024]{1,0:T(8,128)(2,1)}, bf16[2048,1024]{1,0:T(8,128)(2,1)}, u32[]{:S(2)}, u32[]{:S(2)}) collective-permute-start(bf16[2048,1024]{1,0:T(8,128)(2,1)} %bitcast.183), channel_id=1, source_target_pairs={{0,1},{1,0},{2,3},{3,2},{4,5},{5,4},{6,7},{7,6},{8,9},{9,8},{10,11... | collective-permute-start | bytes 12582920 | tf_op jit(solution)/shard_map/ppermute | solution.py:1131
  141.8 24.6 %collective-permute-start.15 = (bf16[128,1024]{1,0:T(8,128)(2,1)S(1)}, bf16[128,1024]{1,0:T(8,128)(2,1)S(1)}, u32[]{:S(2)}, u32[]{:S(2)}) collective-permute-start(bf16[128,1024]{1,0:T(8,128)(2,1)S(1)} %get-tuple-element.707.prev_ref), channel_id=1, source_target_pairs={{0,8},{8,16},{16,24},{1,9},{9,17},{17,25},{2,10},{10,18},{18,26},{... | collective-permute-start | bytes 786440 | tf_op jit(solution)/shard_map/ppermute | solution.py:1216
  253.6 42.5 %collective-permute-start.24 = (bf16[128,1024]{1,0:T(8,128)(2,1)S(1)}, bf16[128,1024]{1,0:T(8,128)(2,1)S(1)}, u32[]{:S(2)}, u32[]{:S(2)}) collective-permute-start(bf16[128,1024]{1,0:T(8,128)(2,1)S(1)} %get-tuple-element.887.prev_ref), channel_id=1, source_target_pairs={{8,0},{16,8},{24,16},{9,1},{17,9},{25,17},{10,2},{18,10},{26,18},{... | collective-permute-start | bytes 786440 | tf_op jit(solution)/shard_map/ppermute | solution.py:1216
  264.6 51.3 %collective-permute-start.25 = (bf16[128,1024]{1,0:T(8,128)(2,1)S(1)}, bf16[128,1024]{1,0:T(8,128)(2,1)S(1)}, u32[]{:S(2)}, u32[]{:S(2)}) collective-permute-start(bf16[128,1024]{1,0:T(8,128)(2,1)S(1)} %get-tuple-element.903.prev_ref), channel_id=1, source_target_pairs={{8,0},{16,8},{24,16},{9,1},{17,9},{25,17},{10,2},{18,10},{26,18},{... | collective-permute-start | bytes 786440 | tf_op jit(solution)/shard_map/ppermute | solution.py:1216
  312.9 23.6 %collective-permute-start.26 = (bf16[128,1024]{1,0:T(8,128)(2,1)S(1)}, bf16[128,1024]{1,0:T(8,128)(2,1)S(1)}, u32[]{:S(2)}, u32[]{:S(2)}) collective-permute-start(bf16[128,1024]{1,0:T(8,128)(2,1)S(1)} %get-tuple-element.919.prev_ref), channel_id=1, source_target_pairs={{8,0},{16,8},{24,16},{9,1},{17,9},{25,17},{10,2},{18,10},{26,18},{... | collective-permute-start | bytes 786440 | tf_op jit(solution)/shard_map/ppermute | solution.py:1216
  354.2 25.0 %collective-permute-start.28 = (bf16[128,1024]{1,0:T(8,128)(2,1)S(1)}, bf16[128,1024]{1,0:T(8,128)(2,1)S(1)}, u32[]{:S(2)}, u32[]{:S(2)}) collective-permute-start(bf16[128,1024]{1,0:T(8,128)(2,1)S(1)} %get-tuple-element.951.prev_ref), channel_id=1, source_target_pairs={{8,0},{16,8},{24,16},{9,1},{17,9},{25,17},{10,2},{18,10},{26,18},{... | collective-permute-start | bytes 786440 | tf_op jit(solution)/shard_map/ppermute | solution.py:1216
  396.3 24.3 %collective-permute-start.31 = (bf16[128,1024]{1,0:T(8,128)(2,1)S(1)}, bf16[128,1024]{1,0:T(8,128)(2,1)S(1)}, u32[]{:S(2)}, u32[]{:S(2)}) collective-permute-start(bf16[128,1024]{1,0:T(8,128)(2,1)S(1)} %get-tuple-element.983.prev_ref), channel_id=1, source_target_pairs={{8,0},{16,8},{24,16},{9,1},{17,9},{25,17},{10,2},{18,10},{26,18},{... | collective-permute-start | bytes 786440 | tf_op jit(solution)/shard_map/ppermute | solution.py:1216
  471.5 36.0 %collective-permute-start.33 = (bf16[512,1024]{1,0:T(8,128)(2,1)}, bf16[512,1024]{1,0:T(8,128)(2,1)}, u32[]{:S(2)}, u32[]{:S(2)}) collective-permute-start(bf16[512,1024]{1,0:T(8,128)(2,1)} %get-tuple-element.1013), channel_id=1, source_target_pairs={{0,2},{2,0},{4,6},{6,4},{1,3},{3,1},{5,7},{7,5},{8,10},{10,8},{12,... | collective-permute-start | bytes 3145736 | tf_op jit(solution)/shard_map/ppermute | solution.py:872
  473.5 34.0 %collective-permute-start.34 = (bf16[512,1024]{1,0:T(8,128)(2,1)}, bf16[512,1024]{1,0:T(8,128)(2,1)}, u32[]{:S(2)}, u32[]{:S(2)}) collective-permute-start(bf16[512,1024]{1,0:T(8,128)(2,1)} %get-tuple-element.1015), channel_id=1, source_target_pairs={{0,4},{2,6},{4,0},{6,2},{1,5},{3,7},{5,1},{7,3},{8,12},{10,14},{12... | collective-permute-start | bytes 3145736 | tf_op jit(solution)/shard_map/ppermute | solution.py:872
  484.4 46.8 %collective-permute-start.39 = (bf16[256,2048]{1,0:T(8,128)(2,1)}, bf16[256,2048]{1,0:T(8,128)(2,1)}, u32[]{:S(2)}, u32[]{:S(2)}) collective-permute-start(bf16[256,2048]{1,0:T(8,128)(2,1)} %get-tuple-element.1050), channel_id=1, source_target_pairs={{0,2},{2,0},{4,6},{6,4},{1,3},{3,1},{5,7},{7,5},{8,10},{10,8},{12,... | collective-permute-start | bytes 3145736 | tf_op jit(solution)/shard_map/ppermute | solution.py:872
  485.1 47.5 %collective-permute-start.40 = (bf16[256,2048]{1,0:T(8,128)(2,1)}, bf16[256,2048]{1,0:T(8,128)(2,1)}, u32[]{:S(2)}, u32[]{:S(2)}) collective-permute-start(bf16[256,2048]{1,0:T(8,128)(2,1)} %get-tuple-element.1051), channel_id=1, source_target_pairs={{0,4},{2,6},{4,0},{6,2},{1,5},{3,7},{5,1},{7,3},{8,12},{10,14},{12... | collective-permute-start | bytes 3145736 | tf_op jit(solution)/shard_map/ppermute | solution.py:872
  485.7 68.1 %collective-permute-start.19 = (bf16[512,1024]{1,0:T(8,128)(2,1)}, bf16[512,1024]{1,0:T(8,128)(2,1)}, u32[]{:S(2)}, u32[]{:S(2)}) collective-permute-start(bf16[512,1024]{1,0:T(8,128)(2,1)} %get-tuple-element.799), channel_id=1, source_target_pairs={{0,1},{1,0},{2,3},{3,2},{4,5},{5,4},{6,7},{7,6},{8,9},{9,8},{10,11... | collective-permute-start | bytes 3145736 | tf_op jit(solution)/shard_map/ppermute | solution.py:1131
  535.9 47.2 %collective-permute-start.46 = (bf16[128,2048]{1,0:T(8,128)(2,1)}, bf16[128,2048]{1,0:T(8,128)(2,1)S(1)}, u32[]{:S(2)}, u32[]{:S(2)}) collective-permute-start(bf16[128,2048]{1,0:T(8,128)(2,1)} %get-tuple-element.1066), channel_id=1, source_target_pairs={{0,4},{2,6},{4,0},{6,2},{1,5},{3,7},{5,1},{7,3},{8,12},{10,14},{12... | collective-permute-start | bytes 1572872 | tf_op jit(solution)/shard_map/ppermute | solution.py:872
  538.0 45.5 %collective-permute-start.47 = (bf16[128,2048]{1,0:T(8,128)(2,1)S(1)}, bf16[128,2048]{1,0:T(8,128)(2,1)S(1)}, u32[]{:S(2)}, u32[]{:S(2)}) collective-permute-start(bf16[128,2048]{1,0:T(8,128)(2,1)S(1)} %copy-done.62), channel_id=1, source_target_pairs={{0,2},{2,0},{4,6},{6,4},{1,3},{3,1},{5,7},{7,5},{8,10},{10,8},{12,... | collective-permute-start | bytes 1572872 | tf_op jit(solution)/shard_map/ppermute | solution.py:872
  548.9 29.9 %collective-permute-start.42 = (bf16[256,2048]{1,0:T(8,128)(2,1)}, bf16[256,2048]{1,0:T(8,128)(2,1)S(1)}, u32[]{:S(2)}, u32[]{:S(2)}) collective-permute-start(bf16[256,2048]{1,0:T(8,128)(2,1)} %get-tuple-element.1060), channel_id=1, source_target_pairs={{0,2},{2,0},{4,6},{6,4},{1,3},{3,1},{5,7},{7,5},{8,10},{10,8},{12,... | collective-permute-start | bytes 3145736 | tf_op jit(solution)/shard_map/ppermute | solution.py:872
  550.7 28.4 %collective-permute-start.43 = (bf16[256,2048]{1,0:T(8,128)(2,1)}, bf16[256,2048]{1,0:T(8,128)(2,1)S(1)}, u32[]{:S(2)}, u32[]{:S(2)}) collective-permute-start(bf16[256,2048]{1,0:T(8,128)(2,1)} %get-tuple-element.1061), channel_id=1, source_target_pairs={{0,4},{2,6},{4,0},{6,2},{1,5},{3,7},{5,1},{7,3},{8,12},{10,14},{12... | collective-permute-start | bytes 3145736 | tf_op jit(solution)/shard_map/ppermute | solution.py:872
  556.2 28.9 %collective-permute-start.41 = (bf16[512,1024]{1,0:T(8,128)(2,1)S(1)}, bf16[512,1024]{1,0:T(8,128)(2,1)S(1)}, u32[]{:S(2)}, u32[]{:S(2)}) collective-permute-start(bf16[512,1024]{1,0:T(8,128)(2,1)S(1)} %copy-done.52), channel_id=1, source_target_pairs={{0,1},{1,0},{2,3},{3,2},{4,5},{5,4},{6,7},{7,6},{8,9},{9,8},{10,11... | collective-permute-start | bytes 3145736 | tf_op jit(solution)/shard_map/ppermute | solution.py:1131
  583.5 25.7 %collective-permute-start.52 = (bf16[256,1024]{1,0:T(8,128)(2,1)S(1)}, bf16[256,1024]{1,0:T(8,128)(2,1)S(1)}, u32[]{:S(2)}, u32[]{:S(2)}) collective-permute-start(bf16[256,1024]{1,0:T(8,128)(2,1)S(1)} %copy-done.29), channel_id=1, source_target_pairs={{0,2},{2,0},{4,6},{6,4},{1,3},{3,1},{5,7},{7,5},{8,10},{10,8},{12,... | collective-permute-start | bytes 1572872 | tf_op jit(solution)/shard_map/ppermute | solution.py:872
  585.2 25.5 %collective-permute-start.55 = (bf16[256,1024]{1,0:T(8,128)(2,1)S(1)}, bf16[256,1024]{1,0:T(8,128)(2,1)S(1)}, u32[]{:S(2)}, u32[]{:S(2)}) collective-permute-start(bf16[256,1024]{1,0:T(8,128)(2,1)S(1)} %copy-done.30), channel_id=1, source_target_pairs={{0,4},{2,6},{4,0},{6,2},{1,5},{3,7},{5,1},{7,3},{8,12},{10,14},{12... | collective-permute-start | bytes 1572872 | tf_op jit(solution)/shard_map/ppermute | solution.py:872
  586.6 29.5 %collective-permute-start.44 = (bf16[128,2048]{1,0:T(8,128)(2,1)}, bf16[128,2048]{1,0:T(8,128)(2,1)S(1)}, u32[]{:S(2)}, u32[]{:S(2)}) collective-permute-start(bf16[128,2048]{1,0:T(8,128)(2,1)} %get-tuple-element.1063), channel_id=1, source_target_pairs={{0,4},{2,6},{4,0},{6,2},{1,5},{3,7},{5,1},{7,3},{8,12},{10,14},{12... | collective-permute-start | bytes 1572872 | tf_op jit(solution)/shard_map/ppermute | solution.py:872
  593.7 26.8 %collective-permute-start.45 = (bf16[128,2048]{1,0:T(8,128)(2,1)}, bf16[128,2048]{1,0:T(8,128)(2,1)S(1)}, u32[]{:S(2)}, u32[]{:S(2)}) collective-permute-start(bf16[128,2048]{1,0:T(8,128)(2,1)} %get-tuple-element.1065), channel_id=1, source_target_pairs={{0,2},{2,0},{4,6},{6,4},{1,3},{3,1},{5,7},{7,5},{8,10},{10,8},{12,... | collective-permute-start | bytes 1572872 | tf_op jit(solution)/shard_map/ppermute | solution.py:872
  598.0 33.7 %collective-permute-start.53 = (bf16[256,1024]{1,0:T(8,128)(2,1)S(1)}, bf16[256,1024]{1,0:T(8,128)(2,1)S(1)}, u32[]{:S(2)}, u32[]{:S(2)}) collective-permute-start(bf16[256,1024]{1,0:T(8,128)(2,1)S(1)} %collective-permute-done.51.refs_1_), channel_id=1, source_target_pairs={{0,2},{2,0},{4,6},{6,4},{1,3},{3,1},{5,7},{7,5},{8,10},{10,8},{12,... | collective-permute-start | bytes 1572872 | tf_op jit(solution)/shard_map/ppermute | solution.py:872
  609.2 23.9 %collective-permute-start.56 = (bf16[256,1024]{1,0:T(8,128)(2,1)S(1)}, bf16[256,1024]{1,0:T(8,128)(2,1)S(1)}, u32[]{:S(2)}, u32[]{:S(2)}) collective-permute-start(bf16[256,1024]{1,0:T(8,128)(2,1)S(1)} %collective-permute-done.54.refs_5_), channel_id=1, source_target_pairs={{0,4},{2,6},{4,0},{6,2},{1,5},{3,7},{5,1},{7,3},{8,12},{10,14},{12... | collective-permute-start | bytes 1572872 | tf_op jit(solution)/shard_map/ppermute | solution.py:872
  610.7 27.9 %collective-permute-start.63 = (bf16[128,2048]{1,0:T(8,128)(2,1)}, bf16[128,2048]{1,0:T(8,128)(2,1)S(1)}, u32[]{:S(2)}, u32[]{:S(2)}) collective-permute-start(bf16[128,2048]{1,0:T(8,128)(2,1)} %get-tuple-element.1069.refs_4_.refs_0_), channel_id=1, source_target_pairs={{0,4},{2,6},{4,0},{6,2},{1,5},{3,7},{5,1},{7,3},{8,12},{10,14},{12... | collective-permute-start | bytes 1572872 | tf_op jit(solution)/shard_map/ppermute | solution.py:872
  616.1 26.9 %collective-permute-start.66 = (bf16[128,2048]{1,0:T(8,128)(2,1)}, bf16[128,2048]{1,0:T(8,128)(2,1)}, u32[]{:S(2)}, u32[]{:S(2)}) collective-permute-start(bf16[128,2048]{1,0:T(8,128)(2,1)} %get-tuple-element.1077.refs_4_), channel_id=1, source_target_pairs={{0,2},{2,0},{4,6},{6,4},{1,3},{3,1},{5,7},{7,5},{8,10},{10,8},{12,... | collective-permute-start | bytes 1572872 | tf_op jit(solution)/shard_map/ppermute | solution.py:872
  620.5 33.7 %collective-permute-start.64 = (bf16[128,2048]{1,0:T(8,128)(2,1)}, bf16[128,2048]{1,0:T(8,128)(2,1)S(1)}, u32[]{:S(2)}, u32[]{:S(2)}) collective-permute-start(bf16[128,2048]{1,0:T(8,128)(2,1)} %get-tuple-element.1069.refs_4_.refs_0_), channel_id=1, source_target_pairs={{0,2},{2,0},{4,6},{6,4},{1,3},{3,1},{5,7},{7,5},{8,10},{10,8},{12,... | collective-permute-start | bytes 1572872 | tf_op jit(solution)/shard_map/ppermute | solution.py:872
  631.7 30.5 %collective-permute-start.67 = (bf16[128,2048]{1,0:T(8,128)(2,1)S(1)}, bf16[128,2048]{1,0:T(8,128)(2,1)S(1)}, u32[]{:S(2)}, u32[]{:S(2)}) collective-permute-start(bf16[128,2048]{1,0:T(8,128)(2,1)S(1)} %copy-done.32), channel_id=1, source_target_pairs={{0,4},{2,6},{4,0},{6,2},{1,5},{3,7},{5,1},{7,3},{8,12},{10,14},{12... | collective-permute-start | bytes 1572872 | tf_op jit(solution)/shard_map/ppermute | solution.py:872
  633.1 45.8 %collective-permute-start.57 = (bf16[128,2048]{1,0:T(8,128)(2,1)}, bf16[128,2048]{1,0:T(8,128)(2,1)}, u32[]{:S(2)}, u32[]{:S(2)}) collective-permute-start(bf16[128,2048]{1,0:T(8,128)(2,1)} %get-tuple-element.1070.after_ref.refs_0_), channel_id=1, source_target_pairs={{0,4},{2,6},{4,0},{6,2},{1,5},{3,7},{5,1},{7,3},{8,12},{10,14},{12... | collective-permute-start | bytes 1572872 | tf_op jit(solution)/shard_map/ppermute | solution.py:872
  638.6 41.0 %collective-permute-start.60 = (bf16[128,2048]{1,0:T(8,128)(2,1)}, bf16[128,2048]{1,0:T(8,128)(2,1)}, u32[]{:S(2)}, u32[]{:S(2)}) collective-permute-start(bf16[128,2048]{1,0:T(8,128)(2,1)} %get-tuple-element.1076.refs_4_), channel_id=1, source_target_pairs={{0,2},{2,0},{4,6},{6,4},{1,3},{3,1},{5,7},{7,5},{8,10},{10,8},{12,... | collective-permute-start | bytes 1572872 | tf_op jit(solution)/shard_map/ppermute | solution.py:872
  643.0 33.6 %collective-permute-start.65 = (bf16[128,2048]{1,0:T(8,128)(2,1)S(1)}, bf16[128,2048]{1,0:T(8,128)(2,1)S(1)}, u32[]{:S(2)}, u32[]{:S(2)}) collective-permute-start(bf16[128,2048]{1,0:T(8,128)(2,1)S(1)} %collective-permute-done.63.refs_1_), channel_id=1, source_target_pairs={{0,2},{2,0},{4,6},{6,4},{1,3},{3,1},{5,7},{7,5},{8,10},{10,8},{12,... | collective-permute-start | bytes 1572872 | tf_op jit(solution)/shard_map/ppermute | solution.py:872
  663.1 30.1 %collective-permute-start.58 = (bf16[128,2048]{1,0:T(8,128)(2,1)S(1)}, bf16[128,2048]{1,0:T(8,128)(2,1)}, u32[]{:S(2)}, u32[]{:S(2)}) collective-permute-start(bf16[128,2048]{1,0:T(8,128)(2,1)S(1)} %copy-done.33), channel_id=1, source_target_pairs={{0,2},{2,0},{4,6},{6,4},{1,3},{3,1},{5,7},{7,5},{8,10},{10,8},{12,... | collective-permute-start | bytes 1572872 | tf_op jit(solution)/shard_map/ppermute | solution.py:872
  (127 other events, 2021.9 us)

commit v4 on v3

--- a/solution.py
+++ b/solution.py
@@ -508,7 +508,7 @@
             return carry
 
         loads[2].wait()
-        lax.fori_loop(0, 2 * tiles, active_back, 0, unroll=8)
+        lax.fori_loop(0, 2 * tiles, active_back, 0, unroll=2)
         send(dur_s, dur_buf.at[here])
 
         def expand_back(number, carry):

time: 716 us -> 711 us (level)
  transfers between devices with their start and end apart: 69 -> 69, of which waited for: 25 -> 27; matrix products, arithmetic and copies ran while one was open for 1% -> 1% of each run, Pallas kernels for 50% -> 49%
where the time goes in v4:
time: 711 us; the launch traced here: 700 us
  Pallas kernels  393 us (55%)
  waiting for transfers between devices  171 us (24%)
  starting transfers between devices  93.3 us (13%)
  local copies, waits for them, and re-layouts  38.8 us (5%)
    pallas_call x42, Pallas kernels, call(): pl.pallas_call(kernel, in_specs=specs + carried_specs, out_specs=carried_...  274 us
    ppermute x32, waiting for transfers between devices, crossed(): return lax.ppermute(value, 'batch', route)  91.8 us
    ppermute x24, waiting for transfers between devices, shifted(): return lax.ppermute(value, 'section', route)  73.9 us
    ppermute x24, starting transfers between devices, shifted(): return lax.ppermute(value, 'section', route)  56.9 us
    ppermute x32, starting transfers between devices, crossed(): return lax.ppermute(value, 'batch', route)  32.5 us
    unnamed x188, local copies, waits for them, and re-layouts  30.8 us
    pallas_call x3, Pallas kernels, own_part(): pl.pallas_call(kernel, grid_spec=pltpu.PrefetchScalarGridSpec(num_scalar_...  29 us
    pallas_call x3, Pallas kernels, other_part(): pl.pallas_call(kernel, grid=(rows // tile,), in_specs=[pl.BlockSpec((leng...  26.3 us
  transfers between devices with their start and end apart: 69, of which 27 were waited for; matrix products, arithmetic and copies ran while one was open for 1% of the time, Pallas kernels for 49%

profile of v4, /device:TPU:0, one launch (start us, length us, event | category | flops | bytes accessed | tf_op | source)
XLA Modules:
  0.0 699.9 jit_solution(1360144681081030826)
XLA Ops:
  33.9 10.9 %shard_map.298 = (bf16[1024,1024]{1,0:T(8,128)(2,1)S(1)}, bf16[1024,1024]{1,0:T(8,128)(2,1)S(1)}, bf16[1024,1024]{1,0:T(8,128)(2,1)}, bf16[1024,1024]{1,0:T(8,12...) custom-call(s32[1]{0:T(128)} %constant.94.clone.1.tick_ref, ...), custom_call_target="tpu_custom_call", output_to_operand_aliasing={{0}: (18, {}), {1}: (19, {}), {2}: (20, {}), {3}: (21, {}),... | custom-call | flops 4294967296 | bytes 4194304 | tf_op jit(solution)/shard_map/pallas_call | solution.py:798
  46.2 11.4 %shard_map.299 = (bf16[1024,1024]{1,0:T(8,128)(2,1)S(1)}, bf16[1024,1024]{1,0:T(8,128)(2,1)S(1)}, bf16[1024,1024]{1,0:T(8,128)(2,1)}, bf16[1024,1024]{1,0:T(8,12...) custom-call(s32[1]{0:T(128)} %constant.93.clone.1.tick_ref, ...), custom_call_target="tpu_custom_call", output_to_operand_aliasing={{0}: (18, {}), {1}: (19, {}), {2}: (20, {}), {3}: (21, {}),... | custom-call | flops 4294967296 | bytes 4194304 | tf_op jit(solution)/shard_map/pallas_call | solution.py:798
  58.9 11.0 %shard_map.300 = (bf16[1024,1024]{1,0:T(8,128)(2,1)S(1)}, bf16[1024,1024]{1,0:T(8,128)(2,1)S(1)}, bf16[1024,1024]{1,0:T(8,128)(2,1)}, bf16[1024,1024]{1,0:T(8,12...) custom-call(s32[1]{0:T(128)} %constant.92.clone.1.tick_ref, ...), custom_call_target="tpu_custom_call", output_to_operand_aliasing={{0}: (18, {}), {1}: (19, {}), {2}: (20, {}), {3}: (21, {}),... | custom-call | flops 4294967296 | bytes 4194304 | tf_op jit(solution)/shard_map/pallas_call | solution.py:798
  71.2 11.2 %shard_map.301 = (bf16[1024,1024]{1,0:T(8,128)(2,1)S(1)}, bf16[1024,1024]{1,0:T(8,128)(2,1)S(1)}, bf16[1024,1024]{1,0:T(8,128)(2,1)}, bf16[1024,1024]{1,0:T(8,12...) custom-call(s32[1]{0:T(128)} %constant.91.clone.1.tick_ref, ...), custom_call_target="tpu_custom_call", output_to_operand_aliasing={{0}: (18, {}), {1}: (19, {}), {2}: (20, {}), {3}: (21, {}),... | custom-call | flops 4294967296 | bytes 4194304 | tf_op jit(solution)/shard_map/pallas_call | solution.py:798
  83.7 12.7 %shard_map.302 = (bf16[1024,1024]{1,0:T(8,128)(2,1)S(1)}, bf16[1024,1024]{1,0:T(8,128)(2,1)S(1)}, bf16[1024,1024]{1,0:T(8,128)(2,1)}, bf16[1024,1024]{1,0:T(8,12...) custom-call(s32[1]{0:T(128)} %constant.74.clone.1.tick_ref, ...), custom_call_target="tpu_custom_call", output_to_operand_aliasing={{0}: (18, {}), {1}: (19, {}), {2}: (20, {}), {3}: (21, {}),... | custom-call | flops 4294967296 | bytes 4194304 | tf_op jit(solution)/shard_map/pallas_call | solution.py:798
  97.7 13.1 %shard_map.303 = (bf16[1024,1024]{1,0:T(8,128)(2,1)S(1)}, bf16[1024,1024]{1,0:T(8,128)(2,1)S(1)}, bf16[1024,1024]{1,0:T(8,128)(2,1)}, bf16[1024,1024]{1,0:T(8,12...) custom-call(s32[1]{0:T(128)} %constant.90.clone.1.tick_ref, ...), custom_call_target="tpu_custom_call", output_to_operand_aliasing={{0}: (18, {}), {1}: (19, {}), {2}: (20, {}), {3}: (21, {}),... | custom-call | flops 4294967296 | bytes 4194304 | tf_op jit(solution)/shard_map/pallas_call | solution.py:798
  112.1 12.7 %shard_map.304 = (bf16[1024,1024]{1,0:T(8,128)(2,1)S(1)}, bf16[1024,1024]{1,0:T(8,128)(2,1)S(1)}, bf16[1024,1024]{1,0:T(8,128)(2,1)}, bf16[1024,1024]{1,0:T(8,12...) custom-call(s32[1]{0:T(128)} %constant.89.clone.1.tick_ref, ...), custom_call_target="tpu_custom_call", output_to_operand_aliasing={{0}: (18, {}), {1}: (19, {}), {2}: (20, {}), {3}: (21, {}),... | custom-call | flops 4294967296 | bytes 4194304 | tf_op jit(solution)/shard_map/pallas_call | solution.py:798
  126.1 12.8 %shard_map.305 = (bf16[1024,1024]{1,0:T(8,128)(2,1)S(1)}, bf16[1024,1024]{1,0:T(8,128)(2,1)S(1)}, bf16[1024,1024]{1,0:T(8,128)(2,1)}, bf16[1024,1024]{1,0:T(8,12...) custom-call(s32[1]{0:T(128)} %constant.88.clone.1.tick_ref, ...), custom_call_target="tpu_custom_call", output_to_operand_aliasing={{0}: (18, {}), {1}: (19, {}), {2}: (20, {}), {3}: (21, {}),... | custom-call | flops 4294967296 | bytes 4194304 | tf_op jit(solution)/shard_map/pallas_call | solution.py:798
  141.8 9.6 %collective-permute-start.15 = (bf16[128,1024]{1,0:T(8,128)(2,1)S(1)}, bf16[128,1024]{1,0:T(8,128)(2,1)S(1)}, u32[]{:S(2)}, u32[]{:S(2)}) collective-permute-start(bf16[128,1024]{1,0:T(8,128)(2,1)S(1)} %get-tuple-element.707.prev_ref), channel_id=1, source_target_pairs={{0,8},{8,16},{16,24},{1,9},{9,17},{17,25},{2,10},{10,18},{18,26},{... | collective-permute-start | bytes 786440 | tf_op jit(solution)/shard_map/ppermute | solution.py:1216
  152.6 13.8 %collective-permute-start.16 = (bf16[128,1024]{1,0:T(8,128)(2,1)S(1)}, bf16[128,1024]{1,0:T(8,128)(2,1)S(1)}, u32[]{:S(2)}, u32[]{:S(2)}) collective-permute-start(bf16[128,1024]{1,0:T(8,128)(2,1)S(1)} %get-tuple-element.725.prev_ref), channel_id=1, source_target_pairs={{0,8},{8,16},{16,24},{1,9},{9,17},{17,25},{2,10},{10,18},{18,26},{... | collective-permute-start | bytes 786440 | tf_op jit(solution)/shard_map/ppermute | solution.py:1216
  221.3 9.0 %shard_map.323 = (f32[7,1024]{1,0:T(8,128)S(1)}, f32[1024,1024]{1,0:T(8,128)S(1)}, f32[1024,1024]{1,0:T(8,128)S(1)}, bf16[1024,1024]{1,0:T(8,128)(2,1)}, bf16[10...) custom-call(s32[1]{0:T(128)} %constant.92.clone.1.tick_ref, ...), custom_call_target="tpu_custom_call", output_to_operand_aliasing={{0}: (18, {}), {1}: (19, {}), {2}: (20, {}), {3}: (21, {}),... | custom-call | flops 11000000512 | bytes 4194304 | tf_op jit(solution)/shard_map/pallas_call | solution.py:798
  234.6 10.8 %collective-permute-done.22.inc_ref = bf16[128,1024]{1,0:T(8,128)(2,1)S(1)} collective-permute-done((bf16[128,1024]{1,0:T(8,128)(2,1)S(1)}, bf16[128,1024]{1,0:T(8,128)(2,1)S(1)}, u32[]{:S(2)}, u32[]{:S(2)}) %collective-permute-start.22) | collective-permute-done | bytes 262176 | tf_op jit(solution)/shard_map/ppermute | solution.py:1216
  246.0 9.3 %shard_map.327 = (f32[7,1024]{1,0:T(8,128)S(1)}, f32[1024,1024]{1,0:T(8,128)S(1)}, f32[1024,1024]{1,0:T(8,128)S(1)}, bf16[1024,1024]{1,0:T(8,128)(2,1)}, bf16[10...) custom-call(s32[1]{0:T(128)} %constant.74.clone.1.tick_ref, ...), custom_call_target="tpu_custom_call", output_to_operand_aliasing={{0}: (18, {}), {1}: (19, {}), {2}: (20, {}), {3}: (21, {}),... | custom-call | flops 11000000512 | bytes 4194304 | tf_op jit(solution)/shard_map/pallas_call | solution.py:798
  259.5 37.2 %collective-permute-done.24.inc_ref = bf16[128,1024]{1,0:T(8,128)(2,1)S(1)} collective-permute-done((bf16[128,1024]{1,0:T(8,128)(2,1)S(1)}, bf16[128,1024]{1,0:T(8,128)(2,1)S(1)}, u32[]{:S(2)}, u32[]{:S(2)}) %collective-permute-start.24) | collective-permute-done | bytes 262176 | tf_op jit(solution)/shard_map/ppermute | solution.py:1216
  304.2 10.6 %shard_map.331 = (f32[7,1024]{1,0:T(8,128)S(1)}, f32[1024,1024]{1,0:T(8,128)S(1)}, f32[1024,1024]{1,0:T(8,128)S(1)}, bf16[1024,1024]{1,0:T(8,128)(2,1)}, bf16[10...) custom-call(s32[1]{0:T(128)} %constant.89.clone.1.tick_ref, ...), custom_call_target="tpu_custom_call", output_to_operand_aliasing={{0}: (18, {}), {1}: (19, {}), {2}: (20, {}), {3}: (21, {}),... | custom-call | flops 11000000512 | bytes 4194304 | tf_op jit(solution)/shard_map/pallas_call | solution.py:798
  324.2 10.5 %shard_map.333 = (f32[7,1024]{1,0:T(8,128)S(1)}, f32[1024,1024]{1,0:T(8,128)S(1)}, f32[1024,1024]{1,0:T(8,128)S(1)}, bf16[1024,1024]{1,0:T(8,128)(2,1)}, bf16[10...) custom-call(s32[1]{0:T(128)} %constant.88.clone.1.tick_ref, ...), custom_call_target="tpu_custom_call", output_to_operand_aliasing={{0}: (18, {}), {1}: (19, {}), {2}: (20, {}), {3}: (21, {}),... | custom-call | flops 11000000512 | bytes 4194304 | tf_op jit(solution)/shard_map/pallas_call | solution.py:798
  344.4 10.6 %shard_map.335 = (f32[7,1024]{1,0:T(8,128)S(1)}, f32[1024,1024]{1,0:T(8,128)S(1)}, f32[1024,1024]{1,0:T(8,128)S(1)}, bf16[1024,1024]{1,0:T(8,128)(2,1)}, bf16[10...) custom-call(s32[1]{0:T(128)} %constant.87.clone.1.tick_ref, ...), custom_call_target="tpu_custom_call", output_to_operand_aliasing={{0}: (18, {}), {1}: (19, {}), {2}: (20, {}), {3}: (21, {}),... | custom-call | flops 11000000512 | bytes 4194304 | tf_op jit(solution)/shard_map/pallas_call | solution.py:798
  364.6 10.6 %shard_map.337 = (f32[7,1024]{1,0:T(8,128)S(1)}, f32[1024,1024]{1,0:T(8,128)S(1)}, f32[1024,1024]{1,0:T(8,128)S(1)}, bf16[1024,1024]{1,0:T(8,128)(2,1)}, bf16[10...) custom-call(s32[1]{0:T(128)} %constant.86.clone.1.tick_ref, ...), custom_call_target="tpu_custom_call", output_to_operand_aliasing={{0}: (18, {}), {1}: (19, {}), {2}: (20, {}), {3}: (21, {}),... | custom-call | flops 11000000512 | bytes 4194304 | tf_op jit(solution)/shard_map/pallas_call | solution.py:798
  383.9 9.2 %shard_map.339 = (f32[7,1024]{1,0:T(8,128)S(1)}, f32[1024,1024]{1,0:T(8,128)S(1)}, f32[1024,1024]{1,0:T(8,128)S(1)}, bf16[1024,1024]{1,0:T(8,128)(2,1)}, bf16[10...) custom-call(s32[1]{0:T(128)} %constant.85.clone.1.tick_ref, ...), custom_call_target="tpu_custom_call", output_to_operand_aliasing={{0}: (18, {}), {1}: (19, {}), {2}: (20, {}), {3}: (21, {}),... | custom-call | flops 11000000512 | bytes 4194304 | tf_op jit(solution)/shard_map/pallas_call | solution.py:798
  419.6 9.8 %collective-permute-done.30.inc_ref = bf16[128,1024]{1,0:T(8,128)(2,1)S(1)} collective-permute-done((bf16[128,1024]{1,0:T(8,128)(2,1)S(1)}, bf16[128,1024]{1,0:T(8,128)(2,1)S(1)}, u32[]{:S(2)}, u32[]{:S(2)}) %collective-permute-start.30) | collective-permute-done | bytes 262176 | tf_op jit(solution)/shard_map/ppermute | solution.py:1216
  429.4 9.4 %shard_map.343 = (f32[4,1024]{1,0:T(4,128)S(1)}, f32[3,4096]{1,0:T(4,128)S(1)}, bf16[1024,1024]{1,0:T(8,128)(2,1)}, bf16[1024,4096]{1,0:T(8,128)(2,1)}, f32[128,1024]{1,0:T(8,128)S(1)}) custom-call(s32[1]{0:T(128)} %constant.81.clone.1.tick_ref, ...), custom_call_target="tpu_custom_call", output_to_operand_aliasing={{0}: (12, {}), {1}: (13, {}), {2}: (14, {}), {3}: (15, {})} | custom-call | flops 2147483648 | bytes 4194304 | tf_op jit(solution)/shard_map/pallas_call | solution.py:798
  447.4 8.7 %shard_map.345.refs_3_ = bf16[1024,2048]{1,0:T(8,128)(2,1)} custom-call(bf16[1024,1024]{1,0:T(8,128)(2,1)} %get-tuple-element.1010.refs_0_, bf16[1024,4096]{1,0:T(8,128)(2,1)} %get-tuple-element.1011.refs_1_, bf16[2048,1024]{1,0:T(8,128)(2,1)} %shard_map.344.refs_2_), custom_call_target="tpu_custom_call" | custom-call | flops 1100000000 | bytes 1024 | tf_op jit(solution)/shard_map/pallas_call | solution.py:906
  456.5 9.1 %shard_map.346 = (bf16[512,1024]{1,0:T(8,128)(2,1)}, bf16[512,1024]{1,0:T(8,128)(2,1)}, bf16[512,1024]{1,0:T(8,128)(2,1)}, bf16[512,1024]{1,0:T(8,128)(2,1)}) custom-call(s32[6]{0:T(128)S(1)} %stack.46.after.place_ref.section_ref, bf16[1024,4096]{1,0:T(8,128)(2,1)} %get-tuple-element.800.refs_0_, bf16[1024,1024]{1,0:T(8,128)(2,1)} %get-tuple-element.1009.refs_1_.refs_2_, ...), custom_call_target="tpu_custom_call" | custom-call | flops 1100000000 | bytes 1024 | tf_op jit(solution)/shard_map/pallas_call | solution.py:965
  469.2 9.4 %shard_map.347 = (bf16[256,2048]{1,0:T(8,128)(2,1)}, bf16[256,2048]{1,0:T(8,128)(2,1)}, bf16[256,2048]{1,0:T(8,128)(2,1)}, bf16[256,2048]{1,0:T(8,128)(2,1)}) custom-call(s32[6]{0:T(128)S(1)} %stack.46.after.place_ref.section_ref, bf16[1024,1024]{1,0:T(8,128)(2,1)} %get-tuple-element.1010.refs_0_, bf16[1024,4096]{1,0:T(8,128)(2,1)} %get-tuple-element.1011.refs_1_, ...), custom_call_target="tpu_custom_call" | custom-call | flops 1100000000 | bytes 1024 | tf_op jit(solution)/shard_map/pallas_call | solution.py:965
  505.0 10.0 %shard_map.350 = (f32[7,1024]{1,0:T(8,128)S(1)}, f32[1024,1024]{1,0:T(8,128)S(1)}, f32[1024,1024]{1,0:T(8,128)S(1)}, bf16[1024,1024]{1,0:T(8,128)(2,1)}, bf16[10...) custom-call(s32[1]{0:T(128)} %constant.81.clone.1.tick_ref, ...), custom_call_target="tpu_custom_call", output_to_operand_aliasing={{0}: (18, {}), {1}: (19, {}), {2}: (20, {}), {3}: (21, {}),... | custom-call | flops 1100000000 | bytes 4194304 | tf_op jit(solution)/shard_map/pallas_call | solution.py:798
  515.1 9.2 %shard_map.351.refs_4_ = bf16[1024,2048]{1,0:T(8,128)(2,1)} custom-call(bf16[1024,1024]{1,0:T(8,128)(2,1)} %get-tuple-element.1032.refs_0_, bf16[1024,1024]{1,0:T(8,128)(2,1)} %get-tuple-element.1043.refs_1_, bf16[1024,1024]{1,0:T(8,128)(2,1)} %get-tuple-element.1044.refs_2_, bf16[1024,1024]{1,0:T(8,128)(2,1)} %get-tuple-element.1045.refs_3_, ...), custom_call_target="tpu_custom_call" | custom-call | flops 1100000000 | bytes 1024 | tf_op jit(solution)/shard_map/pallas_call | solution.py:906
  533.9 10.5 %shard_map.353 = (bf16[256,2048]{1,0:T(8,128)(2,1)}, bf16[256,2048]{1,0:T(8,128)(2,1)}, bf16[256,2048]{1,0:T(8,128)(2,1)}, bf16[256,2048]{1,0:T(8,128)(2,1)}) custom-call(s32[6]{0:T(128)S(1)} %stack.46.after.place_ref.section_ref, bf16[1024,1024]{1,0:T(8,128)(2,1)} %get-tuple-element.1032.refs_0_, bf16[1024,1024]{1,0:T(8,128)(2,1)} %get-tuple-element.1043.refs_1_, ...), custom_call_target="tpu_custom_call" | custom-call | flops 1100000000 | bytes 1024 | tf_op jit(solution)/shard_map/pallas_call | solution.py:965
  552.4 21.9 %collective-permute-done.42.refs_1_ = bf16[256,2048]{1,0:T(8,128)(2,1)S(1)} collective-permute-done((bf16[256,2048]{1,0:T(8,128)(2,1)}, bf16[256,2048]{1,0:T(8,128)(2,1)S(1)}, u32[]{:S(2)}, u32[]{:S(2)}) %collective-permute-start.42) | collective-permute-done | bytes 1048608 | tf_op jit(solution)/shard_map/ppermute | solution.py:872
  593.9 10.9 %collective-permute-done.52.refs_2_ = bf16[256,1024]{1,0:T(8,128)(2,1)S(1)} collective-permute-done((bf16[256,1024]{1,0:T(8,128)(2,1)S(1)}, bf16[256,1024]{1,0:T(8,128)(2,1)S(1)}, u32[]{:S(2)}, u32[]{:S(2)}) %collective-permute-start.52) | collective-permute-done | bytes 524320 | tf_op jit(solution)/shard_map/ppermute | solution.py:872
  618.0 9.2 %collective-permute-done.53.refs_3_ = bf16[256,1024]{1,0:T(8,128)(2,1)S(1)} collective-permute-done((bf16[256,1024]{1,0:T(8,128)(2,1)S(1)}, bf16[256,1024]{1,0:T(8,128)(2,1)S(1)}, u32[]{:S(2)}, u32[]{:S(2)}) %collective-permute-start.53) | collective-permute-done | bytes 524320 | tf_op jit(solution)/shard_map/ppermute | solution.py:872
  640.4 9.2 %collective-permute-done.64.refs_2_ = bf16[128,2048]{1,0:T(8,128)(2,1)S(1)} collective-permute-done((bf16[128,2048]{1,0:T(8,128)(2,1)}, bf16[128,2048]{1,0:T(8,128)(2,1)S(1)}, u32[]{:S(2)}, u32[]{:S(2)}) %collective-permute-start.64) | collective-permute-done | bytes 524320 | tf_op jit(solution)/shard_map/ppermute | solution.py:872
  659.0 13.2 %collective-permute-done.65.refs_3_ = bf16[128,2048]{1,0:T(8,128)(2,1)S(1)} collective-permute-done((bf16[128,2048]{1,0:T(8,128)(2,1)S(1)}, bf16[128,2048]{1,0:T(8,128)(2,1)S(1)}, u32[]{:S(2)}, u32[]{:S(2)}) %collective-permute-start.65) | collective-permute-done | bytes 524320 | tf_op jit(solution)/shard_map/ppermute | solution.py:872
  (435 shorter events, 319.3 us)
Async XLA Ops:
  0.7 26.9 %collective-permute-start.4 = (bf16[1024,2048]{1,0:T(8,128)(2,1)}, bf16[1024,2048]{1,0:T(8,128)(2,1)}, u32[]{:S(2)}, u32[]{:S(2)}) collective-permute-start(bf16[1024,2048]{1,0:T(8,128)(2,1)} %bitcast.181), channel_id=1, source_target_pairs={{0,1},{1,0},{2,3},{3,2},{4,5},{5,4},{6,7},{7,6},{8,9},{9,8},{10,11... | collective-permute-start | bytes 12582920 | tf_op jit(solution)/shard_map/ppermute | solution.py:1131
  1.3 28.6 %collective-permute-start.5 = (bf16[2048,1024]{1,0:T(8,128)(2,1)}, bf16[2048,1024]{1,0:T(8,128)(2,1)}, u32[]{:S(2)}, u32[]{:S(2)}) collective-permute-start(bf16[2048,1024]{1,0:T(8,128)(2,1)} %bitcast.183), channel_id=1, source_target_pairs={{0,1},{1,0},{2,3},{3,2},{4,5},{5,4},{6,7},{7,6},{8,9},{9,8},{10,11... | collective-permute-start | bytes 12582920 | tf_op jit(solution)/shard_map/ppermute | solution.py:1131
  141.8 24.6 %collective-permute-start.15 = (bf16[128,1024]{1,0:T(8,128)(2,1)S(1)}, bf16[128,1024]{1,0:T(8,128)(2,1)S(1)}, u32[]{:S(2)}, u32[]{:S(2)}) collective-permute-start(bf16[128,1024]{1,0:T(8,128)(2,1)S(1)} %get-tuple-element.707.prev_ref), channel_id=1, source_target_pairs={{0,8},{8,16},{16,24},{1,9},{9,17},{17,25},{2,10},{10,18},{18,26},{... | collective-permute-start | bytes 786440 | tf_op jit(solution)/shard_map/ppermute | solution.py:1216
  233.0 23.6 %collective-permute-start.23 = (bf16[128,1024]{1,0:T(8,128)(2,1)S(1)}, bf16[128,1024]{1,0:T(8,128)(2,1)S(1)}, u32[]{:S(2)}, u32[]{:S(2)}) collective-permute-start(bf16[128,1024]{1,0:T(8,128)(2,1)S(1)} %get-tuple-element.871.prev_ref), channel_id=1, source_target_pairs={{8,0},{16,8},{24,16},{9,1},{17,9},{25,17},{10,2},{18,10},{26,18},{... | collective-permute-start | bytes 786440 | tf_op jit(solution)/shard_map/ppermute | solution.py:1216
  255.3 41.5 %collective-permute-start.24 = (bf16[128,1024]{1,0:T(8,128)(2,1)S(1)}, bf16[128,1024]{1,0:T(8,128)(2,1)S(1)}, u32[]{:S(2)}, u32[]{:S(2)}) collective-permute-start(bf16[128,1024]{1,0:T(8,128)(2,1)S(1)} %get-tuple-element.887.prev_ref), channel_id=1, source_target_pairs={{8,0},{16,8},{24,16},{9,1},{17,9},{25,17},{10,2},{18,10},{26,18},{... | collective-permute-start | bytes 786440 | tf_op jit(solution)/shard_map/ppermute | solution.py:1216
  258.0 58.8 %collective-permute-start.25 = (bf16[128,1024]{1,0:T(8,128)(2,1)S(1)}, bf16[128,1024]{1,0:T(8,128)(2,1)S(1)}, u32[]{:S(2)}, u32[]{:S(2)}) collective-permute-start(bf16[128,1024]{1,0:T(8,128)(2,1)S(1)} %get-tuple-element.903.prev_ref), channel_id=1, source_target_pairs={{8,0},{16,8},{24,16},{9,1},{17,9},{25,17},{10,2},{18,10},{26,18},{... | collective-permute-start | bytes 786440 | tf_op jit(solution)/shard_map/ppermute | solution.py:1216
  334.8 22.2 %collective-permute-start.27 = (bf16[128,1024]{1,0:T(8,128)(2,1)S(1)}, bf16[128,1024]{1,0:T(8,128)(2,1)S(1)}, u32[]{:S(2)}, u32[]{:S(2)}) collective-permute-start(bf16[128,1024]{1,0:T(8,128)(2,1)S(1)} %get-tuple-element.935.prev_ref), channel_id=1, source_target_pairs={{8,0},{16,8},{24,16},{9,1},{17,9},{25,17},{10,2},{18,10},{26,18},{... | collective-permute-start | bytes 786440 | tf_op jit(solution)/shard_map/ppermute | solution.py:1216
  465.6 35.9 %collective-permute-start.33 = (bf16[512,1024]{1,0:T(8,128)(2,1)}, bf16[512,1024]{1,0:T(8,128)(2,1)}, u32[]{:S(2)}, u32[]{:S(2)}) collective-permute-start(bf16[512,1024]{1,0:T(8,128)(2,1)} %get-tuple-element.1013), channel_id=1, source_target_pairs={{0,2},{2,0},{4,6},{6,4},{1,3},{3,1},{5,7},{7,5},{8,10},{10,8},{12,... | collective-permute-start | bytes 3145736 | tf_op jit(solution)/shard_map/ppermute | solution.py:872
  467.7 33.8 %collective-permute-start.34 = (bf16[512,1024]{1,0:T(8,128)(2,1)}, bf16[512,1024]{1,0:T(8,128)(2,1)}, u32[]{:S(2)}, u32[]{:S(2)}) collective-permute-start(bf16[512,1024]{1,0:T(8,128)(2,1)} %get-tuple-element.1015), channel_id=1, source_target_pairs={{0,4},{2,6},{4,0},{6,2},{1,5},{3,7},{5,1},{7,3},{8,12},{10,14},{12... | collective-permute-start | bytes 3145736 | tf_op jit(solution)/shard_map/ppermute | solution.py:872
  478.6 48.1 %collective-permute-start.39 = (bf16[256,2048]{1,0:T(8,128)(2,1)}, bf16[256,2048]{1,0:T(8,128)(2,1)}, u32[]{:S(2)}, u32[]{:S(2)}) collective-permute-start(bf16[256,2048]{1,0:T(8,128)(2,1)} %get-tuple-element.1050), channel_id=1, source_target_pairs={{0,2},{2,0},{4,6},{6,4},{1,3},{3,1},{5,7},{7,5},{8,10},{10,8},{12,... | collective-permute-start | bytes 3145736 | tf_op jit(solution)/shard_map/ppermute | solution.py:872
  479.2 49.0 %collective-permute-start.40 = (bf16[256,2048]{1,0:T(8,128)(2,1)}, bf16[256,2048]{1,0:T(8,128)(2,1)}, u32[]{:S(2)}, u32[]{:S(2)}) collective-permute-start(bf16[256,2048]{1,0:T(8,128)(2,1)} %get-tuple-element.1051), channel_id=1, source_target_pairs={{0,4},{2,6},{4,0},{6,2},{1,5},{3,7},{5,1},{7,3},{8,12},{10,14},{12... | collective-permute-start | bytes 3145736 | tf_op jit(solution)/shard_map/ppermute | solution.py:872
  479.9 69.5 %collective-permute-start.19 = (bf16[512,1024]{1,0:T(8,128)(2,1)}, bf16[512,1024]{1,0:T(8,128)(2,1)}, u32[]{:S(2)}, u32[]{:S(2)}) collective-permute-start(bf16[512,1024]{1,0:T(8,128)(2,1)} %get-tuple-element.799), channel_id=1, source_target_pairs={{0,1},{1,0},{2,3},{3,2},{4,5},{5,4},{6,7},{7,6},{8,9},{9,8},{10,11... | collective-permute-start | bytes 3145736 | tf_op jit(solution)/shard_map/ppermute | solution.py:1131
  531.5 47.1 %collective-permute-start.46 = (bf16[128,2048]{1,0:T(8,128)(2,1)}, bf16[128,2048]{1,0:T(8,128)(2,1)S(1)}, u32[]{:S(2)}, u32[]{:S(2)}) collective-permute-start(bf16[128,2048]{1,0:T(8,128)(2,1)} %get-tuple-element.1066), channel_id=1, source_target_pairs={{0,4},{2,6},{4,0},{6,2},{1,5},{3,7},{5,1},{7,3},{8,12},{10,14},{12... | collective-permute-start | bytes 1572872 | tf_op jit(solution)/shard_map/ppermute | solution.py:872
  533.5 45.5 %collective-permute-start.47 = (bf16[128,2048]{1,0:T(8,128)(2,1)S(1)}, bf16[128,2048]{1,0:T(8,128)(2,1)S(1)}, u32[]{:S(2)}, u32[]{:S(2)}) collective-permute-start(bf16[128,2048]{1,0:T(8,128)(2,1)S(1)} %copy-done.62), channel_id=1, source_target_pairs={{0,2},{2,0},{4,6},{6,4},{1,3},{3,1},{5,7},{7,5},{8,10},{10,8},{12,... | collective-permute-start | bytes 1572872 | tf_op jit(solution)/shard_map/ppermute | solution.py:872
  544.4 29.8 %collective-permute-start.42 = (bf16[256,2048]{1,0:T(8,128)(2,1)}, bf16[256,2048]{1,0:T(8,128)(2,1)S(1)}, u32[]{:S(2)}, u32[]{:S(2)}) collective-permute-start(bf16[256,2048]{1,0:T(8,128)(2,1)} %get-tuple-element.1060), channel_id=1, source_target_pairs={{0,2},{2,0},{4,6},{6,4},{1,3},{3,1},{5,7},{7,5},{8,10},{10,8},{12,... | collective-permute-start | bytes 3145736 | tf_op jit(solution)/shard_map/ppermute | solution.py:872
  546.2 28.4 %collective-permute-start.43 = (bf16[256,2048]{1,0:T(8,128)(2,1)}, bf16[256,2048]{1,0:T(8,128)(2,1)S(1)}, u32[]{:S(2)}, u32[]{:S(2)}) collective-permute-start(bf16[256,2048]{1,0:T(8,128)(2,1)} %get-tuple-element.1061), channel_id=1, source_target_pairs={{0,4},{2,6},{4,0},{6,2},{1,5},{3,7},{5,1},{7,3},{8,12},{10,14},{12... | collective-permute-start | bytes 3145736 | tf_op jit(solution)/shard_map/ppermute | solution.py:872
  551.8 28.9 %collective-permute-start.41 = (bf16[512,1024]{1,0:T(8,128)(2,1)S(1)}, bf16[512,1024]{1,0:T(8,128)(2,1)S(1)}, u32[]{:S(2)}, u32[]{:S(2)}) collective-permute-start(bf16[512,1024]{1,0:T(8,128)(2,1)S(1)} %copy-done.52), channel_id=1, source_target_pairs={{0,1},{1,0},{2,3},{3,2},{4,5},{5,4},{6,7},{7,6},{8,9},{9,8},{10,11... | collective-permute-start | bytes 3145736 | tf_op jit(solution)/shard_map/ppermute | solution.py:1131
  579.0 25.7 %collective-permute-start.52 = (bf16[256,1024]{1,0:T(8,128)(2,1)S(1)}, bf16[256,1024]{1,0:T(8,128)(2,1)S(1)}, u32[]{:S(2)}, u32[]{:S(2)}) collective-permute-start(bf16[256,1024]{1,0:T(8,128)(2,1)S(1)} %copy-done.29), channel_id=1, source_target_pairs={{0,2},{2,0},{4,6},{6,4},{1,3},{3,1},{5,7},{7,5},{8,10},{10,8},{12,... | collective-permute-start | bytes 1572872 | tf_op jit(solution)/shard_map/ppermute | solution.py:872
  580.7 25.6 %collective-permute-start.55 = (bf16[256,1024]{1,0:T(8,128)(2,1)S(1)}, bf16[256,1024]{1,0:T(8,128)(2,1)S(1)}, u32[]{:S(2)}, u32[]{:S(2)}) collective-permute-start(bf16[256,1024]{1,0:T(8,128)(2,1)S(1)} %copy-done.30), channel_id=1, source_target_pairs={{0,4},{2,6},{4,0},{6,2},{1,5},{3,7},{5,1},{7,3},{8,12},{10,14},{12... | collective-permute-start | bytes 1572872 | tf_op jit(solution)/shard_map/ppermute | solution.py:872
  582.2 29.4 %collective-permute-start.44 = (bf16[128,2048]{1,0:T(8,128)(2,1)}, bf16[128,2048]{1,0:T(8,128)(2,1)S(1)}, u32[]{:S(2)}, u32[]{:S(2)}) collective-permute-start(bf16[128,2048]{1,0:T(8,128)(2,1)} %get-tuple-element.1063), channel_id=1, source_target_pairs={{0,4},{2,6},{4,0},{6,2},{1,5},{3,7},{5,1},{7,3},{8,12},{10,14},{12... | collective-permute-start | bytes 1572872 | tf_op jit(solution)/shard_map/ppermute | solution.py:872
  589.1 26.8 %collective-permute-start.45 = (bf16[128,2048]{1,0:T(8,128)(2,1)}, bf16[128,2048]{1,0:T(8,128)(2,1)S(1)}, u32[]{:S(2)}, u32[]{:S(2)}) collective-permute-start(bf16[128,2048]{1,0:T(8,128)(2,1)} %get-tuple-element.1065), channel_id=1, source_target_pairs={{0,2},{2,0},{4,6},{6,4},{1,3},{3,1},{5,7},{7,5},{8,10},{10,8},{12,... | collective-permute-start | bytes 1572872 | tf_op jit(solution)/shard_map/ppermute | solution.py:872
  593.5 33.7 %collective-permute-start.53 = (bf16[256,1024]{1,0:T(8,128)(2,1)S(1)}, bf16[256,1024]{1,0:T(8,128)(2,1)S(1)}, u32[]{:S(2)}, u32[]{:S(2)}) collective-permute-start(bf16[256,1024]{1,0:T(8,128)(2,1)S(1)} %collective-permute-done.51.refs_1_), channel_id=1, source_target_pairs={{0,2},{2,0},{4,6},{6,4},{1,3},{3,1},{5,7},{7,5},{8,10},{10,8},{12,... | collective-permute-start | bytes 1572872 | tf_op jit(solution)/shard_map/ppermute | solution.py:872
  604.7 24.0 %collective-permute-start.56 = (bf16[256,1024]{1,0:T(8,128)(2,1)S(1)}, bf16[256,1024]{1,0:T(8,128)(2,1)S(1)}, u32[]{:S(2)}, u32[]{:S(2)}) collective-permute-start(bf16[256,1024]{1,0:T(8,128)(2,1)S(1)} %collective-permute-done.54.refs_5_), channel_id=1, source_target_pairs={{0,4},{2,6},{4,0},{6,2},{1,5},{3,7},{5,1},{7,3},{8,12},{10,14},{12... | collective-permute-start | bytes 1572872 | tf_op jit(solution)/shard_map/ppermute | solution.py:872
  606.2 27.8 %collective-permute-start.63 = (bf16[128,2048]{1,0:T(8,128)(2,1)}, bf16[128,2048]{1,0:T(8,128)(2,1)S(1)}, u32[]{:S(2)}, u32[]{:S(2)}) collective-permute-start(bf16[128,2048]{1,0:T(8,128)(2,1)} %get-tuple-element.1069.refs_4_.refs_0_), channel_id=1, source_target_pairs={{0,4},{2,6},{4,0},{6,2},{1,5},{3,7},{5,1},{7,3},{8,12},{10,14},{12... | collective-permute-start | bytes 1572872 | tf_op jit(solution)/shard_map/ppermute | solution.py:872
  611.6 26.9 %collective-permute-start.66 = (bf16[128,2048]{1,0:T(8,128)(2,1)}, bf16[128,2048]{1,0:T(8,128)(2,1)}, u32[]{:S(2)}, u32[]{:S(2)}) collective-permute-start(bf16[128,2048]{1,0:T(8,128)(2,1)} %get-tuple-element.1077.refs_4_), channel_id=1, source_target_pairs={{0,2},{2,0},{4,6},{6,4},{1,3},{3,1},{5,7},{7,5},{8,10},{10,8},{12,... | collective-permute-start | bytes 1572872 | tf_op jit(solution)/shard_map/ppermute | solution.py:872
  616.0 33.7 %collective-permute-start.64 = (bf16[128,2048]{1,0:T(8,128)(2,1)}, bf16[128,2048]{1,0:T(8,128)(2,1)S(1)}, u32[]{:S(2)}, u32[]{:S(2)}) collective-permute-start(bf16[128,2048]{1,0:T(8,128)(2,1)} %get-tuple-element.1069.refs_4_.refs_0_), channel_id=1, source_target_pairs={{0,2},{2,0},{4,6},{6,4},{1,3},{3,1},{5,7},{7,5},{8,10},{10,8},{12,... | collective-permute-start | bytes 1572872 | tf_op jit(solution)/shard_map/ppermute | solution.py:872
  627.2 30.5 %collective-permute-start.67 = (bf16[128,2048]{1,0:T(8,128)(2,1)S(1)}, bf16[128,2048]{1,0:T(8,128)(2,1)S(1)}, u32[]{:S(2)}, u32[]{:S(2)}) collective-permute-start(bf16[128,2048]{1,0:T(8,128)(2,1)S(1)} %copy-done.32), channel_id=1, source_target_pairs={{0,4},{2,6},{4,0},{6,2},{1,5},{3,7},{5,1},{7,3},{8,12},{10,14},{12... | collective-permute-start | bytes 1572872 | tf_op jit(solution)/shard_map/ppermute | solution.py:872
  628.7 45.8 %collective-permute-start.57 = (bf16[128,2048]{1,0:T(8,128)(2,1)}, bf16[128,2048]{1,0:T(8,128)(2,1)}, u32[]{:S(2)}, u32[]{:S(2)}) collective-permute-start(bf16[128,2048]{1,0:T(8,128)(2,1)} %get-tuple-element.1070.after_ref.refs_0_), channel_id=1, source_target_pairs={{0,4},{2,6},{4,0},{6,2},{1,5},{3,7},{5,1},{7,3},{8,12},{10,14},{12... | collective-permute-start | bytes 1572872 | tf_op jit(solution)/shard_map/ppermute | solution.py:872
  634.1 41.0 %collective-permute-start.60 = (bf16[128,2048]{1,0:T(8,128)(2,1)}, bf16[128,2048]{1,0:T(8,128)(2,1)}, u32[]{:S(2)}, u32[]{:S(2)}) collective-permute-start(bf16[128,2048]{1,0:T(8,128)(2,1)} %get-tuple-element.1076.refs_4_), channel_id=1, source_target_pairs={{0,2},{2,0},{4,6},{6,4},{1,3},{3,1},{5,7},{7,5},{8,10},{10,8},{12,... | collective-permute-start | bytes 1572872 | tf_op jit(solution)/shard_map/ppermute | solution.py:872
  638.5 33.6 %collective-permute-start.65 = (bf16[128,2048]{1,0:T(8,128)(2,1)S(1)}, bf16[128,2048]{1,0:T(8,128)(2,1)S(1)}, u32[]{:S(2)}, u32[]{:S(2)}) collective-permute-start(bf16[128,2048]{1,0:T(8,128)(2,1)S(1)} %collective-permute-done.63.refs_1_), channel_id=1, source_target_pairs={{0,2},{2,0},{4,6},{6,4},{1,3},{3,1},{5,7},{7,5},{8,10},{10,8},{12,... | collective-permute-start | bytes 1572872 | tf_op jit(solution)/shard_map/ppermute | solution.py:872
  657.1 22.6 %collective-permute-start.68 = (bf16[128,2048]{1,0:T(8,128)(2,1)}, bf16[128,2048]{1,0:T(8,128)(2,1)}, u32[]{:S(2)}, u32[]{:S(2)}) collective-permute-start(bf16[128,2048]{1,0:T(8,128)(2,1)} %collective-permute-done.66.refs_5_), channel_id=1, source_target_pairs={{0,4},{2,6},{4,0},{6,2},{1,5},{3,7},{5,1},{7,3},{8,12},{10,14},{12... | collective-permute-start | bytes 1572872 | tf_op jit(solution)/shard_map/ppermute | solution.py:872
  658.6 30.0 %collective-permute-start.58 = (bf16[128,2048]{1,0:T(8,128)(2,1)S(1)}, bf16[128,2048]{1,0:T(8,128)(2,1)}, u32[]{:S(2)}, u32[]{:S(2)}) collective-permute-start(bf16[128,2048]{1,0:T(8,128)(2,1)S(1)} %copy-done.33), channel_id=1, source_target_pairs={{0,2},{2,0},{4,6},{6,4},{1,3},{3,1},{5,7},{7,5},{8,10},{10,8},{12,... | collective-permute-start | bytes 1572872 | tf_op jit(solution)/shard_map/ppermute | solution.py:872
  (127 other events, 2008.6 us)
